TPU v7x, 32 devices: a whole 2x2x4 slice. The times are simulated.
32 devices in a mesh: env: 4 (over x, core), tm: 8 (over z, y).
Axes of the slice: x: 2, y: 2, z: 4, core: 2. Of those that a mesh axis runs over, the one named last changes fastest.
Arguments:
- hidden: bfloat16 [4, 8, 256, 1024], P('env', 'tm'), may hold values from -6 to 6
- done_step: int32 [4, 8], P('env', 'tm'), may hold values from 0 to 255
- alive: int32 [4, 8, 256], P('env', None, 'tm'), may hold values 0 or 1
- targets: float32 [4, 8, 256], P('env', None, 'tm'), may hold values from -6 to 6
- gain_t: float32 [1024], replicated, may hold values from 0.25 to 1.75
- w_qkv_t: bfloat16 [1024, 3072], replicated, may hold values from -5 to 5
- w_out_t: bfloat16 [1024, 1024], replicated, may hold values from -0.1875 to 0.1875
- gain_a: float32 [1024], replicated, may hold values from 0.25 to 1.75
- w_qkv_a: bfloat16 [1024, 3072], P('tm'), may hold values from -5 to 5
- w_out_a: bfloat16 [1024, 1024], P('tm'), may hold values from -0.1875 to 0.1875
- w_value: float32 [1024], replicated, may hold values from -0.1875 to 0.1875
Outputs:
- values: float32 [4, 8, 256], P('env', None, 'tm')
- input_grad: bfloat16 [4, 8, 256, 1024], P('env', 'tm')
- qkv_grad: float32 [1024, 3072], P('tm')
- out_grad: float32 [1024, 1024], P('tm')
Inputs may be any that keep to these rules, and one draw needn't show every extreme that they name: `done_step`: the last step of an agent's first episode in the window; later steps form a new episode.
All inputs are finite; a program needn't handle non-finite values. No bound on the sum of `alive` on one device may be relied on, other than what follows from the above.
Results may differ from a plain program's by a relative error of at most 0.02.
Values may be sent and summed in bfloat16 or wider, within the bound.
No kernel may reach another device: no remote copies, remote signals or barrier semaphores. Data moves between devices by JAX's collectives and lax.ppermute only.
A program may use at most 128 MiB of HBM per device.

v0:
```python
import math

import jax
import jax.numpy as jnp
from jax import lax
from jax.sharding import PartitionSpec as P

HEADS = 8


def norm_scale(rows, gain):
    return rows * lax.rsqrt(jnp.mean(rows * rows, axis=-1, keepdims=True) + 1e-06) * gain


def attend(qkv, allowed, head_count, layout):
    width = qkv.shape[-1] // 3
    size = width // head_count
    shape = qkv.shape[:-1] + (head_count, size)
    queries = qkv[..., :width].reshape(shape).astype(jnp.float32)
    key_rows = qkv[..., width : 2 * width].reshape(shape).astype(jnp.float32)
    value_rows = qkv[..., 2 * width :].reshape(shape).astype(jnp.float32)
    if layout == "temporal":
        score_form = "bqhe,bkhe->bhqk"
        mix_form = "bhqk,bkhe->bqhe"
    else:
        score_form = "qbhe,kbhe->bhqk"
        mix_form = "bhqk,kbhe->qbhe"
    scores = jnp.einsum(score_form, queries, key_rows) / math.sqrt(size)
    scores = jnp.where(allowed[:, None], scores, -1e30)
    row_max = jnp.max(scores, axis=-1, keepdims=True)
    weights = jnp.exp(scores - row_max)
    probs = (weights / jnp.sum(weights, axis=-1, keepdims=True)).astype(jnp.bfloat16)
    mixed = jnp.einsum(mix_form, probs.astype(jnp.float32), value_rows)
    return mixed.reshape(qkv.shape[:-1] + (width,))


def temporal_block(rows, done, gain, w_qkv, w_out, head_count):
    batch, length, width = rows.shape
    rows_f = rows.astype(jnp.float32)
    normed = norm_scale(rows_f, gain).astype(jnp.bfloat16)
    qkv = jnp.dot(normed.reshape(-1, width), w_qkv, preferred_element_type=jnp.float32)
    qkv = qkv.astype(jnp.bfloat16).reshape(batch, length, 3 * width)
    positions = jnp.arange(length, dtype=jnp.int32)
    later = positions[None, :] > done[:, None]
    causal = positions[:, None] >= positions[None, :]
    allowed = causal[None] & (later[:, :, None] == later[:, None, :])
    mixed = attend(qkv, allowed, head_count, "temporal").astype(jnp.bfloat16)
    added = jnp.dot(mixed.reshape(-1, width), w_out, preferred_element_type=jnp.float32)
    return (rows_f + added.reshape(batch, length, width)).astype(jnp.bfloat16)


def left_product(left, right):
    return lax.dot_general(
        left, right, (((0,), (0,)), ((), ())), preferred_element_type=jnp.float32
    )


def agent_step(lifted, alive_rows, target_rows, gain, w_qkv, w_out, w_value, head_count):
    agent_count, step_count, width = lifted.shape
    lifted_f = lifted.astype(jnp.float32)
    normed_f, norm_pull = jax.vjp(lambda rows: norm_scale(rows, gain), lifted_f)
    normed = normed_f.astype(jnp.bfloat16).reshape(-1, width)
    qkv = jnp.dot(normed, w_qkv, preferred_element_type=jnp.float32)
    qkv = qkv.astype(jnp.bfloat16).reshape(agent_count, step_count, 3 * width)
    living = alive_rows.T == 1
    allowed = living[:, None, :] | jnp.eye(agent_count, dtype=bool)[None]
    mixed_f, attend_pull = jax.vjp(lambda block: attend(block, allowed, head_count, "agents"), qkv)
    mixed = mixed_f.astype(jnp.bfloat16).reshape(-1, width)
    added = jnp.dot(mixed, w_out, preferred_element_type=jnp.float32)
    top_rows = lifted_f + added.reshape(agent_count, step_count, width)
    predicted = jnp.sum(top_rows * w_value, axis=-1)
    residual_err = 32.0 * alive_rows.astype(jnp.float32) * (predicted - target_rows)
    grad_top = residual_err[..., None] * w_value
    grad_rows = grad_top.astype(jnp.bfloat16).reshape(-1, width)
    grad_mixed = jnp.dot(grad_rows, w_out.T, preferred_element_type=jnp.float32)
    grad_qkv = attend_pull(grad_mixed.reshape(agent_count, step_count, width))[0]
    grad_qkv = grad_qkv.reshape(-1, 3 * width)
    grad_normed = jnp.dot(grad_qkv, w_qkv.T, preferred_element_type=jnp.float32)
    grad_lifted = grad_top + norm_pull(grad_normed.reshape(agent_count, step_count, width))[0]
    return (predicted, grad_lifted.astype(jnp.bfloat16), normed, grad_qkv, mixed, grad_rows)


def per_device(
    hidden, done_step, alive, targets, gain_t, w_qkv_t, w_out_t, gain_a, w_qkv_a, w_out_a, w_value
):
    width = hidden.shape[-1]
    local_rows = hidden[0]
    done_rows = done_step[0]
    first, pull = jax.vjp(
        lambda rows: temporal_block(rows, done_rows, gain_t, w_qkv_t, w_out_t, HEADS), local_rows
    )
    lifted = lax.all_to_all(first, "tm", split_axis=1, concat_axis=0, tiled=True)
    qkv_full, out_full = (
        lax.all_gather(w_qkv_a, "tm", axis=0, tiled=True),
        lax.all_gather(w_out_a, "tm", axis=0, tiled=True),
    )
    predicted, grad_lifted, normed, grad_qkv, mixed, grad_rows = agent_step(
        lifted, alive[0], targets[0], gain_a, qkv_full, out_full, w_value, HEADS
    )
    terms = jnp.concatenate(
        [left_product(normed, grad_qkv), left_product(mixed, grad_rows)], axis=1
    )
    summed = lax.psum_scatter(terms, "tm", scatter_dimension=0, tiled=True)
    totals = lax.psum(summed.astype(jnp.bfloat16), "env").astype(jnp.float32)
    qkv_grad = totals[:, : 3 * width]
    out_grad = totals[:, 3 * width :]
    returned = lax.all_to_all(grad_lifted, "tm", split_axis=0, concat_axis=1, tiled=True)
    input_grad = pull(returned)[0]
    return (predicted[None], input_grad[None], qkv_grad, out_grad)


def solution(mesh):
    in_specs = (
        P("env", "tm", None, None),
        P("env", "tm"),
        P("env", None, "tm"),
        P("env", None, "tm"),
        P(),
        P(),
        P(),
        P(),
        P("tm", None),
        P("tm", None),
        P(),
    )
    out_specs = (P("env", None, "tm"), P("env", "tm", None, None), P("tm", None), P("tm", None))
    return jax.shard_map(
        per_device, mesh=mesh, in_specs=in_specs, out_specs=out_specs, check_vma=False
    )
```

profile of v0, /device:TPU:0, one launch (start us, length us, event | category | flops | bytes accessed | tf_op | source)
XLA Modules:
  0.0 549.0 jit_solution(2475795169403112334)
XLA Ops:
  10.7 4.8 fusion.2
  18.2 2.2 copy.99
  26.9 4.5 reduce.15
  31.4 2.2 reshape.467
  33.6 7.3 %all-to-all-start = ((bf16[8,2,16384]{2,1,0:T(2,128)(2,1)}), bf16[8,2,16384]{2,1,0:T(2,128)(2,1)}, u32[]{:S(2)}, u32[]{:S(2)}) async-start(bf16[8,2,16384]{2,1,0:T(2,128)(2,1)} %reshape.467), calls=%async_computation | async-start | bytes 1048576 | tf_op jit(solution)/shard_map/all_to_all | solution.py:92
  41.2 20.8 %all-to-all-done = bf16[8,2,16384]{2,1,0:T(2,128)(2,1)} async-done(((bf16[8,2,16384]{2,1,0:T(2,128)(2,1)}), bf16[8,2,16384]{2,1,0:T(2,128)(2,1)}, u32[]{:S(2)}, u32[]{:S(2)}) %all-to-all-start) | async-done | bytes 524320 | tf_op jit(solution)/shard_map/all_to_all | solution.py:92
  62.0 2.4 reshape.468
  67.5 2.1 bitcast_convert_fusion
  69.5 51.2 %all-gather.3.cloned.1.call-done = bf16[1024,3072]{1,0:T(8,128)(2,1)} async-done(((bf16[128,3072]{1,0:T(8,128)(2,1)}), bf16[1024,3072]{1,0:T(8,128)(2,1)}) %all-gather.3.cloned.1.call-update) | async-done | bytes 6291472 | tf_op jit(solution)/shard_map/all_gather | solution.py:94
  120.7 5.0 convolution_convert_fusion
  129.1 2.1 convert_element_type.233
  131.9 38.4 %all-gather.5.cloned.1.call-done = bf16[1024,1024]{1,0:T(8,128)(2,1)} async-done(((bf16[128,1024]{1,0:T(8,128)(2,1)}), bf16[1024,1024]{1,0:T(8,128)(2,1)}) %all-gather.5.cloned.1.call-update) | async-done | bytes 2097168 | tf_op jit(solution)/shard_map/all_gather | solution.py:95
  170.4 2.9 fusion.44
  180.9 2.8 convolution_bitcast_fusion.1
  192.9 6.2 %multiply_reduce_fusion = (f32[8,32]{1,0:T(8,128)S(1)}, f32[8,32,1024]{2,1,0:T(8,128)}) fusion(f32[8,32,1024]{2,1,0:T(8,128)S(1)} %bitcast.187, f32[1024]{0:T(1024)S(1)} %copy-done.34, bf16[1024,3072]{1,0:T(8,128)(2,1)} %all-gather.3.cloned.1.call-done, bf16[8,32,1024]{2,1,0:T(8,128)(2,1)} %reshape.451, bf16[8,32,1024]{2,1,0:T(8,128)(2,1)} %reshape.450, ...), kind=kOutput, calls=%fused_computation.89 | convolution fusion | flops 1616117504 | bytes 9966592 | tf_op jit(solution)/shard_map/dot_general | solution.py:78
  201.3 6.0 %pad_maximum_fusion = f32[1024,4096]{1,0:T(8,128)} fusion(f32[1024,1024]{1,0:T(8,128)S(1)} %copy-done.11, f32[1024,3072]{1,0:T(8,128)S(1)} %convolution_bitcast_fusion), kind=kLoop, calls=%fused_computation | loop fusion | flops 4194304 | bytes 33554432 | tf_op jit(solution)/shard_map/concatenate | solution.py:100
  207.3 2.3 fusion.60
  209.6 3.5 all-to-all-start.1
  213.5 28.5 %all-to-all-done.1 = bf16[8,32,1024]{2,1,0:T(8,128)(2,1)S(1)} async-done(((bf16[8,32,1024]{2,1,0:T(8,128)(2,1)}), bf16[8,32,1024]{2,1,0:T(8,128)(2,1)S(1)}, u32[]{:S(2)}, u32[]{:S(2)}) %all-to-all-start.1) | async-done | bytes 524320 | tf_op jit(solution)/shard_map/all_to_all | solution.py:107
  245.6 2.3 fusion.6
  253.6 247.1 %reduce-scatter.2.cloned.1.call-done = f32[128,4096]{1,0:T(8,128)} async-done(((f32[1024,4096]{1,0:T(8,128)}), f32[128,4096]{1,0:T(8,128)}) %reduce-scatter.2.cloned.1.call-update) | async-done | bytes 2097168 | tf_op jit(solution)/shard_map/reduce_scatter | solution.py:103
  500.7 2.7 convert_element_type.264
  503.5 5.1 fusion.58
  509.8 29.1 %all-reduce.8.cloned.1.call-done = bf16[128,4096]{1,0:T(8,128)(2,1)} async-done(((bf16[128,4096]{1,0:T(8,128)(2,1)}), bf16[128,4096]{1,0:T(8,128)(2,1)}) %all-reduce.8.cloned.1.call-update) | async-done | bytes 1048592 | tf_op jit(solution)/shard_map/psum | solution.py:104
  (141 shorter events, 51.8 us)
Async XLA Ops:
  7.2 17.6 %copy-start = (bf16[1024,1024]{1,0:T(8,128)(2,1)S(1)}, bf16[1024,1024]{1,0:T(8,128)(2,1)}, u32[]{:S(2)}) copy-start(bf16[1024,1024]{1,0:T(8,128)(2,1)} %param.17) | copy-start | bytes 6291460
  7.2 113.5 %all-gather.3.cloned.1.call-start = ((), (), s32[]{:S(2)}) async-start(), calls=%async_computation.3 | async-start | bytes 7077888 | tf_op jit(solution)/shard_map/all_gather | solution.py:94
  7.9 162.4 %all-gather.5.cloned.1.call-start = ((), (), s32[]{:S(2)}) async-start(), calls=%async_computation.4 | async-start | bytes 2359296 | tf_op jit(solution)/shard_map/all_gather | solution.py:95
  16.8 6.7 %copy-start.7 = (bf16[32,8,8,128]{3,2,1,0:T(8,128)(2,1)}, bf16[32,8,8,128]{3,2,1,0:T(8,128)(2,1)S(1)}, u32[]{:S(2)}) copy-start(bf16[32,8,8,128]{3,2,1,0:T(8,128)(2,1)S(1)} %copy.101) | copy-start | bytes 1572868
  18.2 3.9 copy-start.12
  26.3 14.6 %copy-start.28 = (s32[1,8,32]{2,1,0:T(8,128)S(1)}, s32[1,8,32]{2,1,0:T(8,128)}, u32[]{:S(2)}) copy-start(s32[1,8,32]{2,1,0:T(8,128)} %param.13) | copy-start | bytes 3076
  33.6 28.4 %all-to-all-start = ((bf16[8,2,16384]{2,1,0:T(2,128)(2,1)}), bf16[8,2,16384]{2,1,0:T(2,128)(2,1)}, u32[]{:S(2)}, u32[]{:S(2)}) async-start(bf16[8,2,16384]{2,1,0:T(2,128)(2,1)} %reshape.467), calls=%async_computation | async-start | bytes 1048576 | tf_op jit(solution)/shard_map/all_to_all | solution.py:92
  40.9 459.8 %reduce-scatter.2.cloned.1.call-start = ((), (), s32[]{:S(2)}) async-start(), calls=%async_computation.5 | async-start | bytes 18874368 | tf_op jit(solution)/shard_map/reduce_scatter | solution.py:103
  66.3 54.5 %copy-start.33 = (f32[1024]{0:T(1024)S(1)}, f32[1024]{0:T(1024)}, u32[]{:S(2)}) copy-start(f32[1024]{0:T(1024)} %param.18) | copy-start | bytes 12292
  128.2 42.1 %copy-start.29 = (f32[1024]{0:T(1024)S(1)}, f32[1024]{0:T(1024)}, u32[]{:S(2)}) copy-start(f32[1024]{0:T(1024)} %param.21) | copy-start | bytes 12292
  131.2 42.1 %copy-start.30 = (f32[1,8,32]{2,1,0:T(8,128)S(1)}, f32[1,8,32]{2,1,0:T(8,128)}, u32[]{:S(2)}) copy-start(f32[1,8,32]{2,1,0:T(8,128)} %param.14) | copy-start | bytes 3076
  170.4 3.0 copy-start.32
  184.8 8.0 %copy-start.10 = (f32[1,256,1024]{2,1,0:T(8,128)S(1)}, f32[1,256,1024]{2,1,0:T(8,128)}, u32[]{:S(2)}) copy-start(f32[1,256,1024]{2,1,0:T(8,128)} %copy.97) | copy-start | bytes 3145732
  184.8 8.0 %copy-start.34 = (f32[1024]{0:T(1024)S(1)}, f32[1024]{0:T(1024)}, u32[]{:S(2)}) copy-start(f32[1024]{0:T(1024)} %param.18) | copy-start | bytes 12292
  192.9 6.2 %copy-start.24 = (bf16[8,32,1024]{2,1,0:T(8,128)(2,1)S(1)}, bf16[8,32,1024]{2,1,0:T(8,128)(2,1)}, u32[]{:S(2)}) copy-start(bf16[8,32,1024]{2,1,0:T(8,128)(2,1)} %reshape.449) | copy-start | bytes 1572868
  192.9 6.2 %copy-start.25 = (bf16[8,32,1024]{2,1,0:T(8,128)(2,1)S(1)}, bf16[8,32,1024]{2,1,0:T(8,128)(2,1)}, u32[]{:S(2)}) copy-start(bf16[8,32,1024]{2,1,0:T(8,128)(2,1)} %reshape.450) | copy-start | bytes 1572868
  192.9 6.2 %copy-start.26 = (bf16[8,32,1024]{2,1,0:T(8,128)(2,1)S(1)}, bf16[8,32,1024]{2,1,0:T(8,128)(2,1)}, u32[]{:S(2)}) copy-start(bf16[8,32,1024]{2,1,0:T(8,128)(2,1)} %reshape.451) | copy-start | bytes 1572868
  209.6 32.3 %all-to-all-start.1 = ((bf16[8,32,1024]{2,1,0:T(8,128)(2,1)}), bf16[8,32,1024]{2,1,0:T(8,128)(2,1)S(1)}, u32[]{:S(2)}, u32[]{:S(2)}) async-start(bf16[8,32,1024]{2,1,0:T(8,128)(2,1)} %fusion.60), calls=%async_computation.1 | async-start | bytes 1048576 | tf_op jit(solution)/shard_map/all_to_all | solution.py:107
  213.1 325.7 %all-reduce.8.cloned.1.call-start = ((), (), s32[]{:S(2)}) async-start(), calls=%async_computation.6 | async-start | bytes 2097152 | tf_op jit(solution)/shard_map/psum | solution.py:104
  242.8 2.8 copy-start.8
  245.6 2.4 copy-start.2
  253.6 249.8 %copy-start.6 = (bf16[1,1,256,1024]{3,2,1,0:T(8,128)(2,1)S(1)}, bf16[1,1,256,1024]{3,2,1,0:T(8,128)(2,1)}, u32[]{:S(2)}) copy-start(bf16[1,1,256,1024]{3,2,1,0:T(8,128)(2,1)} %param.11) | copy-start | bytes 1572868
  253.6 249.8 %copy-start.35 = (f32[1024]{0:T(1024)S(1)}, f32[1024]{0:T(1024)}, u32[]{:S(2)}) copy-start(f32[1024]{0:T(1024)} %param.15) | copy-start | bytes 12292
  503.5 5.1 copy-start.16
  (18 other events, 27.2 us)
Sparse Core Ops, SparseCore 0:
  10.2 110.4 all-gather.2
  122.8 47.4 all-gather.4
  207.4 293.2 reduce-scatter.1
  503.7 35.1 all-reduce.7
where the time goes:
time: 557 us; the launch traced here: 549 us
  waiting for transfers between devices  417 us (75%)
  matrix products  47.6 us (9%)
  local copies, waits for them, and re-layouts  32.6 us (6%)
  other arithmetic  25.5 us (5%)
  between operations  15.5 us (3%)
  starting transfers between devices  11.2 us (2%)
    reduce_scatter x1, waiting for transfers between devices, per_device(): summed = lax.psum_scatter(terms, 'tm', scatter_dimension=0, tiled=True)  247 us
    all_gather x1, waiting for transfers between devices, per_device(): lax.all_gather(w_qkv_a, 'tm', axis=0, tiled=True)  51.2 us
    all_gather x1, waiting for transfers between devices, per_device(): lax.all_gather(w_out_a, 'tm', axis=0, tiled=True)  38.4 us
    psum x1, waiting for transfers between devices, per_device(): totals = lax.psum(summed.astype(jnp.bfloat16), 'env').astype(jnp.float32)  29.1 us
    all_to_all x1, waiting for transfers between devices, per_device(): lax.all_to_all(grad_lifted, 'tm', split_axis=0, concat_axis=1, tiled=True)  28.5 us
    all_to_all x1, waiting for transfers between devices, per_device(): lax.all_to_all(first, 'tm', split_axis=1, concat_axis=0, tiled=True)  20.8 us
    unnamed x81, local copies, waits for them, and re-layouts  11.3 us
  transfers between devices with their start and end apart: 6, of which 6 were waited for; matrix products, arithmetic and copies ran while one was open for 11% of the time, Pallas kernels for 0%

commit v1 on v0

v1 whole, which is shorter than its diff:
```python
import functools
import math

import jax
import jax.numpy as jnp
from jax import lax
from jax.experimental import pallas as pl
from jax.experimental.pallas import tpu as pltpu
from jax.sharding import PartitionSpec as P

HEADS = 8
EPS = 1e-06
F32 = jnp.float32
BF16 = jnp.bfloat16
TILE = 256
VMEM_BYTES = 40 * 1024 * 1024


def dot_nn(a, b):
    return lax.dot_general(a, b, (((1,), (0,)), ((), ())), preferred_element_type=F32)


def dot_nt(a, b):
    return lax.dot_general(a, b, (((1,), (1,)), ((), ())), preferred_element_type=F32)


def dot_tn(a, b):
    return lax.dot_general(a, b, (((0,), (0,)), ((), ())), preferred_element_type=F32)


def inv_rms(rows):
    return lax.rsqrt(jnp.mean(rows * rows, axis=-1, keepdims=True) + EPS)


def norm_pull(rows, gain, grad):
    scale = inv_rms(rows)
    scaled = grad * gain
    inner = jnp.mean(scaled * rows, axis=-1, keepdims=True)
    return scale * scaled - rows * (scale * scale * scale * inner)


def spans(total, size):
    size = min(size, total)
    return [pl.ds(at, size) for at in range(0, total, size)]


def temporal_forward(
    done_ref, rows_ref, gain_ref, w_qkv_hbm, w_out_hbm, h1_ref, qkv_ref, probs_ref,
    w_qkv, w_out, mixed, sems,
):
    length, width = rows_ref.shape
    size = width // HEADS
    copies = []
    for part in range(3):
        span = pl.ds(part * width, width)
        copies.append(
            pltpu.make_async_copy(w_qkv_hbm.at[:, span], w_qkv.at[:, span], sems.at[part])
        )
    copies.append(pltpu.make_async_copy(w_out_hbm, w_out, sems.at[3]))
    for copy in copies:
        copy.start()
    rows = rows_ref[...].astype(F32)
    normed = (rows * inv_rms(rows) * gain_ref[...]).astype(BF16)
    for part in range(3):
        copies[part].wait()
        for at in range(part * width, (part + 1) * width, TILE):
            span = pl.ds(at, TILE)
            qkv_ref[:, span] = dot_nn(normed, w_qkv[:, span]).astype(BF16)
    done = done_ref[0]
    query_at = lax.broadcasted_iota(jnp.int32, (length, length), 0)
    key_at = lax.broadcasted_iota(jnp.int32, (length, length), 1)
    allowed = (key_at <= query_at) & ((key_at > done) == (query_at > done))
    bias = jnp.where(allowed, 0.0, -1e30)
    for head in range(HEADS):
        queries = qkv_ref[:, pl.ds(head * size, size)]
        keys = qkv_ref[:, pl.ds(width + head * size, size)]
        values = qkv_ref[:, pl.ds(2 * width + head * size, size)]
        scores = dot_nt(queries, keys) * (1.0 / math.sqrt(size)) + bias
        weights = jnp.exp(scores - jnp.max(scores, axis=-1, keepdims=True))
        probs = weights * (1.0 / jnp.sum(weights, axis=-1, keepdims=True))
        probs = probs.astype(BF16)
        probs_ref[head] = probs
        mixed[:, pl.ds(head * size, size)] = dot_nn(probs, values).astype(BF16)
    copies[3].wait()
    for span in spans(width, TILE):
        added = dot_nn(mixed[...], w_out[:, span])
        h1_ref[:, span] = (rows_ref[:, span].astype(F32) + added).astype(BF16)


def temporal_backward(
    grad_ref, rows_ref, gain_ref, qkv_ref, probs_ref, w_qkv_hbm, w_out_hbm, out_ref,
    w_qkv, w_out, grad_mixed, grad_qkv, grad_normed, sems,
):
    length, width = rows_ref.shape
    size = width // HEADS
    scale = 1.0 / math.sqrt(size)
    copies = [
        pltpu.make_async_copy(w_out_hbm, w_out, sems.at[0]),
        pltpu.make_async_copy(w_qkv_hbm, w_qkv, sems.at[1]),
    ]
    for copy in copies:
        copy.start()
    copies[0].wait()
    grad = grad_ref[...]
    for span in spans(width, TILE):
        grad_mixed[:, span] = dot_nt(grad, w_out[span, :]).astype(BF16)
    for head in range(HEADS):
        query_span = pl.ds(head * size, size)
        key_span = pl.ds(width + head * size, size)
        value_span = pl.ds(2 * width + head * size, size)
        probs = probs_ref[head]
        head_grad = grad_mixed[:, query_span]
        grad_qkv[:, value_span] = dot_tn(probs, head_grad).astype(BF16)
        grad_probs = dot_nt(head_grad, qkv_ref[:, value_span])
        wide = probs.astype(F32)
        inner = jnp.sum(wide * grad_probs, axis=-1, keepdims=True)
        grad_scores = (wide * (grad_probs - inner) * scale).astype(BF16)
        grad_qkv[:, query_span] = dot_nn(grad_scores, qkv_ref[:, key_span]).astype(BF16)
        grad_qkv[:, key_span] = dot_tn(grad_scores, qkv_ref[:, query_span]).astype(BF16)
    copies[1].wait()
    for span in spans(width, TILE):
        grad_normed[:, span] = dot_nt(grad_qkv[...], w_qkv[span, :])
    rows = rows_ref[...].astype(F32)
    pulled = norm_pull(rows, gain_ref[...], grad_normed[...])
    out_ref[...] = (grad_ref[...].astype(F32) + pulled).astype(BF16)


def agent_kernel(
    blocks, group_steps, place_ref, rows_ref, alive_ref, target_ref, gain_ref, value_ref,
    folded_ref, shard_hbm, *rest,
):
    moved = rest[: 2 * blocks]
    grad_ref, normed_ref, grad_qk_ref, folded_grad_ref, predicted_ref = rest[2 * blocks : 2 * blocks + 5]
    w_qk, qk, probs_all, slopes, column, grad_normed, sems = rest[2 * blocks + 5 :]
    total_rows, width = rows_ref.shape
    size = width // HEADS
    scale = 1.0 / math.sqrt(size)
    groups, group_rows = alive_ref.shape[0], alive_ref.shape[2]
    agents = group_rows // group_steps
    local_steps = total_rows // agents
    depth = shard_hbm.shape[0]

    copies = [
        pltpu.make_async_copy(
            shard_hbm.at[:, pl.ds(0, 2 * width)],
            w_qk.at[pl.ds(pl.multiple_of(place_ref[2 * blocks] * depth, depth), depth), :],
            sems.at[2 * blocks],
        )
    ]
    for at in range(2 * blocks):
        half = place_ref[2 * blocks + 1 + at // blocks]
        target = w_qk.at[
            pl.ds(pl.multiple_of(place_ref[at] * depth, depth), depth),
            pl.ds(pl.multiple_of(half * width, width), width),
        ]
        copies.append(pltpu.make_async_copy(moved[at], target, sems.at[at]))
    for copy in copies:
        copy.start()

    def row_spans(group):
        if groups == 1:
            return [(pl.ds(0, total_rows), pl.ds(0, total_rows))]
        return [
            (
                pl.ds(agent * local_steps + group * group_steps, group_steps),
                pl.ds(group * group_rows + agent * group_steps, group_steps),
            )
            for agent in range(agents)
        ]

    def to_column(row):
        return jnp.transpose(jnp.broadcast_to(row, (128, row.shape[1])))[:, :1]

    for group in range(groups):
        for source, target in row_spans(group):
            rows = rows_ref[source, :].astype(F32)
            normed_ref[target, :] = (rows * inv_rms(rows) * gain_ref[...]).astype(BF16)
            column[target, :] = jnp.broadcast_to(
                jnp.sum(rows * value_ref[...], axis=-1, keepdims=True), (rows.shape[0], 128)
            )
    both = dot_nt(folded_ref[...], normed_ref[...])
    folded_rows = both[:HEADS] + both[HEADS:]
    for copy in copies:
        copy.wait()
    for span in spans(2 * width, TILE):
        qk[:, span] = dot_nn(normed_ref[...], w_qk[:, span]).astype(BF16)

    row_at = lax.broadcasted_iota(jnp.int32, (group_rows, group_rows), 0)
    col_at = lax.broadcasted_iota(jnp.int32, (group_rows, group_rows), 1)
    same_step = row_at % group_steps == col_at % group_steps
    pulls = []
    for group in range(groups):
        group_span = pl.ds(group * group_rows, group_rows)
        alive = alive_ref[group]
        allowed = same_step & ((alive > 0.5) | (row_at == col_at))
        bias = jnp.where(allowed, 0.0, -1e30)
        predicted = column[group_span, :1]
        for head in range(HEADS):
            queries = qk[group_span, pl.ds(head * size, size)]
            keys = qk[group_span, pl.ds(width + head * size, size)]
            scores = dot_nt(queries, keys) * scale + bias
            weights = jnp.exp(scores - jnp.max(scores, axis=-1, keepdims=True))
            probs = weights * (1.0 / jnp.sum(weights, axis=-1, keepdims=True))
            weighted = probs * folded_rows[
                head : head + 1, group * group_rows : (group + 1) * group_rows
            ]
            pooled = jnp.sum(weighted, axis=-1, keepdims=True)
            predicted = predicted + pooled
            probs_all[group * HEADS + head] = probs
            slopes[group * HEADS + head] = (weighted - probs * pooled) * scale
        error = 32.0 * to_column(alive) * (predicted - to_column(target_ref[group]))
        predicted_ref[group] = jnp.transpose(jnp.broadcast_to(predicted, (group_rows, 128)))[:8]
        column[group_span, :] = jnp.broadcast_to(error, (group_rows, 128))
        pull_rows = []
        for head in range(HEADS):
            query_span = pl.ds(head * size, size)
            key_span = pl.ds(width + head * size, size)
            grad_scores = (slopes[group * HEADS + head] * error).astype(BF16)
            grad_qk_ref[group_span, query_span] = dot_nn(
                grad_scores, qk[group_span, key_span]
            ).astype(BF16)
            grad_qk_ref[group_span, key_span] = dot_tn(
                grad_scores, qk[group_span, query_span]
            ).astype(BF16)
            pull_rows.append(
                jnp.sum(probs_all[group * HEADS + head] * error, axis=0, keepdims=True)
            )
        pulls.append(jnp.concatenate(pull_rows, axis=0))
    pull = jnp.concatenate(pulls, axis=1) if groups > 1 else pulls[0]
    pull = pull.astype(BF16)
    twice = jnp.concatenate([pull, pull], axis=0)
    for span in spans(width, TILE):
        grad_normed[:, span] = dot_nt(grad_qk_ref[...], w_qk[span, :]) + dot_tn(
            twice, folded_ref[:, span]
        )
    for group in range(groups):
        for source, target in row_spans(group):
            rows = rows_ref[source, :].astype(F32)
            pulled = norm_pull(rows, gain_ref[...], grad_normed[target, :])
            top = column[target, :1] * value_ref[...]
            grad_ref[source, :] = (top + pulled).astype(BF16)
    folded_grad_ref[...] = dot_nn(pull, normed_ref[...])


def weight_grad_kernel(left_ref, right_ref, out_ref):
    for span in spans(out_ref.shape[1], TILE):
        out_ref[:, span] = dot_tn(left_ref[...], right_ref[:, span]).astype(BF16)


def any_spec():
    return pl.BlockSpec(memory_space=pl.ANY)


def vmem_spec():
    return pl.BlockSpec(memory_space=pltpu.VMEM)


def smem_spec():
    return pl.BlockSpec(memory_space=pltpu.SMEM)


def params():
    return pltpu.CompilerParams(vmem_limit_bytes=VMEM_BYTES)


def cost(flops, moved):
    return pl.CostEstimate(flops=flops, bytes_accessed=moved, transcendentals=0)


def ring_order(count):
    return list(range(0, count, 2)) + list(range(count - 1, 0, -2))


def per_device(
    env_count, tm_count,
    hidden, done_step, alive, targets, gain_t, w_qkv_t, w_out_t, gain_a, w_qkv_a, w_out_a, w_value,
):
    length, width = hidden.shape[2:]
    agents, local_steps = alive.shape[1:]
    depth = w_qkv_a.shape[0]
    size = width // HEADS
    env_at = lax.axis_index("env")
    tm_at = lax.axis_index("tm")
    core = env_at % 2
    order = ring_order(tm_count)
    spot = [order.index(at) for at in range(tm_count)]
    order_array = jnp.array(order, jnp.int32)
    my_spot = jnp.array(spot, jnp.int32)[tm_at]

    def ring(block, step):
        pairs = []
        for env in range(env_count):
            sign = 1 - 2 * (env % 2)
            for at in range(tm_count):
                pairs.append(
                    (env * tm_count + at, env * tm_count + order[(spot[at] + sign * step) % tm_count])
                )
        return lax.ppermute(block, ("env", "tm"), pairs)

    def swap_env(block, bit):
        return lax.ppermute(block, "env", [(at, at ^ bit) for at in range(env_count)])

    def sum_tm(block):
        bit = 1
        while bit < tm_count:
            block = block + lax.ppermute(block, "tm", [(at, at ^ bit) for at in range(tm_count)])
            bit *= 2
        return block

    def sum_env(block):
        bit = 1
        while bit < env_count:
            block = block + swap_env(block, bit)
            bit *= 2
        return block

    far = tm_count // 2
    near = tm_count - 1 - far
    own_half = lax.dynamic_slice(w_qkv_a, (0, core * width), (depth, width))
    forward, backward = [own_half], [own_half]
    for step in range(far):
        forward.append(ring(forward[-1], 1))
        if step < near:
            backward.append(ring(backward[-1], -1))
    own_blocks = forward[1:] + backward[1:]
    other_blocks = [swap_env(block, 1) for block in own_blocks]
    hops = jnp.array([-step for step in range(1, far + 1)] + list(range(1, near + 1)), jnp.int32)
    sign = 1 - 2 * core
    own_places = order_array[(my_spot + sign * hops) % tm_count]
    other_places = order_array[(my_spot - sign * hops) % tm_count]
    places = jnp.concatenate(
        [own_places, other_places, jnp.stack([tm_at, core, 1 - core])]
    ).astype(jnp.int32)

    rows = hidden[0, 0]
    h1, qkv, probs = pl.pallas_call(
        temporal_forward,
        name="temporal_forward",
        out_shape=(
            jax.ShapeDtypeStruct((length, width), BF16),
            jax.ShapeDtypeStruct((length, 3 * width), BF16),
            jax.ShapeDtypeStruct((HEADS, length, length), BF16),
        ),
        in_specs=[smem_spec(), vmem_spec(), vmem_spec(), any_spec(), any_spec()],
        out_specs=[vmem_spec()] * 3,
        scratch_shapes=[
            pltpu.VMEM((width, 3 * width), BF16),
            pltpu.VMEM((width, width), BF16),
            pltpu.VMEM((length, width), BF16),
            pltpu.SemaphoreType.DMA((4,)),
        ],
        compiler_params=params(),
        cost_estimate=cost(8 * length * width * width, 8 * width * width),
    )(done_step[0], rows, gain_t[None], w_qkv_t, w_out_t)
    lifted = lax.all_to_all(h1, "tm", split_axis=0, concat_axis=0, tiled=True)

    local_u = jnp.sum(w_out_a.astype(F32) * w_value, axis=1)
    u = sum_tm(lax.dynamic_update_slice(jnp.zeros((width,), F32), local_u, (tm_at * depth,)))
    w_v = w_qkv_a[:, 2 * width :].astype(F32).reshape(depth, HEADS, size)
    local_folded = jnp.sum(w_v * u.reshape(HEADS, size), axis=-1).T
    folded = sum_tm(
        lax.dynamic_update_slice(jnp.zeros((HEADS, width), F32), local_folded, (0, tm_at * depth))
    )
    folded_high = folded.astype(BF16)
    folded_low = (folded - folded_high.astype(F32)).astype(BF16)
    folded_parts = jnp.concatenate([folded_high, folded_low], axis=0)

    group_steps = 16 if local_steps % 16 == 0 else local_steps
    groups = local_steps // group_steps
    group_rows = agents * group_steps

    def grouped(block):
        block = block.reshape(agents, groups, group_steps)
        return jnp.swapaxes(block, 0, 1).reshape(groups, 1, group_rows)

    total_rows = agents * local_steps
    grad_lifted, normed, grad_qk, folded_grad, predicted = pl.pallas_call(
        functools.partial(agent_kernel, tm_count - 1, group_steps),
        name="agent_block",
        out_shape=(
            jax.ShapeDtypeStruct((total_rows, width), BF16),
            jax.ShapeDtypeStruct((total_rows, width), BF16),
            jax.ShapeDtypeStruct((total_rows, 2 * width), BF16),
            jax.ShapeDtypeStruct((HEADS, width), F32),
            jax.ShapeDtypeStruct((groups, 8, group_rows), F32),
        ),
        in_specs=[smem_spec()] + [vmem_spec()] * 6 + [any_spec()] * (2 * tm_count - 1),
        out_specs=[vmem_spec()] * 5,
        scratch_shapes=[
            pltpu.VMEM((width, 2 * width), BF16),
            pltpu.VMEM((total_rows, 2 * width), BF16),
            pltpu.VMEM((groups * HEADS, group_rows, group_rows), F32),
            pltpu.VMEM((groups * HEADS, group_rows, group_rows), F32),
            pltpu.VMEM((total_rows, 128), F32),
            pltpu.VMEM((total_rows, width), F32),
            pltpu.SemaphoreType.DMA((2 * tm_count - 1,)),
        ],
        compiler_params=params(),
        cost_estimate=cost(8 * total_rows * width * width, 4 * width * width),
    )(
        places, lifted, grouped(alive[0].astype(F32)), grouped(targets[0]), gain_a[None],
        w_value[None], folded_parts, w_qkv_a, *own_blocks, *other_blocks,
    )
    values = predicted[:, 0].reshape(groups, agents, group_steps)
    values = jnp.swapaxes(values, 0, 1).reshape(1, agents, local_steps)

    returned = lax.all_to_all(grad_lifted, "tm", split_axis=0, concat_axis=0, tiled=True)

    def weight_grad(half):
        columns = lax.dynamic_slice(grad_qk, (0, half * width), (total_rows, width))
        return pl.pallas_call(
            weight_grad_kernel,
            name="weight_grad",
            grid=(width // TILE,),
            out_shape=jax.ShapeDtypeStruct((width, width), BF16),
            in_specs=[
                pl.BlockSpec((total_rows, TILE), lambda at: (0, at)),
                pl.BlockSpec((total_rows, width), lambda at: (0, 0)),
            ],
            out_specs=pl.BlockSpec((TILE, width), lambda at: (at, 0)),
            compiler_params=params(),
            cost_estimate=cost(2 * total_rows * width * width, 3 * width * width),
        )(normed, columns)

    received = swap_env(weight_grad(1 - core), 1)
    kept = weight_grad(core)

    def term(hop):
        at = order_array[(my_spot + sign * hop) % tm_count] * depth
        return lax.dynamic_slice(kept, (at, 0), (depth, width)).astype(F32) + lax.dynamic_slice(
            received, (at, 0), (depth, width)
        ).astype(F32)

    ahead = term(far).astype(BF16)
    behind = term(-near).astype(BF16)
    for step in range(far):
        ahead = ring(ahead, 1)
        if step < far - 1:
            ahead = (term(far - 1 - step) + ahead.astype(F32)).astype(BF16)
        if step < near:
            behind = ring(behind, -1)
            if step < near - 1:
                behind = (term(-(near - 1 - step)) + behind.astype(F32)).astype(BF16)
    reduced = (term(0) + ahead.astype(F32) + behind.astype(F32)).astype(BF16)
    bit = 2
    while bit < env_count:
        reduced = (reduced.astype(F32) + swap_env(reduced, bit).astype(F32)).astype(BF16)
        bit *= 2
    other = swap_env(reduced, 1)
    first = jnp.where(core == 0, reduced, other)
    second = jnp.where(core == 0, other, reduced)

    folded_total = sum_tm(sum_env(folded_grad))
    own_folded = lax.dynamic_slice(folded_total, (0, tm_at * depth), (HEADS, depth))
    v_grad = (own_folded.T[:, :, None] * u.reshape(1, HEADS, size)).reshape(depth, width)
    pooled = sum_tm(jnp.sum(w_v * own_folded.T[:, :, None], axis=0).reshape(width))
    own_pooled = lax.dynamic_slice(pooled, (tm_at * depth,), (depth,))
    out_grad = own_pooled[:, None] * w_value[None, :]
    qkv_grad = jnp.concatenate([first.astype(F32), second.astype(F32), v_grad], axis=1)

    input_grad = pl.pallas_call(
        temporal_backward,
        name="temporal_backward",
        out_shape=jax.ShapeDtypeStruct((length, width), BF16),
        in_specs=[vmem_spec()] * 5 + [any_spec()] * 2,
        out_specs=vmem_spec(),
        scratch_shapes=[
            pltpu.VMEM((width, 3 * width), BF16),
            pltpu.VMEM((width, width), BF16),
            pltpu.VMEM((length, width), BF16),
            pltpu.VMEM((length, 3 * width), BF16),
            pltpu.VMEM((length, width), F32),
            pltpu.SemaphoreType.DMA((2,)),
        ],
        compiler_params=params(),
        cost_estimate=cost(8 * length * width * width, 8 * width * width),
    )(returned, rows, gain_t[None], qkv, probs, w_qkv_t, w_out_t)
    return values, input_grad[None, None], qkv_grad, out_grad


def solution(mesh):
    in_specs = (
        P("env", "tm", None, None),
        P("env", "tm"),
        P("env", None, "tm"),
        P("env", None, "tm"),
        P(),
        P(),
        P(),
        P(),
        P("tm", None),
        P("tm", None),
        P(),
    )
    out_specs = (P("env", None, "tm"), P("env", "tm", None, None), P("tm", None), P("tm", None))
    body = functools.partial(per_device, mesh.shape["env"], mesh.shape["tm"])
    return jax.shard_map(
        body, mesh=mesh, in_specs=in_specs, out_specs=out_specs, check_vma=False
    )
```

time: 557 us -> 193 us (0.35); the launches traced: 549 us -> 192 us
  waiting for transfers between devices: 417 us -> 62.2 us
  matrix products: 47.6 us -> 0 us
  starting transfers between devices: 11.2 us -> 44.2 us
  Pallas kernels: 0 us -> 24.4 us
  other arithmetic: 25.5 us -> 19.8 us
    reduce_scatter x1 -> x0, waiting for transfers between devices: 247 us -> none  [per_device(): summed = lax.psum_scatter(terms, 'tm', scatter_dimension=0, tiled=True)]
    all_gather x2 -> x0, waiting for transfers between devices: 89.6 us -> none  [the longest x1 51.2 us: per_device(): lax.all_gather(w_qkv_a, 'tm', axis=0, tiled=True)]
    ppermute x0 -> x38, waiting for transfers between devices: none -> 62.2 us  [the longest x14 30.9 us: ring(): return lax.ppermute(block, ('env', 'tm'), pairs)]
    all_to_all x2, waiting for transfers between devices: 49.3 us -> 0.01 us  [the longest x1 0.01 us: per_device(): lifted = lax.all_to_all(h1, 'tm', split_axis=0, concat_axis=0, tiled=True)]
    dot_general x22 -> x0, matrix products: 47.6 us -> none  [the longest x2 9.96 us: temporal_block(): jnp.dot(normed.reshape(-1, width), w_qkv, preferred_element_type=jnp.floa...]
    ppermute x0 -> x38, starting transfers between devices: none -> 36.3 us  [the longest x14 15.8 us: ring(): return lax.ppermute(block, ('env', 'tm'), pairs)]
    psum x1 -> x0, waiting for transfers between devices: 29.1 us -> none  [per_device(): totals = lax.psum(summed.astype(jnp.bfloat16), 'env').astype(jnp.float32)]
    pallas_call x0 -> x5, Pallas kernels: none -> 24.4 us  [the longest x1 7.17 us: per_device(): pl.pallas_call(temporal_backward, name='temporal_backward', out_shape=jax...]
  transfers between devices with their start and end apart: 6 -> 40, of which waited for: 6 -> 18; matrix products, arithmetic and copies ran while one was open for 11% -> 8% of each run, Pallas kernels for 0% -> 8%
where the time goes in v1:
time: 193 us; the launch traced here: 192 us
  waiting for transfers between devices  62.2 us (32%)
  starting transfers between devices  44.2 us (23%)
  local copies, waits for them, and re-layouts  27.9 us (14%)
  Pallas kernels  24.4 us (13%)
  other arithmetic  19.8 us (10%)
  between operations  13.2 us (7%)
    ppermute x14, waiting for transfers between devices, ring(): return lax.ppermute(block, ('env', 'tm'), pairs)  30.9 us
    ppermute x12, waiting for transfers between devices, sum_tm(): lax.ppermute(block, 'tm', [(at, at ^ bit) for at in range(tm_count)])  28.9 us
    unnamed x67, local copies, waits for them, and re-layouts  22.5 us
    ppermute x14, starting transfers between devices, ring(): return lax.ppermute(block, ('env', 'tm'), pairs)  15.8 us
    ppermute x12, starting transfers between devices, sum_tm(): lax.ppermute(block, 'tm', [(at, at ^ bit) for at in range(tm_count)])  15.2 us
    pallas_call x1, Pallas kernels, per_device(): pl.pallas_call(temporal_backward, name='temporal_backward', out_shape=jax...  7.17 us
    pallas_call x1, Pallas kernels, per_device(): pl.pallas_call(functools.partial(agent_kernel, tm_count - 1, group_steps)...  6.8 us
    pallas_call x1, Pallas kernels, per_device(): pl.pallas_call(temporal_forward, name='temporal_forward', out_shape=(jax....  6.18 us
  transfers between devices with their start and end apart: 40, of which 18 were waited for; matrix products, arithmetic and copies ran while one was open for 8% of the time, Pallas kernels for 8%

profile of v1, /device:TPU:0, one launch (start us, length us, event | category | flops | bytes accessed | tf_op | source)
XLA Modules:
  0.0 191.7 jit_solution(10616321453486524212)
XLA Ops:
  2.8 3.0 %collective-permute-start.6 = (bf16[128,1024]{1,0:T(8,128)(2,1)}, bf16[128,1024]{1,0:T(8,128)(2,1)S(1)}, u32[]{:S(2)}, u32[]{:S(2)}) collective-permute-start(bf16[128,1024]{1,0:T(8,128)(2,1)} %get-tuple-element.24), channel_id=1, source_target_pairs={{0,2},{1,0},{2,4},{3,1},{4,6},{5,3},{6,7},{7,5},{8,9},{9,11},{10,8... | collective-permute-start | bytes 786440 | tf_op jit(solution)/shard_map/ppermute | solution.py:298
  7.2 3.6 %collective-permute-done = f32[1024]{0:T(1024)S(1)} collective-permute-done((f32[1024]{0:T(1024)S(1)}, f32[1024]{0:T(1024)S(1)}, u32[]{:S(2)}, u32[]{:S(2)}) %collective-permute-start) | collective-permute-done | bytes 4128 | tf_op jit(solution)/shard_map/ppermute | solution.py:306
  14.6 2.6 %collective-permute-start.2 = (f32[1024]{0:T(1024)S(1)}, f32[1024]{0:T(1024)S(1)}, u32[]{:S(2)}, u32[]{:S(2)}) collective-permute-start(f32[1024]{0:T(1024)S(1)} %add.247), channel_id=1, source_target_pairs={{0,4},{1,5},{2,6},{3,7},{4,0},{5,1},{6,2},{7,3},{8,12},{9,13},{10,... | collective-permute-start | bytes 12296 | tf_op jit(solution)/shard_map/ppermute | solution.py:306
  22.6 3.6 %collective-permute-done.10.rest_4_ = bf16[128,1024]{1,0:T(8,128)(2,1)S(1)} collective-permute-done((bf16[128,1024]{1,0:T(8,128)(2,1)}, bf16[128,1024]{1,0:T(8,128)(2,1)S(1)}, u32[]{:S(2)}, u32[]{:S(2)}) %collective-permute-start.10) | collective-permute-done | bytes 262176 | tf_op jit(solution)/shard_map/ppermute | solution.py:298
  30.1 2.8 %copy-done = bf16[1024,3072]{1,0:T(8,128)(2,1)S(1)} copy-done((bf16[1024,3072]{1,0:T(8,128)(2,1)S(1)}, bf16[1024,3072]{1,0:T(8,128)(2,1)}, u32[]{:S(2)}) %copy-start) | copy-done | bytes 6291480
  32.9 6.2 %temporal_forward.1 = (bf16[256,1024]{1,0:T(8,128)(2,1)}, bf16[256,3072]{1,0:T(8,128)(2,1)S(1)}, bf16[8,256,256]{2,1,0:T(8,128)(2,1)S(1)}) custom-call(s32[1]{0:T(128)} %bitcast.42.done_ref, bf16[256,1024]{1,0:T(8,128)(2,1)S(1)} %bitcast.43, f32[1,1024]{1,0:T(1,128)S(1)} %bitcast.49, bf16[1024,3072]{1,0:T(8,128)(2,1)S(1)} %copy-done, ...), custom_call_target="tpu_custom_call" | custom-call | flops 2147483648 | bytes 8388608 | tf_op jit(solution)/shard_map/temporal_forward/pallas_call | solution.py:336
  41.2 3.6 %all-to-all-start = ((bf16[8,32,1024]{2,1,0:T(8,128)(2,1)}), bf16[8,32,1024]{2,1,0:T(8,128)(2,1)S(1)}, u32[]{:S(2)}, u32[]{:S(2)}) async-start(bf16[8,32,1024]{2,1,0:T(8,128)(2,1)} %bitcast.7), calls=%async_computation | async-start | bytes 1048576 | tf_op jit(solution)/shard_map/all_to_all | solution.py:355
  50.6 2.8 %collective-permute-done.4 = f32[8,1024]{1,0:T(8,128)S(1)} collective-permute-done((f32[8,1024]{1,0:T(8,128)S(1)}, f32[8,1024]{1,0:T(8,128)S(1)}, u32[]{:S(2)}, u32[]{:S(2)}) %collective-permute-start.4) | collective-permute-done | bytes 32800 | tf_op jit(solution)/shard_map/ppermute | solution.py:306
  53.4 4.3 %collective-permute-start.5 = (f32[8,1024]{1,0:T(8,128)S(1)}, f32[8,1024]{1,0:T(8,128)S(1)}, u32[]{:S(2)}, u32[]{:S(2)}) collective-permute-start(f32[8,1024]{1,0:T(8,128)S(1)} %add.250), channel_id=1, source_target_pairs={{0,4},{1,5},{2,6},{3,7},{4,0},{5,1},{6,2},{7,3},{8,12},{9,13},{10,... | collective-permute-start | bytes 98312 | tf_op jit(solution)/shard_map/ppermute | solution.py:306
  59.4 3.8 %collective-permute-done.5 = f32[8,1024]{1,0:T(8,128)S(1)} collective-permute-done((f32[8,1024]{1,0:T(8,128)S(1)}, f32[8,1024]{1,0:T(8,128)S(1)}, u32[]{:S(2)}, u32[]{:S(2)}) %collective-permute-start.5) | collective-permute-done | bytes 32800 | tf_op jit(solution)/shard_map/ppermute | solution.py:306
  74.3 6.8 %agent_block.1 = (bf16[256,1024]{1,0:T(8,128)(2,1)S(1)}, bf16[256,1024]{1,0:T(8,128)(2,1)S(1)}, bf16[256,2048]{1,0:T(8,128)(2,1)S(1)}, f32[8,1024]{1,0:T(8,128)S(1)}, f32[2,8,128]{2,1,0:T(8,128)S(1)}) custom-call(s32[17]{0:T(128)S(1)} %concatenate.9.place_ref, bf16[256,1024]{1,0:T(8,128)(2,1)S(1)} %bitcast.47, f32[2,1,128]{2,1,0:T(1,128)S(1)} %reshape.56.alive_ref, ...), custom_call_target="tpu_custom_call" | custom-call | flops 2147483648 | bytes 4194304 | tf_op jit(solution)/shard_map/agent_block/pallas_call | solution.py:377
  82.0 2.8 %weight_grad.3 = bf16[1024,1024]{1,0:T(8,128)(2,1)} custom-call(bf16[256,1024]{1,0:T(8,128)(2,1)S(1)} %get-tuple-element.17.left_ref, bf16[256,1024]{1,0:T(8,128)(2,1)S(1)} %get-tuple-element.23.right_ref), custom_call_target="tpu_custom_call" | custom-call | flops 536870912 | bytes 3145728 | tf_op jit(solution)/shard_map/weight_grad/pallas_call | solution.py:411
  97.2 5.8 %collective-permute-done.21 = bf16[128,1024]{1,0:T(8,128)(2,1)S(1)} collective-permute-done((bf16[128,1024]{1,0:T(8,128)(2,1)S(1)}, bf16[128,1024]{1,0:T(8,128)(2,1)S(1)}, u32[]{:S(2)}, u32[]{:S(2)}) %collective-permute-start.21) | collective-permute-done | bytes 262176 | tf_op jit(solution)/shard_map/ppermute | solution.py:298
  104.8 5.7 %collective-permute-done.22 = bf16[128,1024]{1,0:T(8,128)(2,1)S(1)} collective-permute-done((bf16[128,1024]{1,0:T(8,128)(2,1)S(1)}, bf16[128,1024]{1,0:T(8,128)(2,1)S(1)}, u32[]{:S(2)}, u32[]{:S(2)}) %collective-permute-start.22) | collective-permute-done | bytes 262176 | tf_op jit(solution)/shard_map/ppermute | solution.py:298
  113.0 5.0 %collective-permute-done.23 = bf16[128,1024]{1,0:T(8,128)(2,1)S(1)} collective-permute-done((bf16[128,1024]{1,0:T(8,128)(2,1)S(1)}, bf16[128,1024]{1,0:T(8,128)(2,1)S(1)}, u32[]{:S(2)}, u32[]{:S(2)}) %collective-permute-start.23) | collective-permute-done | bytes 262176 | tf_op jit(solution)/shard_map/ppermute | solution.py:298
  121.4 4.4 %collective-permute-done.25 = bf16[128,1024]{1,0:T(8,128)(2,1)} collective-permute-done((bf16[128,1024]{1,0:T(8,128)(2,1)S(1)}, bf16[128,1024]{1,0:T(8,128)(2,1)}, u32[]{:S(2)}, u32[]{:S(2)}) %collective-permute-start.25) | collective-permute-done | bytes 262176 | tf_op jit(solution)/shard_map/ppermute | solution.py:298
  129.8 4.9 %collective-permute-done.26 = bf16[128,1024]{1,0:T(8,128)(2,1)S(1)} collective-permute-done((bf16[128,1024]{1,0:T(8,128)(2,1)S(1)}, bf16[128,1024]{1,0:T(8,128)(2,1)S(1)}, u32[]{:S(2)}, u32[]{:S(2)}) %collective-permute-start.26) | collective-permute-done | bytes 262176 | tf_op jit(solution)/shard_map/ppermute | solution.py:298
  143.0 3.9 %collective-permute-done.32 = f32[8,1024]{1,0:T(8,128)S(1)} collective-permute-done((f32[8,1024]{1,0:T(8,128)S(1)}, f32[8,1024]{1,0:T(8,128)S(1)}, u32[]{:S(2)}, u32[]{:S(2)}) %collective-permute-start.32) | collective-permute-done | bytes 32800 | tf_op jit(solution)/shard_map/ppermute | solution.py:306
  146.9 4.2 %collective-permute-done.33 = f32[8,1024]{1,0:T(8,128)S(1)} collective-permute-done((f32[8,1024]{1,0:T(8,128)S(1)}, f32[8,1024]{1,0:T(8,128)S(1)}, u32[]{:S(2)}, u32[]{:S(2)}) %collective-permute-start.33) | collective-permute-done | bytes 32800 | tf_op jit(solution)/shard_map/ppermute | solution.py:306
  151.7 4.2 %all-to-all-start.1 = ((bf16[8,32,1024]{2,1,0:T(8,128)(2,1)}), bf16[8,32,1024]{2,1,0:T(8,128)(2,1)S(1)}, u32[]{:S(2)}, u32[]{:S(2)}) async-start(bf16[8,32,1024]{2,1,0:T(8,128)(2,1)} %bitcast.46), calls=%async_computation.1 | async-start | bytes 1048576 | tf_op jit(solution)/shard_map/all_to_all | solution.py:407
  163.1 2.8 %collective-permute-done.35 = f32[1024]{0:T(1024)S(1)} collective-permute-done((f32[1024]{0:T(1024)S(1)}, f32[1024]{0:T(1024)S(1)}, u32[]{:S(2)}, u32[]{:S(2)}) %collective-permute-start.35) | collective-permute-done | bytes 4128 | tf_op jit(solution)/shard_map/ppermute | solution.py:306
  166.7 2.8 %collective-permute-done.36 = f32[1024]{0:T(1024)S(1)} collective-permute-done((f32[1024]{0:T(1024)S(1)}, f32[1024]{0:T(1024)S(1)}, u32[]{:S(2)}, u32[]{:S(2)}) %collective-permute-start.36) | collective-permute-done | bytes 4128 | tf_op jit(solution)/shard_map/ppermute | solution.py:306
  176.8 2.8 %copy-done.1 = bf16[1024,3072]{1,0:T(8,128)(2,1)S(1)} copy-done((bf16[1024,3072]{1,0:T(8,128)(2,1)S(1)}, bf16[1024,3072]{1,0:T(8,128)(2,1)}, u32[]{:S(2)}) %copy-start.1) | copy-done | bytes 6291480
  182.2 7.2 %temporal_backward.1 = bf16[256,1024]{1,0:T(8,128)(2,1)} custom-call(bf16[256,1024]{1,0:T(8,128)(2,1)S(1)} %bitcast.45, bf16[256,1024]{1,0:T(8,128)(2,1)S(1)} %bitcast.44, f32[1,1024]{1,0:T(1,128)S(1)} %bitcast.50, bf16[256,3072]{1,0:T(8,128)(2,1)S(1)} %copy-done.7, bf16[8,256,256]{2,1,0:T(8,128)(2,1)S(1)} %copy-done.9, bf16[1024,3072]{1,0:T(8,128)(2,1)S(1)} %copy-done.1, ...), custom_call_target="tpu_custom_call" | custom-call | flops 2147483648 | bytes 8388608 | tf_op jit(solution)/shard_map/temporal_backward/pallas_call | solution.py:461
  (185 shorter events, 79.0 us)
Async XLA Ops:
  2.8 17.4 %collective-permute-start.6 = (bf16[128,1024]{1,0:T(8,128)(2,1)}, bf16[128,1024]{1,0:T(8,128)(2,1)S(1)}, u32[]{:S(2)}, u32[]{:S(2)}) collective-permute-start(bf16[128,1024]{1,0:T(8,128)(2,1)} %get-tuple-element.24), channel_id=1, source_target_pairs={{0,2},{1,0},{2,4},{3,1},{4,6},{5,3},{6,7},{7,5},{8,9},{9,11},{10,8... | collective-permute-start | bytes 786440 | tf_op jit(solution)/shard_map/ppermute | solution.py:298
  17.2 9.0 %collective-permute-start.10 = (bf16[128,1024]{1,0:T(8,128)(2,1)}, bf16[128,1024]{1,0:T(8,128)(2,1)S(1)}, u32[]{:S(2)}, u32[]{:S(2)}) collective-permute-start(bf16[128,1024]{1,0:T(8,128)(2,1)} %get-tuple-element.24), channel_id=1, source_target_pairs={{0,1},{1,3},{2,0},{3,5},{4,2},{5,7},{6,4},{7,6},{8,10},{9,8},{10,1... | collective-permute-start | bytes 786440 | tf_op jit(solution)/shard_map/ppermute | solution.py:298
  20.2 8.1 %collective-permute-start.7 = (bf16[128,1024]{1,0:T(8,128)(2,1)S(1)}, bf16[128,1024]{1,0:T(8,128)(2,1)S(1)}, u32[]{:S(2)}, u32[]{:S(2)}) collective-permute-start(bf16[128,1024]{1,0:T(8,128)(2,1)S(1)} %collective-permute-done.6.rest_0_), channel_id=1, source_target_pairs={{0,2},{1,0},{2,4},{3,1},{4,6},{5,3},{6,7},{7,5},{8,9},{9,11},{10,8... | collective-permute-start | bytes 786440 | tf_op jit(solution)/shard_map/ppermute | solution.py:298
  21.3 24.1 %collective-permute-start.3 = (f32[8,1024]{1,0:T(8,128)S(1)}, f32[8,1024]{1,0:T(8,128)S(1)}, u32[]{:S(2)}, u32[]{:S(2)}) collective-permute-start(f32[8,1024]{1,0:T(8,128)S(1)} %constant_dynamic-update-slice_fusion.1), channel_id=1, source_target_pairs={{0,1},{1,0},{2,3},{3,2},{4,5},{5,4},{6,7},{7,6},{8,9},{9,8},{10,11... | collective-permute-start | bytes 98312 | tf_op jit(solution)/shard_map/ppermute | solution.py:306
  26.2 21.7 %collective-permute-start.11 = (bf16[128,1024]{1,0:T(8,128)(2,1)S(1)}, bf16[128,1024]{1,0:T(8,128)(2,1)}, u32[]{:S(2)}, u32[]{:S(2)}) collective-permute-start(bf16[128,1024]{1,0:T(8,128)(2,1)S(1)} %collective-permute-done.10.rest_4_), channel_id=1, source_target_pairs={{0,1},{1,3},{2,0},{3,5},{4,2},{5,7},{6,4},{7,6},{8,10},{9,8},{10,1... | collective-permute-start | bytes 786440 | tf_op jit(solution)/shard_map/ppermute | solution.py:298
  28.3 21.1 %collective-permute-start.8 = (bf16[128,1024]{1,0:T(8,128)(2,1)S(1)}, bf16[128,1024]{1,0:T(8,128)(2,1)}, u32[]{:S(2)}, u32[]{:S(2)}) collective-permute-start(bf16[128,1024]{1,0:T(8,128)(2,1)S(1)} %collective-permute-done.7.rest_1_), channel_id=1, source_target_pairs={{0,2},{1,0},{2,4},{3,1},{4,6},{5,3},{6,7},{7,5},{8,9},{9,11},{10,8... | collective-permute-start | bytes 786440 | tf_op jit(solution)/shard_map/ppermute | solution.py:298
  41.2 25.9 %all-to-all-start = ((bf16[8,32,1024]{2,1,0:T(8,128)(2,1)}), bf16[8,32,1024]{2,1,0:T(8,128)(2,1)S(1)}, u32[]{:S(2)}, u32[]{:S(2)}) async-start(bf16[8,32,1024]{2,1,0:T(8,128)(2,1)} %bitcast.7), calls=%async_computation | async-start | bytes 1048576 | tf_op jit(solution)/shard_map/all_to_all | solution.py:355
  45.5 7.9 %collective-permute-start.4 = (f32[8,1024]{1,0:T(8,128)S(1)}, f32[8,1024]{1,0:T(8,128)S(1)}, u32[]{:S(2)}, u32[]{:S(2)}) collective-permute-start(f32[8,1024]{1,0:T(8,128)S(1)} %constant_dynamic-update-slice_fusion), channel_id=1, source_target_pairs={{0,2},{1,3},{2,0},{3,1},{4,6},{5,7},{6,4},{7,5},{8,10},{9,11},{10,... | collective-permute-start | bytes 98312 | tf_op jit(solution)/shard_map/ppermute | solution.py:306
  47.4 15.8 %collective-permute-start.13 = (bf16[128,1024]{1,0:T(8,128)(2,1)S(1)}, bf16[128,1024]{1,0:T(8,128)(2,1)S(1)}, u32[]{:S(2)}, u32[]{:S(2)}) collective-permute-start(bf16[128,1024]{1,0:T(8,128)(2,1)S(1)} %collective-permute-done.6.rest_0_), channel_id=1, source_target_pairs={{0,8},{8,0},{16,24},{24,16},{1,9},{9,1},{17,25},{25,17},{2,10},{10... | collective-permute-start | bytes 786440 | tf_op jit(solution)/shard_map/ppermute | solution.py:301
  47.4 17.0 %collective-permute-start.17 = (bf16[128,1024]{1,0:T(8,128)(2,1)S(1)}, bf16[128,1024]{1,0:T(8,128)(2,1)S(1)}, u32[]{:S(2)}, u32[]{:S(2)}) collective-permute-start(bf16[128,1024]{1,0:T(8,128)(2,1)S(1)} %collective-permute-done.10.rest_4_), channel_id=1, source_target_pairs={{0,8},{8,0},{16,24},{24,16},{1,9},{9,1},{17,25},{25,17},{2,10},{10... | collective-permute-start | bytes 786440 | tf_op jit(solution)/shard_map/ppermute | solution.py:301
  47.9 17.2 %collective-permute-start.12 = (bf16[128,1024]{1,0:T(8,128)(2,1)}, bf16[128,1024]{1,0:T(8,128)(2,1)}, u32[]{:S(2)}, u32[]{:S(2)}) collective-permute-start(bf16[128,1024]{1,0:T(8,128)(2,1)} %collective-permute-done.11.rest_5_), channel_id=1, source_target_pairs={{0,1},{1,3},{2,0},{3,5},{4,2},{5,7},{6,4},{7,6},{8,10},{9,8},{10,1... | collective-permute-start | bytes 786440 | tf_op jit(solution)/shard_map/ppermute | solution.py:298
  49.4 16.2 %collective-permute-start.9 = (bf16[128,1024]{1,0:T(8,128)(2,1)}, bf16[128,1024]{1,0:T(8,128)(2,1)}, u32[]{:S(2)}, u32[]{:S(2)}) collective-permute-start(bf16[128,1024]{1,0:T(8,128)(2,1)} %collective-permute-done.8.rest_2_), channel_id=1, source_target_pairs={{0,2},{1,0},{2,4},{3,1},{4,6},{5,3},{6,7},{7,5},{8,9},{9,11},{10,8... | collective-permute-start | bytes 786440 | tf_op jit(solution)/shard_map/ppermute | solution.py:298
  53.4 9.8 %collective-permute-start.5 = (f32[8,1024]{1,0:T(8,128)S(1)}, f32[8,1024]{1,0:T(8,128)S(1)}, u32[]{:S(2)}, u32[]{:S(2)}) collective-permute-start(f32[8,1024]{1,0:T(8,128)S(1)} %add.250), channel_id=1, source_target_pairs={{0,4},{1,5},{2,6},{3,7},{4,0},{5,1},{6,2},{7,3},{8,12},{9,13},{10,... | collective-permute-start | bytes 98312 | tf_op jit(solution)/shard_map/ppermute | solution.py:306
  84.8 10.7 %collective-permute-start.20 = (bf16[1024,1024]{1,0:T(8,128)(2,1)}, bf16[1024,1024]{1,0:T(8,128)(2,1)}, u32[]{:S(2)}, u32[]{:S(2)}) collective-permute-start(bf16[1024,1024]{1,0:T(8,128)(2,1)} %weight_grad.3), channel_id=1, source_target_pairs={{0,8},{8,0},{16,24},{24,16},{1,9},{9,1},{17,25},{25,17},{2,10},{10... | collective-permute-start | bytes 6291464 | tf_op jit(solution)/shard_map/ppermute | solution.py:301
  96.6 6.4 %collective-permute-start.21 = (bf16[128,1024]{1,0:T(8,128)(2,1)S(1)}, bf16[128,1024]{1,0:T(8,128)(2,1)S(1)}, u32[]{:S(2)}, u32[]{:S(2)}) collective-permute-start(bf16[128,1024]{1,0:T(8,128)(2,1)S(1)} %add_convert_fusion.8), channel_id=1, source_target_pairs={{0,2},{1,0},{2,4},{3,1},{4,6},{5,3},{6,7},{7,5},{8,9},{9,11},{10,8... | collective-permute-start | bytes 786440 | tf_op jit(solution)/shard_map/ppermute | solution.py:298
  104.1 6.4 %collective-permute-start.22 = (bf16[128,1024]{1,0:T(8,128)(2,1)S(1)}, bf16[128,1024]{1,0:T(8,128)(2,1)S(1)}, u32[]{:S(2)}, u32[]{:S(2)}) collective-permute-start(bf16[128,1024]{1,0:T(8,128)(2,1)S(1)} %add_convert_fusion.7), channel_id=1, source_target_pairs={{0,2},{1,0},{2,4},{3,1},{4,6},{5,3},{6,7},{7,5},{8,9},{9,11},{10,8... | collective-permute-start | bytes 786440 | tf_op jit(solution)/shard_map/ppermute | solution.py:298
  119.3 6.5 %collective-permute-start.25 = (bf16[128,1024]{1,0:T(8,128)(2,1)S(1)}, bf16[128,1024]{1,0:T(8,128)(2,1)}, u32[]{:S(2)}, u32[]{:S(2)}) collective-permute-start(bf16[128,1024]{1,0:T(8,128)(2,1)S(1)} %get-tuple-element.21), channel_id=1, source_target_pairs={{0,1},{1,3},{2,0},{3,5},{4,2},{5,7},{6,4},{7,6},{8,10},{9,8},{10,1... | collective-permute-start | bytes 786440 | tf_op jit(solution)/shard_map/ppermute | solution.py:298
  126.9 7.7 %collective-permute-start.26 = (bf16[128,1024]{1,0:T(8,128)(2,1)S(1)}, bf16[128,1024]{1,0:T(8,128)(2,1)S(1)}, u32[]{:S(2)}, u32[]{:S(2)}) collective-permute-start(bf16[128,1024]{1,0:T(8,128)(2,1)S(1)} %add_convert_fusion.3), channel_id=1, source_target_pairs={{0,1},{1,3},{2,0},{3,5},{4,2},{5,7},{6,4},{7,6},{8,10},{9,8},{10,1... | collective-permute-start | bytes 786440 | tf_op jit(solution)/shard_map/ppermute | solution.py:298
  129.1 9.8 %collective-permute-start.30 = (f32[8,1024]{1,0:T(8,128)S(1)}, f32[8,1024]{1,0:T(8,128)S(1)}, u32[]{:S(2)}, u32[]{:S(2)}) collective-permute-start(f32[8,1024]{1,0:T(8,128)S(1)} %get-tuple-element.19), channel_id=1, source_target_pairs={{0,8},{8,0},{16,24},{24,16},{1,9},{9,1},{17,25},{25,17},{2,10},{10... | collective-permute-start | bytes 98312 | tf_op jit(solution)/shard_map/ppermute | solution.py:301
  129.2 27.7 %collective-permute-start.24 = (bf16[128,1024]{1,0:T(8,128)(2,1)S(1)}, bf16[128,1024]{1,0:T(8,128)(2,1)}, u32[]{:S(2)}, u32[]{:S(2)}) collective-permute-start(bf16[128,1024]{1,0:T(8,128)(2,1)S(1)} %get-tuple-element.20), channel_id=1, source_target_pairs={{0,2},{1,0},{2,4},{3,1},{4,6},{5,3},{6,7},{7,5},{8,9},{9,11},{10,8... | collective-permute-start | bytes 786440 | tf_op jit(solution)/shard_map/ppermute | solution.py:298
  136.5 20.5 %collective-permute-start.27 = (bf16[128,1024]{1,0:T(8,128)(2,1)}, bf16[128,1024]{1,0:T(8,128)(2,1)}, u32[]{:S(2)}, u32[]{:S(2)}) collective-permute-start(bf16[128,1024]{1,0:T(8,128)(2,1)} %add_convert_fusion.2), channel_id=1, source_target_pairs={{0,1},{1,3},{2,0},{3,5},{4,2},{5,7},{6,4},{7,6},{8,10},{9,8},{10,1... | collective-permute-start | bytes 786440 | tf_op jit(solution)/shard_map/ppermute | solution.py:298
  151.7 25.0 %all-to-all-start.1 = ((bf16[8,32,1024]{2,1,0:T(8,128)(2,1)}), bf16[8,32,1024]{2,1,0:T(8,128)(2,1)S(1)}, u32[]{:S(2)}, u32[]{:S(2)}) async-start(bf16[8,32,1024]{2,1,0:T(8,128)(2,1)} %bitcast.46), calls=%async_computation.1 | async-start | bytes 1048576 | tf_op jit(solution)/shard_map/all_to_all | solution.py:407
  158.2 15.9 %collective-permute-start.28 = (bf16[128,1024]{1,0:T(8,128)(2,1)S(1)}, bf16[128,1024]{1,0:T(8,128)(2,1)}, u32[]{:S(2)}, u32[]{:S(2)}) collective-permute-start(bf16[128,1024]{1,0:T(8,128)(2,1)S(1)} %add_convert_fusion.1), channel_id=1, source_target_pairs={{0,16},{8,24},{16,0},{24,8},{1,17},{9,25},{17,1},{25,9},{2,18},{10... | collective-permute-start | bytes 786440 | tf_op jit(solution)/shard_map/ppermute | solution.py:301
  175.9 13.5 %collective-permute-start.29 = (bf16[128,1024]{1,0:T(8,128)(2,1)}, bf16[128,1024]{1,0:T(8,128)(2,1)S(1)}, u32[]{:S(2)}, u32[]{:S(2)}) collective-permute-start(bf16[128,1024]{1,0:T(8,128)(2,1)} %add_convert_fusion), channel_id=1, source_target_pairs={{0,8},{8,0},{16,24},{24,16},{1,9},{9,1},{17,25},{25,17},{2,10},{10... | collective-permute-start | bytes 786440 | tf_op jit(solution)/shard_map/ppermute | solution.py:301
  (49 other events, 370.9 us)

commit v2 on v1

v2 whole, which is shorter than its diff:
```python
import functools
import math

import jax
import jax.numpy as jnp
from jax import lax
from jax.experimental import pallas as pl
from jax.experimental.pallas import tpu as pltpu
from jax.sharding import PartitionSpec as P

HEADS = 8
EPS = 1e-06
F32 = jnp.float32
BF16 = jnp.bfloat16
TILE = 256


def dot_nn(a, b):
    return lax.dot_general(a, b, (((1,), (0,)), ((), ())), preferred_element_type=F32)


def dot_nt(a, b):
    return lax.dot_general(a, b, (((1,), (1,)), ((), ())), preferred_element_type=F32)


def dot_tn(a, b):
    return lax.dot_general(a, b, (((0,), (0,)), ((), ())), preferred_element_type=F32)


def inv_rms(rows):
    return lax.rsqrt(jnp.mean(rows * rows, axis=-1, keepdims=True) + EPS)


def norm_pull(rows, gain, grad):
    scale = inv_rms(rows)
    scaled = grad * gain
    inner = jnp.mean(scaled * rows, axis=-1, keepdims=True)
    return scale * scaled - rows * (scale * scale * scale * inner)


def spans(total, size):
    size = min(size, total)
    return [pl.ds(at, size) for at in range(0, total, size)]


def temporal_forward(
    done_ref, rows_ref, gain_ref, w_qkv_hbm, w_out_hbm, h1_ref, qkv_ref, probs_ref,
    w_qkv, w_out, mixed, sems,
):
    length, width = rows_ref.shape
    size = width // HEADS
    copies = []
    for part in range(3):
        span = pl.ds(part * width, width)
        copies.append(
            pltpu.make_async_copy(w_qkv_hbm.at[:, span], w_qkv.at[:, span], sems.at[part])
        )
    copies.append(pltpu.make_async_copy(w_out_hbm, w_out, sems.at[3]))
    for copy in copies:
        copy.start()
    rows = rows_ref[...].astype(F32)
    normed = (rows * inv_rms(rows) * gain_ref[...]).astype(BF16)
    for part in range(3):
        copies[part].wait()
        for at in range(part * width, (part + 1) * width, TILE):
            span = pl.ds(at, TILE)
            qkv_ref[:, span] = dot_nn(normed, w_qkv[:, span]).astype(BF16)
    done = done_ref[0]
    query_at = lax.broadcasted_iota(jnp.int32, (length, length), 0)
    key_at = lax.broadcasted_iota(jnp.int32, (length, length), 1)
    allowed = (key_at <= query_at) & ((key_at > done) == (query_at > done))
    bias = jnp.where(allowed, 0.0, -1e30)
    for head in range(HEADS):
        queries = qkv_ref[:, pl.ds(head * size, size)]
        keys = qkv_ref[:, pl.ds(width + head * size, size)]
        values = qkv_ref[:, pl.ds(2 * width + head * size, size)]
        scores = dot_nt(queries, keys) * (1.0 / math.sqrt(size)) + bias
        weights = jnp.exp(scores - jnp.max(scores, axis=-1, keepdims=True))
        probs = weights * (1.0 / jnp.sum(weights, axis=-1, keepdims=True))
        probs = probs.astype(BF16)
        probs_ref[head] = probs
        mixed[:, pl.ds(head * size, size)] = dot_nn(probs, values).astype(BF16)
    copies[3].wait()
    for span in spans(width, TILE):
        added = dot_nn(mixed[...], w_out[:, span])
        h1_ref[:, span] = (rows_ref[:, span].astype(F32) + added).astype(BF16)


def temporal_backward(
    grad_ref, rows_ref, gain_ref, qkv_ref, probs_ref, w_qkv, w_out, out_ref,
    grad_mixed, grad_qkv, grad_normed,
):
    length, width = rows_ref.shape
    size = width // HEADS
    scale = 1.0 / math.sqrt(size)
    grad = grad_ref[...]
    for span in spans(width, TILE):
        grad_mixed[:, span] = dot_nt(grad, w_out[span, :]).astype(BF16)
    for head in range(HEADS):
        query_span = pl.ds(head * size, size)
        key_span = pl.ds(width + head * size, size)
        value_span = pl.ds(2 * width + head * size, size)
        probs = probs_ref[head]
        head_grad = grad_mixed[:, query_span]
        grad_qkv[:, value_span] = dot_tn(probs, head_grad).astype(BF16)
        grad_probs = dot_nt(head_grad, qkv_ref[:, value_span])
        wide = probs.astype(F32)
        inner = jnp.sum(wide * grad_probs, axis=-1, keepdims=True)
        grad_scores = (wide * (grad_probs - inner) * scale).astype(BF16)
        grad_qkv[:, query_span] = dot_nn(grad_scores, qkv_ref[:, key_span]).astype(BF16)
        grad_qkv[:, key_span] = dot_tn(grad_scores, qkv_ref[:, query_span]).astype(BF16)
    for span in spans(width, TILE):
        grad_normed[:, span] = dot_nt(grad_qkv[...], w_qkv[span, :])
    rows = rows_ref[...].astype(F32)
    pulled = norm_pull(rows, gain_ref[...], grad_normed[...])
    out_ref[...] = (grad_ref[...].astype(F32) + pulled).astype(BF16)


def agent_kernel(
    blocks, group_steps, place_ref, rows_ref, alive_ref, target_ref, gain_ref, value_ref,
    shard_ref, own_ref, *rest,
):
    moved = rest[: 2 * blocks]
    grad_ref, pack_ref, keep_ref, extra_ref, u_ref, predicted_ref = rest[2 * blocks : 2 * blocks + 6]
    w_all, qk, grad_qk, probs_all, slopes, column, grad_normed, sems = rest[2 * blocks + 6 :]
    total_rows, width = rows_ref.shape
    size = width // HEADS
    scale = 1.0 / math.sqrt(size)
    normed_ref = pack_ref.at[pl.ds(0, total_rows), :]
    groups, group_rows = alive_ref.shape[0], alive_ref.shape[2]
    agents = group_rows // group_steps
    local_steps = total_rows // agents
    depth, block_width = own_ref.shape
    middle = width // 2
    w_q, w_k = w_all.at[:, pl.ds(0, width)], w_all.at[:, pl.ds(block_width, width)]
    w_v = [
        w_all.at[:, pl.ds(width, middle)],
        w_all.at[:, pl.ds(block_width + width, middle)],
    ]
    core, other = place_ref[2 * blocks + 1], place_ref[2 * blocks + 2]

    def row_span(at):
        return pl.ds(pl.multiple_of(place_ref[at] * depth, depth), depth)

    def column_span(start, length):
        return pl.ds(pl.multiple_of(start, 128), length)

    own_rows = row_span(2 * blocks)
    other_at = other * block_width
    moves = [
        (own_ref, w_all.at[own_rows, column_span(core * block_width, block_width)]),
        (
            own_ref.at[:, pl.ds(block_width - 128, 128)],
            w_all.at[own_rows, column_span(other_at + block_width - 128, 128)],
        ),
        (
            shard_ref.at[:, column_span(other * width, width)],
            w_all.at[own_rows, column_span(other_at, width)],
        ),
        (
            shard_ref.at[:, column_span(2 * width + other * middle, middle)],
            w_all.at[own_rows, column_span(other_at + width, middle)],
        ),
    ]
    for at in range(2 * blocks):
        half = core if at < blocks else other
        moves.append(
            (moved[at], w_all.at[row_span(at), column_span(half * block_width, block_width)])
        )
    copies = [
        pltpu.make_async_copy(source, target, sems.at[at])
        for at, (source, target) in enumerate(moves)
    ]
    for copy in copies:
        copy.start()

    def row_spans(group):
        if groups == 1:
            return [(pl.ds(0, total_rows), pl.ds(0, total_rows))]
        return [
            (
                pl.ds(agent * local_steps + group * group_steps, group_steps),
                pl.ds(group * group_rows + agent * group_steps, group_steps),
            )
            for agent in range(agents)
        ]

    def to_column(row):
        return jnp.transpose(jnp.broadcast_to(row, (128, row.shape[1])))[:, :1]

    for group in range(groups):
        for source, target in row_spans(group):
            rows = rows_ref[source, :].astype(F32)
            normed_ref[target, :] = (rows * inv_rms(rows) * gain_ref[...]).astype(BF16)
            column[target, :] = jnp.broadcast_to(
                jnp.sum(rows * value_ref[...], axis=-1, keepdims=True), (rows.shape[0], 128)
            )
    for copy in copies:
        copy.wait()

    u_parts = jnp.transpose(w_all[:, pl.ds(block_width - 128, 128)].astype(F32))
    u_high, u_low = u_parts[0:1], u_parts[1:2]
    u_ref[...] = u_high + u_low
    part_at = lax.broadcasted_iota(jnp.int32, (2 * HEADS, width), 0)
    head_at = lax.broadcasted_iota(jnp.int32, (2 * HEADS, width), 1) // size
    by_head = jnp.where(
        head_at == part_at % HEADS, jnp.where(part_at < HEADS, u_high, u_low), 0.0
    ).astype(BF16)
    both = dot_nt(by_head[:, :middle], w_v[0][...]) + dot_nt(by_head[:, middle:], w_v[1][...])
    folded = both[:HEADS] + both[HEADS:]
    folded_high = folded.astype(BF16)
    folded_parts = jnp.concatenate(
        [folded_high.astype(F32), folded - folded_high.astype(F32)], axis=0
    ).astype(BF16)
    both = dot_nt(folded_parts, normed_ref[...])
    folded_rows = both[:HEADS] + both[HEADS:]
    for at in range(0, width, TILE):
        qk[:, pl.ds(at, TILE)] = dot_nn(normed_ref[...], w_q[:, pl.ds(at, TILE)]).astype(BF16)
    for at in range(0, width, TILE):
        qk[:, pl.ds(width + at, TILE)] = dot_nn(
            normed_ref[...], w_k[:, pl.ds(at, TILE)]
        ).astype(BF16)

    row_at = lax.broadcasted_iota(jnp.int32, (group_rows, group_rows), 0)
    col_at = lax.broadcasted_iota(jnp.int32, (group_rows, group_rows), 1)
    same_step = row_at % group_steps == col_at % group_steps
    pulls = []
    for group in range(groups):
        group_span = pl.ds(group * group_rows, group_rows)
        alive = alive_ref[group]
        allowed = same_step & ((alive > 0.5) | (row_at == col_at))
        bias = jnp.where(allowed, 0.0, -1e30)
        predicted = column[group_span, :1]
        for head in range(HEADS):
            queries = qk[group_span, pl.ds(head * size, size)]
            keys = qk[group_span, pl.ds(width + head * size, size)]
            scores = dot_nt(queries, keys) * scale + bias
            weights = jnp.exp(scores - jnp.max(scores, axis=-1, keepdims=True))
            probs = weights * (1.0 / jnp.sum(weights, axis=-1, keepdims=True))
            weighted = probs * folded_rows[
                head : head + 1, group * group_rows : (group + 1) * group_rows
            ]
            pooled = jnp.sum(weighted, axis=-1, keepdims=True)
            predicted = predicted + pooled
            probs_all[group * HEADS + head] = probs
            slopes[group * HEADS + head] = (weighted - probs * pooled) * scale
        error = 32.0 * to_column(alive) * (predicted - to_column(target_ref[group]))
        predicted_ref[group] = jnp.transpose(jnp.broadcast_to(predicted, (group_rows, 128)))[:8]
        column[group_span, :] = jnp.broadcast_to(error, (group_rows, 128))
        pull_rows = []
        for head in range(HEADS):
            query_span = pl.ds(head * size, size)
            key_span = pl.ds(width + head * size, size)
            grad_scores = (slopes[group * HEADS + head] * error).astype(BF16)
            grad_qk[group_span, query_span] = dot_nn(
                grad_scores, qk[group_span, key_span]
            ).astype(BF16)
            grad_qk[group_span, key_span] = dot_tn(
                grad_scores, qk[group_span, query_span]
            ).astype(BF16)
            pull_rows.append(
                jnp.sum(probs_all[group * HEADS + head] * error, axis=0, keepdims=True)
            )
        pulls.append(jnp.concatenate(pull_rows, axis=0))
    pull = jnp.concatenate(pulls, axis=1) if groups > 1 else pulls[0]
    pull = pull.astype(BF16)
    twice = jnp.concatenate([pull, pull], axis=0)
    for at in range(0, width, TILE):
        span = pl.ds(at, TILE)
        grad_normed[:, span] = (
            dot_nt(grad_qk[:, pl.ds(0, width)], w_q[span, :])
            + dot_nt(grad_qk[:, pl.ds(width, width)], w_k[span, :])
            + dot_tn(twice, folded_parts[:, at : at + TILE])
        )
    for group in range(groups):
        for source, target in row_spans(group):
            rows = rows_ref[source, :].astype(F32)
            pulled = norm_pull(rows, gain_ref[...], grad_normed[target, :])
            top = column[target, :1] * value_ref[...]
            grad_ref[source, :] = (top + pulled).astype(BF16)
    keep_ref[...] = grad_qk[:, column_span(core * width, width)]
    pack_ref[pl.ds(total_rows, total_rows), :] = grad_qk[:, column_span(other * width, width)]

    folded_grad = dot_nn(pull, normed_ref[...])
    folded_grad_low = folded_grad.astype(BF16)
    pooled = jnp.concatenate(
        [dot_nn(folded_grad_low, w_v[0][...]), dot_nn(folded_grad_low, w_v[1][...])], axis=1
    )
    pooled = jnp.sum(
        jnp.where(head_at[:HEADS] == part_at[:HEADS], pooled, 0.0), axis=0, keepdims=True
    )
    extra = jnp.concatenate(
        [folded_grad, pooled, jnp.zeros((127 - HEADS, width), F32)], axis=0
    )
    extra_ref[...] = jnp.transpose(extra).astype(BF16)


def weight_grad_kernel(place_ref, pack_ref, keep_ref, moved_ref, extra_ref, *rest):
    outs, (total, sems) = rest[:-2], rest[-2:]
    half, width = keep_ref.shape
    depth = width // len(outs)
    own, other = pl.ds(0, half), pl.ds(half, half)
    total[:, pl.ds(width, 128)] = extra_ref[...]
    for rows in spans(width, TILE):
        for columns in spans(width, TILE):
            total[rows, columns] = (
                dot_tn(pack_ref[own, rows], keep_ref[:, columns])
                + dot_tn(moved_ref[own, rows], moved_ref[other, columns])
            ).astype(BF16)
    copies = [
        pltpu.make_async_copy(
            total.at[pl.ds(pl.multiple_of(place_ref[at] * depth, depth), depth), :],
            out,
            sems.at[at],
        )
        for at, out in enumerate(outs)
    ]
    for copy in copies:
        copy.start()
    for copy in copies:
        copy.wait()


def pack_block_kernel(core_ref, qk_ref, v_ref, w_out_ref, value_ref, out_ref):
    width, middle = qk_ref.shape[1], v_ref.shape[1]
    out_ref[:, pl.ds(0, width)] = qk_ref[...]
    out_ref[:, pl.ds(width, middle)] = v_ref[...]
    u = jnp.sum(w_out_ref[...].astype(F32) * value_ref[...], axis=-1, keepdims=True)
    high = u.astype(BF16).astype(F32)
    lane = lax.broadcasted_iota(jnp.int32, (qk_ref.shape[0], 128), 1)
    parts = jnp.where(lane == 0, high, jnp.where(lane == 1, u - high, 0.0))
    out_ref[:, pl.ds(width + middle, 128)] = parts.astype(BF16)


def finish_kernel(core_ref, own_ref, other_ref, u_ref, value_ref, qkv_ref, out_ref):
    width = u_ref.shape[1]
    size = width // HEADS
    own, other = own_ref[:, pl.ds(0, width)], other_ref[:, pl.ds(0, width)]
    core = core_ref[0]
    qkv_ref[:, pl.ds(pl.multiple_of(core * width, width), width)] = own.astype(F32)
    qkv_ref[:, pl.ds(pl.multiple_of((1 - core) * width, width), width)] = other.astype(F32)
    extra = own_ref[:, pl.ds(width, 128)].astype(F32) + other_ref[:, pl.ds(width, 128)].astype(F32)
    for head in range(HEADS):
        qkv_ref[:, pl.ds(2 * width + head * size, size)] = (
            extra[:, head : head + 1] * u_ref[:, pl.ds(head * size, size)]
        )
    out_ref[...] = extra[:, HEADS : HEADS + 1] * value_ref[...]


def any_spec():
    return pl.BlockSpec(memory_space=pl.ANY)


def hbm_spec():
    return pl.BlockSpec(memory_space=pltpu.HBM)


def vmem_spec():
    return pl.BlockSpec(memory_space=pltpu.VMEM)


def smem_spec():
    return pl.BlockSpec(memory_space=pltpu.SMEM)


def params(mebibytes):
    return pltpu.CompilerParams(vmem_limit_bytes=mebibytes * 1024 * 1024)


def cost(flops, moved):
    return pl.CostEstimate(flops=flops, bytes_accessed=moved, transcendentals=0)


def ring_order(count):
    return list(range(0, count, 2)) + list(range(count - 1, 0, -2))


def per_device(
    env_count, tm_count,
    hidden, done_step, alive, targets, gain_t, w_qkv_t, w_out_t, gain_a, w_qkv_a, w_out_a, w_value,
):
    length, width = hidden.shape[2:]
    agents, local_steps = alive.shape[1:]
    depth = w_qkv_a.shape[0]
    size = width // HEADS
    env_at = lax.axis_index("env")
    tm_at = lax.axis_index("tm")
    core = env_at % 2
    order = ring_order(tm_count)
    spot = [order.index(at) for at in range(tm_count)]
    order_array = jnp.array(order, jnp.int32)
    my_spot = jnp.array(spot, jnp.int32)[tm_at]

    ways = [1 if at in (0, 3) else -1 for at in range(env_count)]
    way = jnp.array(ways, jnp.int32)[env_at]

    def ring(block):
        pairs = [
            (env * tm_count + at, env * tm_count + order[(spot[at] + ways[env]) % tm_count])
            for env in range(env_count)
            for at in range(tm_count)
        ]
        return lax.ppermute(block, ("env", "tm"), pairs)

    def swap_core(block):
        return lax.ppermute(block, "env", [(at, at ^ 1) for at in range(env_count)])

    def swap_chip(block):
        return lax.ppermute(block, "env", [(at, at ^ 2) for at in range(env_count)])

    far = tm_count // 2
    near = tm_count - 1 - far

    def places(hops):
        return order_array[(my_spot + way * jnp.array(hops, jnp.int32)) % tm_count]

    core_index = core[None].astype(jnp.int32)
    block_width = width + width // 2 + 128
    own_block = pl.pallas_call(
        pack_block_kernel,
        name="pack_block",
        out_shape=jax.ShapeDtypeStruct((depth, block_width), BF16),
        grid_spec=pltpu.PrefetchScalarGridSpec(
            num_scalar_prefetch=1,
            grid=(1,),
            in_specs=[
                pl.BlockSpec((depth, width), lambda at, core: (0, core[0])),
                pl.BlockSpec((depth, width // 2), lambda at, core: (0, 4 + core[0])),
                pl.BlockSpec((depth, width), lambda at, core: (0, 0)),
                pl.BlockSpec((1, width), lambda at, core: (0, 0)),
            ],
            out_specs=pl.BlockSpec((depth, block_width), lambda at, core: (0, 0)),
        ),
        compiler_params=params(16),
        cost_estimate=cost(2 * depth * width, 8 * depth * width),
    )(core_index, w_qkv_a, w_qkv_a, w_out_a, w_value[None])
    first_block = ring(own_block)

    rows = hidden[0, 0]
    h1, qkv, probs = pl.pallas_call(
        temporal_forward,
        name="temporal_forward",
        out_shape=(
            jax.ShapeDtypeStruct((length, width), BF16),
            jax.ShapeDtypeStruct((length, 3 * width), BF16),
            jax.ShapeDtypeStruct((HEADS, length, length), BF16),
        ),
        in_specs=[smem_spec(), vmem_spec(), vmem_spec(), hbm_spec(), hbm_spec()],
        out_specs=[vmem_spec()] * 3,
        scratch_shapes=[
            pltpu.VMEM((width, 3 * width), BF16),
            pltpu.VMEM((width, width), BF16),
            pltpu.VMEM((length, width), BF16),
            pltpu.SemaphoreType.DMA((4,)),
        ],
        compiler_params=params(24),
        cost_estimate=cost(8 * length * width * width, 8 * width * width),
    )(done_step[0], rows, gain_t[None], w_qkv_t, w_out_t)
    h1, first_block = lax.optimization_barrier((h1, first_block))
    lifted = lax.all_to_all(h1, "tm", split_axis=0, concat_axis=0, tiled=True)

    ringed, crossed = [first_block], []
    for hop in range(1, far):
        if hop <= near:
            crossed.append(swap_chip(ringed[-1]))
        ringed.append(ring(ringed[-1]))
    crossed += [swap_chip(block) for block in ringed[len(crossed) : near]]
    own_blocks = ringed + crossed
    other_blocks = [swap_core(block) for block in own_blocks]
    ahead_hops = list(range(1, far + 1))
    behind_hops = list(range(1, near + 1))
    block_places = jnp.concatenate(
        [
            places([-hop for hop in ahead_hops] + behind_hops),
            places(ahead_hops + [-hop for hop in behind_hops]),
            jnp.stack([tm_at, core, 1 - core]).astype(jnp.int32),
        ]
    )

    group_steps = 16 if local_steps % 16 == 0 else local_steps
    groups = local_steps // group_steps
    group_rows = agents * group_steps

    def grouped(block):
        block = block.reshape(agents, groups, group_steps)
        return jnp.swapaxes(block, 0, 1).reshape(groups, 1, group_rows)

    total_rows = agents * local_steps
    grad_lifted, pack, keep, extra, u, predicted = pl.pallas_call(
        functools.partial(agent_kernel, tm_count - 1, group_steps),
        name="agent_block",
        out_shape=(
            jax.ShapeDtypeStruct((total_rows, width), BF16),
            jax.ShapeDtypeStruct((2 * total_rows, width), BF16),
            jax.ShapeDtypeStruct((total_rows, width), BF16),
            jax.ShapeDtypeStruct((width, 128), BF16),
            jax.ShapeDtypeStruct((1, width), F32),
            jax.ShapeDtypeStruct((groups, 8, group_rows), F32),
        ),
        in_specs=[smem_spec()] + [vmem_spec()] * (2 * tm_count + 5),
        out_specs=[vmem_spec()] * 6,
        scratch_shapes=[
            pltpu.VMEM((width, 2 * block_width), BF16),
            pltpu.VMEM((total_rows, 2 * width), BF16),
            pltpu.VMEM((total_rows, 2 * width), BF16),
            pltpu.VMEM((groups * HEADS, group_rows, group_rows), F32),
            pltpu.VMEM((groups * HEADS, group_rows, group_rows), F32),
            pltpu.VMEM((total_rows, 128), F32),
            pltpu.VMEM((total_rows, width), F32),
            pltpu.SemaphoreType.DMA((2 * tm_count + 2,)),
        ],
        compiler_params=params(36),
        cost_estimate=cost(8 * total_rows * width * width, 4 * width * width),
    )(
        block_places, lifted, grouped(alive[0].astype(F32)), grouped(targets[0]), gain_a[None],
        w_value[None], w_qkv_a, own_block, *own_blocks, *other_blocks,
    )
    values = predicted[:, 0].reshape(groups, agents, group_steps)
    values = jnp.swapaxes(values, 0, 1).reshape(1, agents, local_steps)

    returned = lax.all_to_all(grad_lifted, "tm", split_axis=0, concat_axis=0, tiled=True)

    moved = swap_core(pack)
    hops = [0] + ahead_hops + [-hop for hop in behind_hops]
    terms = pl.pallas_call(
        weight_grad_kernel,
        name="weight_grad",
        out_shape=[jax.ShapeDtypeStruct((depth, width + 128), BF16)] * tm_count,
        in_specs=[smem_spec()] + [vmem_spec()] * 4,
        out_specs=[any_spec()] * tm_count,
        scratch_shapes=[
            pltpu.VMEM((width, width + 128), BF16),
            pltpu.SemaphoreType.DMA((tm_count,)),
        ],
        compiler_params=params(20),
        cost_estimate=cost(4 * total_rows * width * width, 4 * width * width),
    )(places(hops), pack, keep, moved, extra)
    term = dict(zip(hops, terms))
    chip_terms = {hop: swap_chip(term[-hop]) for hop in reversed(behind_hops)}
    travelling = ring(term[far])
    for hop in range(far - 1, 0, -1):
        travelling = travelling.astype(F32) + term[hop].astype(F32)
        if hop in chip_terms:
            travelling = travelling + chip_terms[hop].astype(F32)
        travelling = ring(travelling.astype(BF16))
    reduced = (travelling.astype(F32) + term[0].astype(F32)).astype(BF16)
    reduced = (reduced.astype(F32) + swap_chip(reduced).astype(F32)).astype(BF16)
    other = swap_core(reduced)
    qkv_grad, out_grad = pl.pallas_call(
        finish_kernel,
        name="finish",
        out_shape=(
            jax.ShapeDtypeStruct((depth, 3 * width), F32),
            jax.ShapeDtypeStruct((depth, width), F32),
        ),
        in_specs=[smem_spec()] + [vmem_spec()] * 4,
        out_specs=[vmem_spec()] * 2,
        compiler_params=params(16),
        cost_estimate=cost(8 * depth * width, 20 * depth * width),
    )(core_index, reduced, other, u, w_value[None])

    input_grad = pl.pallas_call(
        temporal_backward,
        name="temporal_backward",
        out_shape=jax.ShapeDtypeStruct((length, width), BF16),
        in_specs=[vmem_spec()] * 7,
        out_specs=vmem_spec(),
        scratch_shapes=[
            pltpu.VMEM((length, width), BF16),
            pltpu.VMEM((length, 3 * width), BF16),
            pltpu.VMEM((length, width), F32),
        ],
        compiler_params=params(30),
        cost_estimate=cost(8 * length * width * width, 8 * width * width),
    )(returned, rows, gain_t[None], qkv, probs, w_qkv_t, w_out_t)
    return values, input_grad[None, None], qkv_grad, out_grad


def solution(mesh):
    in_specs = (
        P("env", "tm", None, None),
        P("env", "tm"),
        P("env", None, "tm"),
        P("env", None, "tm"),
        P(),
        P(),
        P(),
        P(),
        P("tm", None),
        P("tm", None),
        P(),
    )
    out_specs = (P("env", None, "tm"), P("env", "tm", None, None), P("tm", None), P("tm", None))
    body = functools.partial(per_device, mesh.shape["env"], mesh.shape["tm"])
    return jax.shard_map(
        body, mesh=mesh, in_specs=in_specs, out_specs=out_specs, check_vma=False
    )
```

time: 193 us -> 144 us (0.75)
  the two profiles are of different devices: /device:TPU:0 before, /device:TPU:23 now
where the time goes in v2:
time: 144 us; the launch traced here: 143 us
  starting transfers between devices  51.8 us (36%)
  waiting for transfers between devices  33.3 us (23%)
  Pallas kernels  27.6 us (19%)
  local copies, waits for them, and re-layouts  24 us (17%)
  other arithmetic  4.85 us (3%)
  between operations  1.64 us (1%)
    ppermute x9, starting transfers between devices, swap_core(): return lax.ppermute(block, 'env', [(at, at ^ 1) for at in range(env_count)])  29.5 us
    ppermute x7, waiting for transfers between devices, swap_chip(): return lax.ppermute(block, 'env', [(at, at ^ 2) for at in range(env_count)])  22.3 us
    unnamed x64, local copies, waits for them, and re-layouts  19.7 us
    ppermute x8, waiting for transfers between devices, ring(): return lax.ppermute(block, ('env', 'tm'), pairs)  10.3 us
    pallas_call x1, Pallas kernels, per_device(): pl.pallas_call(functools.partial(agent_kernel, tm_count - 1, group_steps)...  9.59 us
    ppermute x7, starting transfers between devices, swap_chip(): return lax.ppermute(block, 'env', [(at, at ^ 2) for at in range(env_count)])  7.99 us
    all_to_all x1, starting transfers between devices, per_device(): lax.all_to_all(grad_lifted, 'tm', split_axis=0, concat_axis=0, tiled=True)  6.75 us
    pallas_call x1, Pallas kernels, per_device(): pl.pallas_call(temporal_backward, name='temporal_backward', out_shape=jax...  6.45 us
  transfers between devices with their start and end apart: 26, of which 9 were waited for; matrix products, arithmetic and copies ran while one was open for 6% of the time, Pallas kernels for 8%

profile of v2, /device:TPU:23, one launch (start us, length us, event | category | flops | bytes accessed | tf_op | source)
XLA Modules:
  0.0 143.2 jit_solution(4889475869066605781)
XLA Ops:
  4.6 2.8 %copy-done = bf16[1024,3072]{1,0:T(8,128)(2,1)S(1)} copy-done((bf16[1024,3072]{1,0:T(8,128)(2,1)S(1)}, bf16[1024,3072]{1,0:T(8,128)(2,1)}, u32[]{:S(2)}) %copy-start) | copy-done | bytes 6291480
  8.5 5.4 %temporal_forward.1 = (bf16[256,1024]{1,0:T(8,128)(2,1)S(1)}, bf16[256,3072]{1,0:T(8,128)(2,1)S(1)}, bf16[8,256,256]{2,1,0:T(8,128)(2,1)S(1)}) custom-call(s32[1]{0:T(128)} %bitcast.22.done_ref, bf16[256,1024]{1,0:T(8,128)(2,1)S(1)} %bitcast.23, f32[1,1024]{1,0:T(1,128)S(1)} %bitcast.29, bf16[1024,3072]{1,0:T(8,128)(2,1)S(1)} %copy-done, ...), custom_call_target="tpu_custom_call" | custom-call | flops 2147483648 | bytes 8388608 | tf_op jit(solution)/shard_map/temporal_forward/pallas_call | solution.py:440
  16.4 1.5 %collective-permute-start.4 = (bf16[128,1664]{1,0:T(8,128)(2,1)}, bf16[128,1664]{1,0:T(8,128)(2,1)}, u32[]{:S(2)}, u32[]{:S(2)}) collective-permute-start(bf16[128,1664]{1,0:T(8,128)(2,1)} %collective-permute-done.rest_0_), channel_id=1, source_target_pairs={{0,16},{8,24},{16,0},{24,8},{1,17},{9,25},{17,1},{25,9},{2,18},{10... | collective-permute-start | bytes 1277960 | tf_op jit(solution)/shard_map/ppermute | solution.py:409
  17.8 6.0 %collective-permute-done.1.rest_1_ = bf16[128,1664]{1,0:T(8,128)(2,1)} collective-permute-done((bf16[128,1664]{1,0:T(8,128)(2,1)}, bf16[128,1664]{1,0:T(8,128)(2,1)}, u32[]{:S(2)}, u32[]{:S(2)}) %collective-permute-start.1) | collective-permute-done | bytes 426016 | tf_op jit(solution)/shard_map/ppermute | solution.py:403
  23.9 5.8 %all-to-all-start = ((bf16[8,32,1024]{2,1,0:T(8,128)(2,1)}), bf16[8,32,1024]{2,1,0:T(8,128)(2,1)S(1)}, u32[]{:S(2)}, u32[]{:S(2)}) async-start(bf16[8,32,1024]{2,1,0:T(8,128)(2,1)} %bitcast.28), calls=%async_computation | async-start | bytes 1048576 | tf_op jit(solution)/shard_map/all_to_all | solution.py:460
  29.7 2.6 %collective-permute-start.7 = (bf16[128,1664]{1,0:T(8,128)(2,1)}, bf16[128,1664]{1,0:T(8,128)(2,1)}, u32[]{:S(2)}, u32[]{:S(2)}) collective-permute-start(bf16[128,1664]{1,0:T(8,128)(2,1)} %collective-permute-done.rest_0_), channel_id=1, source_target_pairs={{0,8},{8,0},{16,24},{24,16},{1,9},{9,1},{17,25},{25,17},{2,10},{10... | collective-permute-start | bytes 1277960 | tf_op jit(solution)/shard_map/ppermute | solution.py:406
  32.7 1.4 %collective-permute-start.6 = (bf16[128,1664]{1,0:T(8,128)(2,1)}, bf16[128,1664]{1,0:T(8,128)(2,1)}, u32[]{:S(2)}, u32[]{:S(2)}) collective-permute-start(bf16[128,1664]{1,0:T(8,128)(2,1)} %collective-permute-done.2.rest_2_), channel_id=1, source_target_pairs={{0,16},{8,24},{16,0},{24,8},{1,17},{9,25},{17,1},{25,9},{2,18},{10... | collective-permute-start | bytes 1277960 | tf_op jit(solution)/shard_map/ppermute | solution.py:409
  35.4 8.7 %collective-permute-start.8 = (bf16[128,1664]{1,0:T(8,128)(2,1)}, bf16[128,1664]{1,0:T(8,128)(2,1)}, u32[]{:S(2)}, u32[]{:S(2)}) collective-permute-start(bf16[128,1664]{1,0:T(8,128)(2,1)} %collective-permute-done.1.rest_1_), channel_id=1, source_target_pairs={{0,8},{8,0},{16,24},{24,16},{1,9},{9,1},{17,25},{25,17},{2,10},{10... | collective-permute-start | bytes 1277960 | tf_op jit(solution)/shard_map/ppermute | solution.py:406
  44.2 1.7 %collective-permute-start.12 = (bf16[128,1664]{1,0:T(8,128)(2,1)}, bf16[128,1664]{1,0:T(8,128)(2,1)}, u32[]{:S(2)}, u32[]{:S(2)}) collective-permute-start(bf16[128,1664]{1,0:T(8,128)(2,1)} %collective-permute-done.5.rest_5_), channel_id=1, source_target_pairs={{0,8},{8,0},{16,24},{24,16},{1,9},{9,1},{17,25},{25,17},{2,10},{10... | collective-permute-start | bytes 1277960 | tf_op jit(solution)/shard_map/ppermute | solution.py:406
  45.9 6.0 %collective-permute-done.6.rest_6_ = bf16[128,1664]{1,0:T(8,128)(2,1)} collective-permute-done((bf16[128,1664]{1,0:T(8,128)(2,1)}, bf16[128,1664]{1,0:T(8,128)(2,1)}, u32[]{:S(2)}, u32[]{:S(2)}) %collective-permute-start.6) | collective-permute-done | bytes 426016 | tf_op jit(solution)/shard_map/ppermute | solution.py:409
  51.9 2.2 %collective-permute-start.13 = (bf16[128,1664]{1,0:T(8,128)(2,1)}, bf16[128,1664]{1,0:T(8,128)(2,1)}, u32[]{:S(2)}, u32[]{:S(2)}) collective-permute-start(bf16[128,1664]{1,0:T(8,128)(2,1)} %collective-permute-done.6.rest_6_), channel_id=1, source_target_pairs={{0,8},{8,0},{16,24},{24,16},{1,9},{9,1},{17,25},{25,17},{2,10},{10... | collective-permute-start | bytes 1277960 | tf_op jit(solution)/shard_map/ppermute | solution.py:406
  58.3 9.6 %agent_block.1 = (bf16[256,1024]{1,0:T(8,128)(2,1)S(1)}, bf16[512,1024]{1,0:T(8,128)(2,1)}, bf16[256,1024]{1,0:T(8,128)(2,1)S(1)}, bf16[1024,128]{1,0:T(8,128)(2...) custom-call(s32[17]{0:T(128)S(1)} %concatenate.3.place_ref, bf16[256,1024]{1,0:T(8,128)(2,1)S(1)} %bitcast.26, ...), custom_call_target="tpu_custom_call" | custom-call | flops 2147483648 | bytes 4194304 | tf_op jit(solution)/shard_map/agent_block/pallas_call | solution.py:489
  75.3 3.5 %weight_grad.1 = (bf16[128,1152]{1,0:T(8,128)(2,1)S(1)}, bf16[128,1152]{1,0:T(8,128)(2,1)S(1)}, bf16[128,1152]{1,0:T(8,128)(2,1)S(1)}, bf16[128,1152]{1,0:T(8,12...) custom-call(s32[8]{0:T(128)S(1)} %gather_fusion.2, ...), custom_call_target="tpu_custom_call" | custom-call | flops 1073741824 | bytes 4194304 | tf_op jit(solution)/shard_map/weight_grad/pallas_call | solution.py:525
  80.6 4.1 %collective-permute-done.15 = bf16[128,1152]{1,0:T(8,128)(2,1)S(1)} collective-permute-done((bf16[128,1152]{1,0:T(8,128)(2,1)S(1)}, bf16[128,1152]{1,0:T(8,128)(2,1)S(1)}, u32[]{:S(2)}, u32[]{:S(2)}) %collective-permute-start.15) | collective-permute-done | bytes 294944 | tf_op jit(solution)/shard_map/ppermute | solution.py:403
  84.7 1.9 %collective-permute-done.16 = bf16[128,1152]{1,0:T(8,128)(2,1)S(1)} collective-permute-done((bf16[128,1152]{1,0:T(8,128)(2,1)S(1)}, bf16[128,1152]{1,0:T(8,128)(2,1)S(1)}, u32[]{:S(2)}, u32[]{:S(2)}) %collective-permute-start.16) | collective-permute-done | bytes 294944 | tf_op jit(solution)/shard_map/ppermute | solution.py:409
  87.1 2.0 %collective-permute-start.20 = (bf16[128,1152]{1,0:T(8,128)(2,1)S(1)}, bf16[128,1152]{1,0:T(8,128)(2,1)S(1)}, u32[]{:S(2)}, u32[]{:S(2)}) collective-permute-start(bf16[128,1152]{1,0:T(8,128)(2,1)S(1)} %get-tuple-element.41), channel_id=1, source_target_pairs={{0,16},{8,24},{16,0},{24,8},{1,17},{9,25},{17,1},{25,9},{2,18},{10... | collective-permute-start | bytes 884744 | tf_op jit(solution)/shard_map/ppermute | solution.py:409
  89.1 3.9 %collective-permute-done.18 = bf16[128,1152]{1,0:T(8,128)(2,1)S(1)} collective-permute-done((bf16[128,1152]{1,0:T(8,128)(2,1)S(1)}, bf16[128,1152]{1,0:T(8,128)(2,1)S(1)}, u32[]{:S(2)}, u32[]{:S(2)}) %collective-permute-start.18) | collective-permute-done | bytes 294944 | tf_op jit(solution)/shard_map/ppermute | solution.py:409
  93.4 5.8 %collective-permute-done.20 = bf16[128,1152]{1,0:T(8,128)(2,1)S(1)} collective-permute-done((bf16[128,1152]{1,0:T(8,128)(2,1)S(1)}, bf16[128,1152]{1,0:T(8,128)(2,1)S(1)}, u32[]{:S(2)}, u32[]{:S(2)}) %collective-permute-start.20) | collective-permute-done | bytes 294944 | tf_op jit(solution)/shard_map/ppermute | solution.py:409
  100.4 6.8 %all-to-all-start.1 = ((bf16[8,32,1024]{2,1,0:T(8,128)(2,1)}), bf16[8,32,1024]{2,1,0:T(8,128)(2,1)S(1)}, u32[]{:S(2)}, u32[]{:S(2)}) async-start(bf16[8,32,1024]{2,1,0:T(8,128)(2,1)} %bitcast.27), calls=%async_computation.1 | async-start | bytes 1048576 | tf_op jit(solution)/shard_map/all_to_all | solution.py:521
  109.6 4.6 %collective-permute-done.22 = bf16[128,1152]{1,0:T(8,128)(2,1)S(1)} collective-permute-done((bf16[128,1152]{1,0:T(8,128)(2,1)S(1)}, bf16[128,1152]{1,0:T(8,128)(2,1)S(1)}, u32[]{:S(2)}, u32[]{:S(2)}) %collective-permute-start.22) | collective-permute-done | bytes 294944 | tf_op jit(solution)/shard_map/ppermute | solution.py:409
  114.3 13.7 %collective-permute-start.23 = (bf16[128,1152]{1,0:T(8,128)(2,1)S(1)}, bf16[128,1152]{1,0:T(8,128)(2,1)}, u32[]{:S(2)}, u32[]{:S(2)}) collective-permute-start(bf16[128,1152]{1,0:T(8,128)(2,1)S(1)} %add_convert_fusion.own_ref), channel_id=1, source_target_pairs={{0,8},{8,0},{16,24},{24,16},{1,9},{9,1},{17,25},{25,17},{2,10},{10... | collective-permute-start | bytes 884744 | tf_op jit(solution)/shard_map/ppermute | solution.py:406
  128.8 2.8 %copy-done.1 = bf16[1024,3072]{1,0:T(8,128)(2,1)S(1)} copy-done((bf16[1024,3072]{1,0:T(8,128)(2,1)S(1)}, bf16[1024,3072]{1,0:T(8,128)(2,1)}, u32[]{:S(2)}) %copy-start.1) | copy-done | bytes 6291480
  134.2 6.4 %temporal_backward.1 = bf16[256,1024]{1,0:T(8,128)(2,1)} custom-call(bf16[256,1024]{1,0:T(8,128)(2,1)S(1)} %bitcast.25, bf16[256,1024]{1,0:T(8,128)(2,1)S(1)} %bitcast.24, f32[1,1024]{1,0:T(1,128)S(1)} %bitcast.30, bf16[256,3072]{1,0:T(8,128)(2,1)S(1)} %copy-done.8, bf16[8,256,256]{2,1,0:T(8,128)(2,1)S(1)} %copy-done.10, bf16[1024,3072]{1,0:T(8,128)(2,1)S(1)} %copy-done.1, ...), custom_call_target="tpu_custom_call" | custom-call | flops 2147483648 | bytes 8388608 | tf_op jit(solution)/shard_map/temporal_backward/pallas_call | solution.py:562
  140.7 2.5 %finish.1 = (f32[128,3072]{1,0:T(8,128)}, f32[128,1024]{1,0:T(8,128)}) custom-call(s32[1]{0:T(128)} %bitcast.3.core_ref, bf16[128,1152]{1,0:T(8,128)(2,1)S(1)} %add_convert_fusion.own_ref, bf16[128,1152]{1,0:T(8,128)(2,1)} %collective-permute-done.23.other_ref, f32[1,1024]{1,0:T(1,128)S(1)} %get-tuple-element.43.u_ref, f32[1,1024]{1,0:T(1,128)S(1)} %bitcast.33), custom_call_target="tpu_custom_call" | custom-call | flops 1048576 | bytes 2621440 | tf_op jit(solution)/shard_map/finish/pallas_call | solution.py:549
  (125 shorter events, 29.9 us)
Async XLA Ops:
  3.7 12.4 %collective-permute-start = (bf16[128,1664]{1,0:T(8,128)(2,1)S(1)}, bf16[128,1664]{1,0:T(8,128)(2,1)}, u32[]{:S(2)}, u32[]{:S(2)}) collective-permute-start(bf16[128,1664]{1,0:T(8,128)(2,1)S(1)} %pack_block.1.own_ref), channel_id=1, source_target_pairs={{0,2},{1,0},{2,4},{3,1},{4,6},{5,3},{6,7},{7,5},{8,9},{9,11},{10,8... | collective-permute-start | bytes 1277960 | tf_op jit(solution)/shard_map/ppermute | solution.py:403
  16.2 7.6 %collective-permute-start.1 = (bf16[128,1664]{1,0:T(8,128)(2,1)}, bf16[128,1664]{1,0:T(8,128)(2,1)}, u32[]{:S(2)}, u32[]{:S(2)}) collective-permute-start(bf16[128,1664]{1,0:T(8,128)(2,1)} %collective-permute-done.rest_0_), channel_id=1, source_target_pairs={{0,2},{1,0},{2,4},{3,1},{4,6},{5,3},{6,7},{7,5},{8,9},{9,11},{10,8... | collective-permute-start | bytes 1277960 | tf_op jit(solution)/shard_map/ppermute | solution.py:403
  16.4 16.0 %collective-permute-start.4 = (bf16[128,1664]{1,0:T(8,128)(2,1)}, bf16[128,1664]{1,0:T(8,128)(2,1)}, u32[]{:S(2)}, u32[]{:S(2)}) collective-permute-start(bf16[128,1664]{1,0:T(8,128)(2,1)} %collective-permute-done.rest_0_), channel_id=1, source_target_pairs={{0,16},{8,24},{16,0},{24,8},{1,17},{9,25},{17,1},{25,9},{2,18},{10... | collective-permute-start | bytes 1277960 | tf_op jit(solution)/shard_map/ppermute | solution.py:409
  23.8 8.9 %collective-permute-start.2 = (bf16[128,1664]{1,0:T(8,128)(2,1)}, bf16[128,1664]{1,0:T(8,128)(2,1)}, u32[]{:S(2)}, u32[]{:S(2)}) collective-permute-start(bf16[128,1664]{1,0:T(8,128)(2,1)} %collective-permute-done.1.rest_1_), channel_id=1, source_target_pairs={{0,2},{1,0},{2,4},{3,1},{4,6},{5,3},{6,7},{7,5},{8,9},{9,11},{10,8... | collective-permute-start | bytes 1277960 | tf_op jit(solution)/shard_map/ppermute | solution.py:403
  23.9 33.3 %all-to-all-start = ((bf16[8,32,1024]{2,1,0:T(8,128)(2,1)}), bf16[8,32,1024]{2,1,0:T(8,128)(2,1)S(1)}, u32[]{:S(2)}, u32[]{:S(2)}) async-start(bf16[8,32,1024]{2,1,0:T(8,128)(2,1)} %bitcast.28), calls=%async_computation | async-start | bytes 1048576 | tf_op jit(solution)/shard_map/all_to_all | solution.py:460
  29.7 5.7 %collective-permute-start.7 = (bf16[128,1664]{1,0:T(8,128)(2,1)}, bf16[128,1664]{1,0:T(8,128)(2,1)}, u32[]{:S(2)}, u32[]{:S(2)}) collective-permute-start(bf16[128,1664]{1,0:T(8,128)(2,1)} %collective-permute-done.rest_0_), channel_id=1, source_target_pairs={{0,8},{8,0},{16,24},{24,16},{1,9},{9,1},{17,25},{25,17},{2,10},{10... | collective-permute-start | bytes 1277960 | tf_op jit(solution)/shard_map/ppermute | solution.py:406
  32.4 11.8 %collective-permute-start.11 = (bf16[128,1664]{1,0:T(8,128)(2,1)}, bf16[128,1664]{1,0:T(8,128)(2,1)}, u32[]{:S(2)}, u32[]{:S(2)}) collective-permute-start(bf16[128,1664]{1,0:T(8,128)(2,1)} %collective-permute-done.4.rest_4_), channel_id=1, source_target_pairs={{0,8},{8,0},{16,24},{24,16},{1,9},{9,1},{17,25},{25,17},{2,10},{10... | collective-permute-start | bytes 1277960 | tf_op jit(solution)/shard_map/ppermute | solution.py:406
  32.5 11.8 %collective-permute-start.5 = (bf16[128,1664]{1,0:T(8,128)(2,1)}, bf16[128,1664]{1,0:T(8,128)(2,1)}, u32[]{:S(2)}, u32[]{:S(2)}) collective-permute-start(bf16[128,1664]{1,0:T(8,128)(2,1)} %collective-permute-done.1.rest_1_), channel_id=1, source_target_pairs={{0,16},{8,24},{16,0},{24,8},{1,17},{9,25},{17,1},{25,9},{2,18},{10... | collective-permute-start | bytes 1277960 | tf_op jit(solution)/shard_map/ppermute | solution.py:409
  32.7 19.2 %collective-permute-start.6 = (bf16[128,1664]{1,0:T(8,128)(2,1)}, bf16[128,1664]{1,0:T(8,128)(2,1)}, u32[]{:S(2)}, u32[]{:S(2)}) collective-permute-start(bf16[128,1664]{1,0:T(8,128)(2,1)} %collective-permute-done.2.rest_2_), channel_id=1, source_target_pairs={{0,16},{8,24},{16,0},{24,8},{1,17},{9,25},{17,1},{25,9},{2,18},{10... | collective-permute-start | bytes 1277960 | tf_op jit(solution)/shard_map/ppermute | solution.py:409
  34.2 20.0 %collective-permute-start.3 = (bf16[128,1664]{1,0:T(8,128)(2,1)}, bf16[128,1664]{1,0:T(8,128)(2,1)}, u32[]{:S(2)}, u32[]{:S(2)}) collective-permute-start(bf16[128,1664]{1,0:T(8,128)(2,1)} %collective-permute-done.2.rest_2_), channel_id=1, source_target_pairs={{0,2},{1,0},{2,4},{3,1},{4,6},{5,3},{6,7},{7,5},{8,9},{9,11},{10,8... | collective-permute-start | bytes 1277960 | tf_op jit(solution)/shard_map/ppermute | solution.py:403
  35.4 21.8 %collective-permute-start.8 = (bf16[128,1664]{1,0:T(8,128)(2,1)}, bf16[128,1664]{1,0:T(8,128)(2,1)}, u32[]{:S(2)}, u32[]{:S(2)}) collective-permute-start(bf16[128,1664]{1,0:T(8,128)(2,1)} %collective-permute-done.1.rest_1_), channel_id=1, source_target_pairs={{0,8},{8,0},{16,24},{24,16},{1,9},{9,1},{17,25},{25,17},{2,10},{10... | collective-permute-start | bytes 1277960 | tf_op jit(solution)/shard_map/ppermute | solution.py:406
  44.2 13.1 %collective-permute-start.9 = (bf16[128,1664]{1,0:T(8,128)(2,1)}, bf16[128,1664]{1,0:T(8,128)(2,1)}, u32[]{:S(2)}, u32[]{:S(2)}) collective-permute-start(bf16[128,1664]{1,0:T(8,128)(2,1)} %collective-permute-done.2.rest_2_), channel_id=1, source_target_pairs={{0,8},{8,0},{16,24},{24,16},{1,9},{9,1},{17,25},{25,17},{2,10},{10... | collective-permute-start | bytes 1277960 | tf_op jit(solution)/shard_map/ppermute | solution.py:406
  44.2 13.0 %collective-permute-start.12 = (bf16[128,1664]{1,0:T(8,128)(2,1)}, bf16[128,1664]{1,0:T(8,128)(2,1)}, u32[]{:S(2)}, u32[]{:S(2)}) collective-permute-start(bf16[128,1664]{1,0:T(8,128)(2,1)} %collective-permute-done.5.rest_5_), channel_id=1, source_target_pairs={{0,8},{8,0},{16,24},{24,16},{1,9},{9,1},{17,25},{25,17},{2,10},{10... | collective-permute-start | bytes 1277960 | tf_op jit(solution)/shard_map/ppermute | solution.py:406
  51.9 5.4 %collective-permute-start.13 = (bf16[128,1664]{1,0:T(8,128)(2,1)}, bf16[128,1664]{1,0:T(8,128)(2,1)}, u32[]{:S(2)}, u32[]{:S(2)}) collective-permute-start(bf16[128,1664]{1,0:T(8,128)(2,1)} %collective-permute-done.6.rest_6_), channel_id=1, source_target_pairs={{0,8},{8,0},{16,24},{24,16},{1,9},{9,1},{17,25},{25,17},{2,10},{10... | collective-permute-start | bytes 1277960 | tf_op jit(solution)/shard_map/ppermute | solution.py:406
  78.8 5.9 %collective-permute-start.15 = (bf16[128,1152]{1,0:T(8,128)(2,1)S(1)}, bf16[128,1152]{1,0:T(8,128)(2,1)S(1)}, u32[]{:S(2)}, u32[]{:S(2)}) collective-permute-start(bf16[128,1152]{1,0:T(8,128)(2,1)S(1)} %get-tuple-element.35), channel_id=1, source_target_pairs={{0,2},{1,0},{2,4},{3,1},{4,6},{5,3},{6,7},{7,5},{8,9},{9,11},{10,8... | collective-permute-start | bytes 884744 | tf_op jit(solution)/shard_map/ppermute | solution.py:403
  79.1 7.5 %collective-permute-start.16 = (bf16[128,1152]{1,0:T(8,128)(2,1)S(1)}, bf16[128,1152]{1,0:T(8,128)(2,1)S(1)}, u32[]{:S(2)}, u32[]{:S(2)}) collective-permute-start(bf16[128,1152]{1,0:T(8,128)(2,1)S(1)} %get-tuple-element.37), channel_id=1, source_target_pairs={{0,16},{8,24},{16,0},{24,8},{1,17},{9,25},{17,1},{25,9},{2,18},{10... | collective-permute-start | bytes 884744 | tf_op jit(solution)/shard_map/ppermute | solution.py:409
  80.3 12.6 %collective-permute-start.18 = (bf16[128,1152]{1,0:T(8,128)(2,1)S(1)}, bf16[128,1152]{1,0:T(8,128)(2,1)S(1)}, u32[]{:S(2)}, u32[]{:S(2)}) collective-permute-start(bf16[128,1152]{1,0:T(8,128)(2,1)S(1)} %get-tuple-element.39), channel_id=1, source_target_pairs={{0,16},{8,24},{16,0},{24,8},{1,17},{9,25},{17,1},{25,9},{2,18},{10... | collective-permute-start | bytes 884744 | tf_op jit(solution)/shard_map/ppermute | solution.py:409
  86.8 6.2 %collective-permute-start.17 = (bf16[128,1152]{1,0:T(8,128)(2,1)S(1)}, bf16[128,1152]{1,0:T(8,128)(2,1)S(1)}, u32[]{:S(2)}, u32[]{:S(2)}) collective-permute-start(bf16[128,1152]{1,0:T(8,128)(2,1)S(1)} %add_convert_fusion.4), channel_id=1, source_target_pairs={{0,2},{1,0},{2,4},{3,1},{4,6},{5,3},{6,7},{7,5},{8,9},{9,11},{10,8... | collective-permute-start | bytes 884744 | tf_op jit(solution)/shard_map/ppermute | solution.py:403
  87.1 12.2 %collective-permute-start.20 = (bf16[128,1152]{1,0:T(8,128)(2,1)S(1)}, bf16[128,1152]{1,0:T(8,128)(2,1)S(1)}, u32[]{:S(2)}, u32[]{:S(2)}) collective-permute-start(bf16[128,1152]{1,0:T(8,128)(2,1)S(1)} %get-tuple-element.41), channel_id=1, source_target_pairs={{0,16},{8,24},{16,0},{24,8},{1,17},{9,25},{17,1},{25,9},{2,18},{10... | collective-permute-start | bytes 884744 | tf_op jit(solution)/shard_map/ppermute | solution.py:409
  93.1 6.4 %collective-permute-start.19 = (bf16[128,1152]{1,0:T(8,128)(2,1)S(1)}, bf16[128,1152]{1,0:T(8,128)(2,1)S(1)}, u32[]{:S(2)}, u32[]{:S(2)}) collective-permute-start(bf16[128,1152]{1,0:T(8,128)(2,1)S(1)} %add_convert_fusion.3), channel_id=1, source_target_pairs={{0,2},{1,0},{2,4},{3,1},{4,6},{5,3},{6,7},{7,5},{8,9},{9,11},{10,8... | collective-permute-start | bytes 884744 | tf_op jit(solution)/shard_map/ppermute | solution.py:403
  100.3 6.8 %collective-permute-start.21 = (bf16[128,1152]{1,0:T(8,128)(2,1)}, bf16[128,1152]{1,0:T(8,128)(2,1)}, u32[]{:S(2)}, u32[]{:S(2)}) collective-permute-start(bf16[128,1152]{1,0:T(8,128)(2,1)} %add_convert_fusion.2), channel_id=1, source_target_pairs={{0,2},{1,0},{2,4},{3,1},{4,6},{5,3},{6,7},{7,5},{8,9},{9,11},{10,8... | collective-permute-start | bytes 884744 | tf_op jit(solution)/shard_map/ppermute | solution.py:403
  100.4 28.4 %all-to-all-start.1 = ((bf16[8,32,1024]{2,1,0:T(8,128)(2,1)}), bf16[8,32,1024]{2,1,0:T(8,128)(2,1)S(1)}, u32[]{:S(2)}, u32[]{:S(2)}) async-start(bf16[8,32,1024]{2,1,0:T(8,128)(2,1)} %bitcast.27), calls=%async_computation.1 | async-start | bytes 1048576 | tf_op jit(solution)/shard_map/all_to_all | solution.py:521
  108.2 6.0 %collective-permute-start.22 = (bf16[128,1152]{1,0:T(8,128)(2,1)S(1)}, bf16[128,1152]{1,0:T(8,128)(2,1)S(1)}, u32[]{:S(2)}, u32[]{:S(2)}) collective-permute-start(bf16[128,1152]{1,0:T(8,128)(2,1)S(1)} %add_convert_fusion.1), channel_id=1, source_target_pairs={{0,16},{8,24},{16,0},{24,8},{1,17},{9,25},{17,1},{25,9},{2,18},{10... | collective-permute-start | bytes 884744 | tf_op jit(solution)/shard_map/ppermute | solution.py:409
  114.3 26.3 %collective-permute-start.23 = (bf16[128,1152]{1,0:T(8,128)(2,1)S(1)}, bf16[128,1152]{1,0:T(8,128)(2,1)}, u32[]{:S(2)}, u32[]{:S(2)}) collective-permute-start(bf16[128,1152]{1,0:T(8,128)(2,1)S(1)} %add_convert_fusion.own_ref), channel_id=1, source_target_pairs={{0,8},{8,0},{16,24},{24,16},{1,9},{9,1},{17,25},{25,17},{2,10},{10... | collective-permute-start | bytes 884744 | tf_op jit(solution)/shard_map/ppermute | solution.py:406
  (34 other events, 492.8 us)

commit v3 on v2

--- a/solution.py
+++ b/solution.py
@@ -13,6 +13,7 @@
 F32 = jnp.float32
 BF16 = jnp.bfloat16
 TILE = 256
+VMEM_BYTES = 60 * 1024 * 1024
 
 
 def dot_nn(a, b):
@@ -43,28 +44,53 @@
     return [pl.ds(at, size) for at in range(0, total, size)]
 
 
+def core_of(env_ref):
+    return env_ref[0] % 2
+
+
+def place_of(env_ref, tm_ref, count, hop):
+    at = tm_ref[0]
+    way = 1 - 2 * ((env_ref[0] + env_ref[0] // 2) % 2)
+    spot = jnp.where(at % 2 == 0, at // 2, count - 1 - at // 2)
+    spot = (spot + way * hop + count) % count
+    return jnp.where(spot < count // 2, 2 * spot, 2 * (count - 1 - spot) + 1)
+
+
+def copies_of(moves, sems):
+    return [
+        pltpu.make_async_copy(source, target, sems.at[at])
+        for at, (source, target) in enumerate(moves)
+    ]
+
+
+def started(moves, sems):
+    copies = copies_of(moves, sems)
+    for copy in copies:
+        copy.start()
+    return copies
+
+
 def temporal_forward(
-    done_ref, rows_ref, gain_ref, w_qkv_hbm, w_out_hbm, h1_ref, qkv_ref, probs_ref,
-    w_qkv, w_out, mixed, sems,
+    done_ref, rows_ref, gain_ref, w_qkv_hbm, w_out_hbm, h1_ref, qkv_hbm, probs_hbm,
+    w_qkv, w_out, qkv_ref, probs_ref, mixed, sems, out_sems,
 ):
     length, width = rows_ref.shape
     size = width // HEADS
-    copies = []
-    for part in range(3):
-        span = pl.ds(part * width, width)
-        copies.append(
-            pltpu.make_async_copy(w_qkv_hbm.at[:, span], w_qkv.at[:, span], sems.at[part])
-        )
-    copies.append(pltpu.make_async_copy(w_out_hbm, w_out, sems.at[3]))
-    for copy in copies:
-        copy.start()
+    chunks = spans(3 * width, width // 2)
+    moves = [(w_qkv_hbm.at[:, span], w_qkv.at[:, span]) for span in chunks]
+    copies = started(moves + [(w_out_hbm, w_out)], sems)
     rows = rows_ref[...].astype(F32)
     normed = (rows * inv_rms(rows) * gain_ref[...]).astype(BF16)
-    for part in range(3):
+    outs = copies_of(
+        [(qkv_ref, qkv_hbm)] + [(probs_ref.at[head], probs_hbm.at[head]) for head in range(HEADS)],
+        out_sems,
+    )
+    for part, chunk in enumerate(chunks):
         copies[part].wait()
-        for at in range(part * width, (part + 1) * width, TILE):
+        for at in range(chunk.start, chunk.start + chunk.size, TILE):
             span = pl.ds(at, TILE)
             qkv_ref[:, span] = dot_nn(normed, w_qkv[:, span]).astype(BF16)
+    outs[0].start()
     done = done_ref[0]
     query_at = lax.broadcasted_iota(jnp.int32, (length, length), 0)
     key_at = lax.broadcasted_iota(jnp.int32, (length, length), 1)
@@ -79,23 +105,57 @@
         probs = weights * (1.0 / jnp.sum(weights, axis=-1, keepdims=True))
         probs = probs.astype(BF16)
         probs_ref[head] = probs
+        outs[1 + head].start()
         mixed[:, pl.ds(head * size, size)] = dot_nn(probs, values).astype(BF16)
-    copies[3].wait()
+    copies[-1].wait()
     for span in spans(width, TILE):
         added = dot_nn(mixed[...], w_out[:, span])
         h1_ref[:, span] = (rows_ref[:, span].astype(F32) + added).astype(BF16)
+    for out in outs:
+        out.wait()
 
 
 def temporal_backward(
-    grad_ref, rows_ref, gain_ref, qkv_ref, probs_ref, w_qkv, w_out, out_ref,
-    grad_mixed, grad_qkv, grad_normed,
+    gain_ref, grad_ref, rows_hbm, qkv_hbm, probs_hbm, w_qkv_hbm, w_out_hbm, out_ref,
+    rows_ref, qkv_ref, probs_ref, w_qkv, w_out, grad_mixed, grad_qkv, grad_normed, sems,
 ):
     length, width = rows_ref.shape
     size = width // HEADS
     scale = 1.0 / math.sqrt(size)
-    grad = grad_ref[...]
-    for span in spans(width, TILE):
-        grad_mixed[:, span] = dot_nt(grad, w_out[span, :]).astype(BF16)
+    tiles = width // TILE
+
+    def rows_of(step):
+        return pl.ds(pl.multiple_of(step * TILE, TILE), TILE)
+
+    def w_out_copy(step):
+        return pltpu.make_async_copy(
+            w_out_hbm.at[rows_of(step), :], w_out.at[rows_of(step), :], sems.at[step]
+        )
+
+    def w_qkv_copy(step):
+        return pltpu.make_async_copy(
+            w_qkv_hbm.at[rows_of(step), :], w_qkv.at[rows_of(step), :], sems.at[tiles + step]
+        )
+
+    qkv_copy = pltpu.make_async_copy(qkv_hbm, qkv_ref, sems.at[2 * tiles])
+    probs_copy = pltpu.make_async_copy(probs_hbm, probs_ref, sems.at[2 * tiles + 1])
+    rows_copy = pltpu.make_async_copy(rows_hbm, rows_ref, sems.at[2 * tiles + 2])
+    for step in range(tiles):
+        w_out_copy(step).start()
+    qkv_copy.start()
+    probs_copy.start()
+
+    @pl.loop(0, tiles)
+    def _(step):
+        w_out_copy(step).wait()
+        grad_mixed[:, rows_of(step)] = dot_nt(grad_ref[...], w_out[rows_of(step), :]).astype(BF16)
+
+    for step in range(tiles):
+        w_qkv_copy(step).start()
+    rows_copy.start()
+    qkv_copy.wait()
+    probs_copy.wait()
+
     for head in range(HEADS):
         query_span = pl.ds(head * size, size)
         key_span = pl.ds(width + head * size, size)
@@ -109,15 +169,20 @@
         grad_scores = (wide * (grad_probs - inner) * scale).astype(BF16)
         grad_qkv[:, query_span] = dot_nn(grad_scores, qkv_ref[:, key_span]).astype(BF16)
         grad_qkv[:, key_span] = dot_tn(grad_scores, qkv_ref[:, query_span]).astype(BF16)
-    for span in spans(width, TILE):
-        grad_normed[:, span] = dot_nt(grad_qkv[...], w_qkv[span, :])
+
+    @pl.loop(0, tiles)
+    def _(step):
+        w_qkv_copy(step).wait()
+        grad_normed[:, rows_of(step)] = dot_nt(grad_qkv[...], w_qkv[rows_of(step), :])
+
+    rows_copy.wait()
     rows = rows_ref[...].astype(F32)
     pulled = norm_pull(rows, gain_ref[...], grad_normed[...])
     out_ref[...] = (grad_ref[...].astype(F32) + pulled).astype(BF16)
 
 
 def agent_kernel(
-    blocks, group_steps, place_ref, rows_ref, alive_ref, target_ref, gain_ref, value_ref,
+    blocks, group_steps, env_ref, tm_ref, rows_ref, alive_ref, target_ref, gain_ref, value_ref,
     shard_ref, own_ref, *rest,
 ):
     moved = rest[: 2 * blocks]
@@ -137,15 +202,21 @@
         w_all.at[:, pl.ds(width, middle)],
         w_all.at[:, pl.ds(block_width + width, middle)],
     ]
-    core, other = place_ref[2 * blocks + 1], place_ref[2 * blocks + 2]
-
-    def row_span(at):
-        return pl.ds(pl.multiple_of(place_ref[at] * depth, depth), depth)
+    core = core_of(env_ref)
+    other = 1 - core
+    near = blocks // 2
+    far = blocks - near
+    own_hops = [-hop for hop in range(1, far + 1)] + list(range(1, near + 1))
+    hops = own_hops + [-hop for hop in own_hops]
+
+    def row_span(hop):
+        place = place_of(env_ref, tm_ref, blocks + 1, hop)
+        return pl.ds(pl.multiple_of(place * depth, depth), depth)
 
     def column_span(start, length):
         return pl.ds(pl.multiple_of(start, 128), length)
 
-    own_rows = row_span(2 * blocks)
+    own_rows = row_span(0)
     other_at = other * block_width
     moves = [
         (own_ref, w_all.at[own_rows, column_span(core * block_width, block_width)]),
@@ -165,14 +236,9 @@
     for at in range(2 * blocks):
         half = core if at < blocks else other
         moves.append(
-            (moved[at], w_all.at[row_span(at), column_span(half * block_width, block_width)])
+            (moved[at], w_all.at[row_span(hops[at]), column_span(half * block_width, block_width)])
         )
-    copies = [
-        pltpu.make_async_copy(source, target, sems.at[at])
-        for at, (source, target) in enumerate(moves)
-    ]
-    for copy in copies:
-        copy.start()
+    copies = started(moves, sems)
 
     def row_spans(group):
         if groups == 1:
@@ -295,7 +361,7 @@
     extra_ref[...] = jnp.transpose(extra).astype(BF16)
 
 
-def weight_grad_kernel(place_ref, pack_ref, keep_ref, moved_ref, extra_ref, *rest):
+def weight_grad_kernel(hops, env_ref, tm_ref, pack_ref, keep_ref, moved_ref, extra_ref, *rest):
     outs, (total, sems) = rest[:-2], rest[-2:]
     half, width = keep_ref.shape
     depth = width // len(outs)
@@ -309,11 +375,16 @@
             ).astype(BF16)
     copies = [
         pltpu.make_async_copy(
-            total.at[pl.ds(pl.multiple_of(place_ref[at] * depth, depth), depth), :],
+            total.at[
+                pl.ds(
+                    pl.multiple_of(place_of(env_ref, tm_ref, len(outs), hop) * depth, depth), depth
+                ),
+                :,
+            ],
             out,
             sems.at[at],
         )
-        for at, out in enumerate(outs)
+        for at, (hop, out) in enumerate(zip(hops, outs))
     ]
     for copy in copies:
         copy.start()
@@ -321,7 +392,7 @@
         copy.wait()
 
 
-def pack_block_kernel(core_ref, qk_ref, v_ref, w_out_ref, value_ref, out_ref):
+def pack_block_kernel(env_ref, qk_ref, v_ref, w_out_ref, value_ref, out_ref):
     width, middle = qk_ref.shape[1], v_ref.shape[1]
     out_ref[:, pl.ds(0, width)] = qk_ref[...]
     out_ref[:, pl.ds(width, middle)] = v_ref[...]
@@ -332,11 +403,11 @@
     out_ref[:, pl.ds(width + middle, 128)] = parts.astype(BF16)
 
 
-def finish_kernel(core_ref, own_ref, other_ref, u_ref, value_ref, qkv_ref, out_ref):
+def finish_kernel(env_ref, own_ref, other_ref, u_ref, value_ref, qkv_ref, out_ref):
     width = u_ref.shape[1]
     size = width // HEADS
     own, other = own_ref[:, pl.ds(0, width)], other_ref[:, pl.ds(0, width)]
-    core = core_ref[0]
+    core = core_of(env_ref)
     qkv_ref[:, pl.ds(pl.multiple_of(core * width, width), width)] = own.astype(F32)
     qkv_ref[:, pl.ds(pl.multiple_of((1 - core) * width, width), width)] = other.astype(F32)
     extra = own_ref[:, pl.ds(width, 128)].astype(F32) + other_ref[:, pl.ds(width, 128)].astype(F32)
@@ -363,8 +434,8 @@
     return pl.BlockSpec(memory_space=pltpu.SMEM)
 
 
-def params(mebibytes):
-    return pltpu.CompilerParams(vmem_limit_bytes=mebibytes * 1024 * 1024)
+def params():
+    return pltpu.CompilerParams(vmem_limit_bytes=VMEM_BYTES)
 
 
 def cost(flops, moved):
@@ -382,17 +453,12 @@
     length, width = hidden.shape[2:]
     agents, local_steps = alive.shape[1:]
     depth = w_qkv_a.shape[0]
-    size = width // HEADS
-    env_at = lax.axis_index("env")
-    tm_at = lax.axis_index("tm")
-    core = env_at % 2
+    env_index = lax.axis_index("env").astype(jnp.int32)[None]
+    tm_index = lax.axis_index("tm").astype(jnp.int32)[None]
     order = ring_order(tm_count)
     spot = [order.index(at) for at in range(tm_count)]
-    order_array = jnp.array(order, jnp.int32)
-    my_spot = jnp.array(spot, jnp.int32)[tm_at]
 
     ways = [1 if at in (0, 3) else -1 for at in range(env_count)]
-    way = jnp.array(ways, jnp.int32)[env_at]
 
     def ring(block):
         pairs = [
@@ -411,10 +477,6 @@
     far = tm_count // 2
     near = tm_count - 1 - far
 
-    def places(hops):
-        return order_array[(my_spot + way * jnp.array(hops, jnp.int32)) % tm_count]
-
-    core_index = core[None].astype(jnp.int32)
     block_width = width + width // 2 + 128
     own_block = pl.pallas_call(
         pack_block_kernel,
@@ -424,16 +486,16 @@
             num_scalar_prefetch=1,
             grid=(1,),
             in_specs=[
-                pl.BlockSpec((depth, width), lambda at, core: (0, core[0])),
-                pl.BlockSpec((depth, width // 2), lambda at, core: (0, 4 + core[0])),
-                pl.BlockSpec((depth, width), lambda at, core: (0, 0)),
-                pl.BlockSpec((1, width), lambda at, core: (0, 0)),
+                pl.BlockSpec((depth, width), lambda at, env: (0, core_of(env))),
+                pl.BlockSpec((depth, width // 2), lambda at, env: (0, 4 + core_of(env))),
+                pl.BlockSpec((depth, width), lambda at, env: (0, 0)),
+                pl.BlockSpec((1, width), lambda at, env: (0, 0)),
             ],
-            out_specs=pl.BlockSpec((depth, block_width), lambda at, core: (0, 0)),
+            out_specs=pl.BlockSpec((depth, block_width), lambda at, env: (0, 0)),
         ),
-        compiler_params=params(16),
+        compiler_params=params(),
         cost_estimate=cost(2 * depth * width, 8 * depth * width),
-    )(core_index, w_qkv_a, w_qkv_a, w_out_a, w_value[None])
+    )(env_index, w_qkv_a, w_qkv_a, w_out_a, w_value[None])
     first_block = ring(own_block)
 
     rows = hidden[0, 0]
@@ -445,15 +507,18 @@
             jax.ShapeDtypeStruct((length, 3 * width), BF16),
             jax.ShapeDtypeStruct((HEADS, length, length), BF16),
         ),
-        in_specs=[smem_spec(), vmem_spec(), vmem_spec(), hbm_spec(), hbm_spec()],
-        out_specs=[vmem_spec()] * 3,
+        in_specs=[smem_spec()] + [vmem_spec()] * 2 + [hbm_spec()] * 2,
+        out_specs=[vmem_spec()] + [hbm_spec()] * 2,
         scratch_shapes=[
             pltpu.VMEM((width, 3 * width), BF16),
             pltpu.VMEM((width, width), BF16),
+            pltpu.VMEM((length, 3 * width), BF16),
+            pltpu.VMEM((HEADS, length, length), BF16),
             pltpu.VMEM((length, width), BF16),
-            pltpu.SemaphoreType.DMA((4,)),
+            pltpu.SemaphoreType.DMA((7,)),
+            pltpu.SemaphoreType.DMA((HEADS + 1,)),
         ],
-        compiler_params=params(24),
+        compiler_params=params(),
         cost_estimate=cost(8 * length * width * width, 8 * width * width),
     )(done_step[0], rows, gain_t[None], w_qkv_t, w_out_t)
     h1, first_block = lax.optimization_barrier((h1, first_block))
@@ -461,21 +526,16 @@
 
     ringed, crossed = [first_block], []
     for hop in range(1, far):
+        if len(crossed) > 0:
+            ringed[-1], crossed[-1] = lax.optimization_barrier((ringed[-1], crossed[-1]))
         if hop <= near:
             crossed.append(swap_chip(ringed[-1]))
         ringed.append(ring(ringed[-1]))
     crossed += [swap_chip(block) for block in ringed[len(crossed) : near]]
     own_blocks = ringed + crossed
+    gated = far + near // 2
+    lifted, own_blocks[gated] = lax.optimization_barrier((lifted, own_blocks[gated]))
     other_blocks = [swap_core(block) for block in own_blocks]
-    ahead_hops = list(range(1, far + 1))
-    behind_hops = list(range(1, near + 1))
-    block_places = jnp.concatenate(
-        [
-            places([-hop for hop in ahead_hops] + behind_hops),
-            places(ahead_hops + [-hop for hop in behind_hops]),
-            jnp.stack([tm_at, core, 1 - core]).astype(jnp.int32),
-        ]
-    )
 
     group_steps = 16 if local_steps % 16 == 0 else local_steps
     groups = local_steps // group_steps
@@ -497,7 +557,7 @@
             jax.ShapeDtypeStruct((1, width), F32),
             jax.ShapeDtypeStruct((groups, 8, group_rows), F32),
         ),
-        in_specs=[smem_spec()] + [vmem_spec()] * (2 * tm_count + 5),
+        in_specs=[smem_spec()] * 2 + [vmem_spec()] * 5 + [hbm_spec()] * (2 * tm_count),
         out_specs=[vmem_spec()] * 6,
         scratch_shapes=[
             pltpu.VMEM((width, 2 * block_width), BF16),
@@ -509,10 +569,10 @@
             pltpu.VMEM((total_rows, width), F32),
             pltpu.SemaphoreType.DMA((2 * tm_count + 2,)),
         ],
-        compiler_params=params(36),
+        compiler_params=params(),
         cost_estimate=cost(8 * total_rows * width * width, 4 * width * width),
     )(
-        block_places, lifted, grouped(alive[0].astype(F32)), grouped(targets[0]), gain_a[None],
+        env_index, tm_index, lifted, grouped(alive[0].astype(F32)), grouped(targets[0]), gain_a[None],
         w_value[None], w_qkv_a, own_block, *own_blocks, *other_blocks,
     )
     values = predicted[:, 0].reshape(groups, agents, group_steps)
@@ -521,30 +581,60 @@
     returned = lax.all_to_all(grad_lifted, "tm", split_axis=0, concat_axis=0, tiled=True)
 
     moved = swap_core(pack)
-    hops = [0] + ahead_hops + [-hop for hop in behind_hops]
+    hops = list(range(far + 1)) + [-hop for hop in range(1, near + 1)]
     terms = pl.pallas_call(
-        weight_grad_kernel,
+        functools.partial(weight_grad_kernel, hops),
         name="weight_grad",
         out_shape=[jax.ShapeDtypeStruct((depth, width + 128), BF16)] * tm_count,
-        in_specs=[smem_spec()] + [vmem_spec()] * 4,
-        out_specs=[any_spec()] * tm_count,
+        in_specs=[smem_spec()] * 2 + [vmem_spec()] * 4,
+        out_specs=[hbm_spec()] * tm_count,
         scratch_shapes=[
             pltpu.VMEM((width, width + 128), BF16),
             pltpu.SemaphoreType.DMA((tm_count,)),
         ],
-        compiler_params=params(20),
+        compiler_params=params(),
         cost_estimate=cost(4 * total_rows * width * width, 4 * width * width),
-    )(places(hops), pack, keep, moved, extra)
+    )(env_index, tm_index, pack, keep, moved, extra)
+    def temporal_gradient(returned):
+        return pl.pallas_call(
+            temporal_backward,
+            name="temporal_backward",
+            out_shape=jax.ShapeDtypeStruct((length, width), BF16),
+            in_specs=[vmem_spec()] * 2 + [hbm_spec()] * 5,
+            out_specs=vmem_spec(),
+            scratch_shapes=[
+                pltpu.VMEM((length, width), BF16),
+                pltpu.VMEM((length, 3 * width), BF16),
+                pltpu.VMEM((HEADS, length, length), BF16),
+                pltpu.VMEM((width, 3 * width), BF16),
+                pltpu.VMEM((width, width), BF16),
+                pltpu.VMEM((length, width), BF16),
+                pltpu.VMEM((length, 3 * width), BF16),
+                pltpu.VMEM((length, width), F32),
+                pltpu.SemaphoreType.DMA((3 + 2 * (width // TILE),)),
+            ],
+            compiler_params=params(),
+            cost_estimate=cost(8 * length * width * width, 8 * width * width),
+        )(gain_t[None], returned, rows, qkv, probs, w_qkv_t, w_out_t)
+
     term = dict(zip(hops, terms))
-    chip_terms = {hop: swap_chip(term[-hop]) for hop in reversed(behind_hops)}
     travelling = ring(term[far])
+    chip_term = swap_chip(term[-near])
     for hop in range(far - 1, 0, -1):
-        travelling = travelling.astype(F32) + term[hop].astype(F32)
-        if hop in chip_terms:
-            travelling = travelling + chip_terms[hop].astype(F32)
-        travelling = ring(travelling.astype(BF16))
+        if hop > 1:
+            following, chip_term = lax.optimization_barrier((term[1 - hop], chip_term))
+            next_chip_term = swap_chip(following)
+        if hop == 2:
+            travelling, returned = lax.optimization_barrier((travelling, returned))
+        if hop == 1:
+            input_grad = temporal_gradient(returned)
+            travelling, input_grad = lax.optimization_barrier((travelling, input_grad))
+        total = travelling.astype(F32) + term[hop].astype(F32) + chip_term.astype(F32)
+        travelling = ring(total.astype(BF16))
+        chip_term = next_chip_term
     reduced = (travelling.astype(F32) + term[0].astype(F32)).astype(BF16)
     reduced = (reduced.astype(F32) + swap_chip(reduced).astype(F32)).astype(BF16)
+    reduced, values = lax.optimization_barrier((reduced, values))
     other = swap_core(reduced)
     qkv_grad, out_grad = pl.pallas_call(
         finish_kernel,
@@ -555,24 +645,9 @@
         ),
         in_specs=[smem_spec()] + [vmem_spec()] * 4,
         out_specs=[vmem_spec()] * 2,
-        compiler_params=params(16),
+        compiler_params=params(),
         cost_estimate=cost(8 * depth * width, 20 * depth * width),
-    )(core_index, reduced, other, u, w_value[None])
-
-    input_grad = pl.pallas_call(
-        temporal_backward,
-        name="temporal_backward",
-        out_shape=jax.ShapeDtypeStruct((length, width), BF16),
-        in_specs=[vmem_spec()] * 7,
-        out_specs=vmem_spec(),
-        scratch_shapes=[
-            pltpu.VMEM((length, width), BF16),
-            pltpu.VMEM((length, 3 * width), BF16),
-            pltpu.VMEM((length, width), F32),
-        ],
-        compiler_params=params(30),
-        cost_estimate=cost(8 * length * width * width, 8 * width * width),
-    )(returned, rows, gain_t[None], qkv, probs, w_qkv_t, w_out_t)
+    )(env_index, reduced, other, u, w_value[None])
     return values, input_grad[None, None], qkv_grad, out_grad
 
 

time: 144 us -> 128 us (0.89)
  the two profiles are of different devices: /device:TPU:23 before, /device:TPU:0 now
where the time goes in v3:
time: 128 us; the launch traced here: 127 us
  waiting for transfers between devices  44.7 us (35%)
  Pallas kernels  38.4 us (30%)
  starting transfers between devices  36.6 us (29%)
  local copies, waits for them, and re-layouts  4.64 us (4%)
  between operations  1.56 us (1%)
  other arithmetic  1.44 us (1%)
    ppermute x7, waiting for transfers between devices, swap_chip(): return lax.ppermute(block, 'env', [(at, at ^ 2) for at in range(env_count)])  24.4 us
    ppermute x8, starting transfers between devices, ring(): return lax.ppermute(block, ('env', 'tm'), pairs)  17.5 us
    pallas_call x1, Pallas kernels, per_device(): pl.pallas_call(functools.partial(agent_kernel, tm_count - 1, group_steps)...  10.9 us
    pallas_call x1, Pallas kernels, temporal_gradient(): pl.pallas_call(temporal_backward, name='temporal_backward', out_shape=jax...  10.4 us
    all_to_all x1, waiting for transfers between devices, per_device(): lax.all_to_all(grad_lifted, 'tm', split_axis=0, concat_axis=0, tiled=True)  8.99 us
    pallas_call x1, Pallas kernels, per_device(): pl.pallas_call(temporal_forward, name='temporal_forward', out_shape=(jax....  7.91 us
    ppermute x7, starting transfers between devices, swap_chip(): return lax.ppermute(block, 'env', [(at, at ^ 2) for at in range(env_count)])  7.48 us
    ppermute x8, waiting for transfers between devices, ring(): return lax.ppermute(block, ('env', 'tm'), pairs)  6.16 us
  transfers between devices with their start and end apart: 26, of which 13 were waited for; matrix products, arithmetic and copies ran while one was open for 3% of the time, Pallas kernels for 14%

profile of v3, /device:TPU:0, one launch (start us, length us, event | category | flops | bytes accessed | tf_op | source)
XLA Modules:
  0.0 127.3 jit_solution(11428008571545627739)
XLA Ops:
  0.6 2.0 %pack_block.1.own_ref = bf16[128,1664]{1,0:T(8,128)(2,1)} custom-call(s32[1]{0:T(128)} %bitcast.env_ref, bf16[128,3072]{1,0:T(8,128)(2,1)} %shard_ref.1, bf16[128,3072]{1,0:T(8,128)(2,1)} %shard_ref.1, bf16[128,1024]{1,0:T(8,128)(2,1)} %w_out_ref.1, f32[1,1024]{1,0:T(1,128)} %bitcast.31), custom_call_target="tpu_custom_call" | custom-call | flops 262144 | bytes 1048576 | tf_op jit(solution)/shard_map/pack_block/pallas_call | solution.py:481
  2.7 3.0 %collective-permute-start = (bf16[128,1664]{1,0:T(8,128)(2,1)}, bf16[128,1664]{1,0:T(8,128)(2,1)S(1)}, u32[]{:S(2)}, u32[]{:S(2)}) collective-permute-start(bf16[128,1664]{1,0:T(8,128)(2,1)} %pack_block.1.own_ref), channel_id=1, source_target_pairs={{0,2},{1,0},{2,4},{3,1},{4,6},{5,3},{6,7},{7,5},{8,9},{9,11},{10,8... | collective-permute-start | bytes 1277960 | tf_op jit(solution)/shard_map/ppermute | solution.py:469
  6.4 7.9 %temporal_forward.1 = (bf16[256,1024]{1,0:T(8,128)(2,1)}, bf16[256,3072]{1,0:T(8,128)(2,1)}, bf16[8,256,256]{2,1,0:T(8,128)(2,1)}) custom-call(s32[1]{0:T(128)} %bitcast.19.done_ref, bf16[256,1024]{1,0:T(8,128)(2,1)} %bitcast.20, f32[1,1024]{1,0:T(1,128)} %bitcast.29, bf16[1024,3072]{1,0:T(8,128)(2,1)} %w_qkv_hbm.3, bf16[1024,1024]{1,0:T(8,128)(2,1)} %w_out_hbm.3), custom_call_target="tpu_custom_call" | custom-call | flops 2147483648 | bytes 8388608 | tf_op jit(solution)/shard_map/temporal_forward/pallas_call | solution.py:502
  16.3 5.8 %all-to-all-start = ((bf16[8,32,1024]{2,1,0:T(8,128)(2,1)}), bf16[8,32,1024]{2,1,0:T(8,128)(2,1)S(1)}, u32[]{:S(2)}, u32[]{:S(2)}) async-start(bf16[8,32,1024]{2,1,0:T(8,128)(2,1)} %bitcast.25), calls=%async_computation | async-start | bytes 1048576 | tf_op jit(solution)/shard_map/all_to_all | solution.py:525
  22.1 3.4 %collective-permute-done.2.rest_4_ = bf16[128,1664]{1,0:T(8,128)(2,1)S(1)} collective-permute-done((bf16[128,1664]{1,0:T(8,128)(2,1)S(1)}, bf16[128,1664]{1,0:T(8,128)(2,1)S(1)}, u32[]{:S(2)}, u32[]{:S(2)}) %collective-permute-start.2) | collective-permute-done | bytes 426016 | tf_op jit(solution)/shard_map/ppermute | solution.py:475
  25.6 1.6 %collective-permute-start.4 = (bf16[128,1664]{1,0:T(8,128)(2,1)S(1)}, bf16[128,1664]{1,0:T(8,128)(2,1)S(1)}, u32[]{:S(2)}, u32[]{:S(2)}) collective-permute-start(bf16[128,1664]{1,0:T(8,128)(2,1)S(1)} %collective-permute-done.1.rest_1_), channel_id=1, source_target_pairs={{0,16},{8,24},{16,0},{24,8},{1,17},{9,25},{17,1},{25,9},{2,18},{10... | collective-permute-start | bytes 1277960 | tf_op jit(solution)/shard_map/ppermute | solution.py:475
  27.2 1.6 %collective-permute-start.3 = (bf16[128,1664]{1,0:T(8,128)(2,1)S(1)}, bf16[128,1664]{1,0:T(8,128)(2,1)S(1)}, u32[]{:S(2)}, u32[]{:S(2)}) collective-permute-start(bf16[128,1664]{1,0:T(8,128)(2,1)S(1)} %collective-permute-done.1.rest_1_), channel_id=1, source_target_pairs={{0,2},{1,0},{2,4},{3,1},{4,6},{5,3},{6,7},{7,5},{8,9},{9,11},{10,8... | collective-permute-start | bytes 1277960 | tf_op jit(solution)/shard_map/ppermute | solution.py:469
  29.3 6.6 %collective-permute-done.4.rest_5_ = bf16[128,1664]{1,0:T(8,128)(2,1)S(1)} collective-permute-done((bf16[128,1664]{1,0:T(8,128)(2,1)S(1)}, bf16[128,1664]{1,0:T(8,128)(2,1)S(1)}, u32[]{:S(2)}, u32[]{:S(2)}) %collective-permute-start.4) | collective-permute-done | bytes 426016 | tf_op jit(solution)/shard_map/ppermute | solution.py:475
  38.2 3.8 %collective-permute-start.5 = (bf16[128,1664]{1,0:T(8,128)(2,1)S(1)}, bf16[128,1664]{1,0:T(8,128)(2,1)}, u32[]{:S(2)}, u32[]{:S(2)}) collective-permute-start(bf16[128,1664]{1,0:T(8,128)(2,1)S(1)} %collective-permute-done.3.rest_2_), channel_id=1, source_target_pairs={{0,2},{1,0},{2,4},{3,1},{4,6},{5,3},{6,7},{7,5},{8,9},{9,11},{10,8... | collective-permute-start | bytes 1277960 | tf_op jit(solution)/shard_map/ppermute | solution.py:469
  42.7 6.7 %collective-permute-done.6.rest_6_ = bf16[128,1664]{1,0:T(8,128)(2,1)} collective-permute-done((bf16[128,1664]{1,0:T(8,128)(2,1)S(1)}, bf16[128,1664]{1,0:T(8,128)(2,1)}, u32[]{:S(2)}, u32[]{:S(2)}) %collective-permute-start.6) | collective-permute-done | bytes 426016 | tf_op jit(solution)/shard_map/ppermute | solution.py:475
  52.1 10.9 %agent_block.1 = (bf16[256,1024]{1,0:T(8,128)(2,1)}, bf16[512,1024]{1,0:T(8,128)(2,1)}, bf16[256,1024]{1,0:T(8,128)(2,1)}, bf16[1024,128]{1,0:T(8,128)(2,1)}, f32[1,1024]{1,0:T(1,128)}, /*index=5*/f32[2,8,128]{2,1,0:T(8,128)}) custom-call(s32[1]{0:T(128)} %bitcast.env_ref, s32[1]{0:T(128)} %bitcast.1.tm_ref, bf16[256,1024]{1,0:T(8,128)(2,1)} %bitcast.24, ...), custom_call_target="tpu_custom_call" | custom-call | flops 2147483648 | bytes 4194304 | tf_op jit(solution)/shard_map/agent_block/pallas_call | solution.py:549
  63.2 2.7 %collective-permute-done.14.moved_ref = bf16[512,1024]{1,0:T(8,128)(2,1)S(1)} collective-permute-done((bf16[512,1024]{1,0:T(8,128)(2,1)}, bf16[512,1024]{1,0:T(8,128)(2,1)S(1)}, u32[]{:S(2)}, u32[]{:S(2)}) %collective-permute-start.14) | collective-permute-done | bytes 1048608 | tf_op jit(solution)/shard_map/ppermute | solution.py:472
  67.0 4.5 %weight_grad.1 = (bf16[128,1152]{1,0:T(8,128)(2,1)}, bf16[128,1152]{1,0:T(8,128)(2,1)}, bf16[128,1152]{1,0:T(8,128)(2,1)}, bf16[128,1152]{1,0:T(8,128)(2,1)}, bf...) custom-call(s32[1]{0:T(128)} %bitcast.env_ref, ...), custom_call_target="tpu_custom_call" | custom-call | flops 1073741824 | bytes 4194304 | tf_op jit(solution)/shard_map/weight_grad/pallas_call | solution.py:585
  71.9 3.3 %collective-permute-start.15 = (bf16[128,1152]{1,0:T(8,128)(2,1)}, bf16[128,1152]{1,0:T(8,128)(2,1)S(1)}, u32[]{:S(2)}, u32[]{:S(2)}) collective-permute-start(bf16[128,1152]{1,0:T(8,128)(2,1)} %get-tuple-element.53), channel_id=1, source_target_pairs={{0,2},{1,0},{2,4},{3,1},{4,6},{5,3},{6,7},{7,5},{8,9},{9,11},{10,8... | collective-permute-start | bytes 884744 | tf_op jit(solution)/shard_map/ppermute | solution.py:469
  75.1 3.8 %all-to-all-start.1 = ((bf16[8,32,1024]{2,1,0:T(8,128)(2,1)}), bf16[8,32,1024]{2,1,0:T(8,128)(2,1)S(1)}, u32[]{:S(2)}, u32[]{:S(2)}) async-start(bf16[8,32,1024]{2,1,0:T(8,128)(2,1)} %bitcast.11), calls=%async_computation.1 | async-start | bytes 1048576 | tf_op jit(solution)/shard_map/all_to_all | solution.py:581
  79.0 1.9 %collective-permute-done.16 = bf16[128,1152]{1,0:T(8,128)(2,1)S(1)} collective-permute-done((bf16[128,1152]{1,0:T(8,128)(2,1)}, bf16[128,1152]{1,0:T(8,128)(2,1)S(1)}, u32[]{:S(2)}, u32[]{:S(2)}) %collective-permute-start.16) | collective-permute-done | bytes 294944 | tf_op jit(solution)/shard_map/ppermute | solution.py:475
  82.2 3.0 %collective-permute-start.17 = (bf16[128,1152]{1,0:T(8,128)(2,1)S(1)}, bf16[128,1152]{1,0:T(8,128)(2,1)S(1)}, u32[]{:S(2)}, u32[]{:S(2)}) collective-permute-start(bf16[128,1152]{1,0:T(8,128)(2,1)S(1)} %add_convert_fusion.4), channel_id=1, source_target_pairs={{0,2},{1,0},{2,4},{3,1},{4,6},{5,3},{6,7},{7,5},{8,9},{9,11},{10,8... | collective-permute-start | bytes 884744 | tf_op jit(solution)/shard_map/ppermute | solution.py:469
  85.2 9.0 %all-to-all-done.1 = bf16[8,32,1024]{2,1,0:T(8,128)(2,1)S(1)} async-done(((bf16[8,32,1024]{2,1,0:T(8,128)(2,1)}), bf16[8,32,1024]{2,1,0:T(8,128)(2,1)S(1)}, u32[]{:S(2)}, u32[]{:S(2)}) %all-to-all-start.1) | async-done | bytes 524320 | tf_op jit(solution)/shard_map/all_to_all | solution.py:581
  95.0 2.1 %collective-permute-start.20 = (bf16[128,1152]{1,0:T(8,128)(2,1)S(1)}, bf16[128,1152]{1,0:T(8,128)(2,1)S(1)}, u32[]{:S(2)}, u32[]{:S(2)}) collective-permute-start(bf16[128,1152]{1,0:T(8,128)(2,1)S(1)} %copy-done.17), channel_id=1, source_target_pairs={{0,16},{8,24},{16,0},{24,8},{1,17},{9,25},{17,1},{25,9},{2,18},{10... | collective-permute-start | bytes 884744 | tf_op jit(solution)/shard_map/ppermute | solution.py:475
  97.1 10.4 %temporal_backward.1 = bf16[256,1024]{1,0:T(8,128)(2,1)} custom-call(f32[1,1024]{1,0:T(1,128)} %bitcast.30, bf16[256,1024]{1,0:T(8,128)(2,1)} %bitcast.22, bf16[256,1024]{1,0:T(8,128)(2,1)} %bitcast.21, bf16[256,3072]{1,0:T(8,128)(2,1)} %get-tuple-element.65.qkv_hbm, bf16[8,256,256]{2,1,0:T(8,128)(2,1)} %get-tuple-element.66.probs_hbm, ...), custom_call_target="tpu_custom_call" | custom-call | flops 2147483648 | bytes 8388608 | tf_op jit(solution)/shard_map/temporal_backward/pallas_call | solution.py:599
  107.7 1.7 %collective-permute-start.21 = (bf16[128,1152]{1,0:T(8,128)(2,1)S(1)}, bf16[128,1152]{1,0:T(8,128)(2,1)S(1)}, u32[]{:S(2)}, u32[]{:S(2)}) collective-permute-start(bf16[128,1152]{1,0:T(8,128)(2,1)S(1)} %add_convert_fusion.2), channel_id=1, source_target_pairs={{0,2},{1,0},{2,4},{3,1},{4,6},{5,3},{6,7},{7,5},{8,9},{9,11},{10,8... | collective-permute-start | bytes 884744 | tf_op jit(solution)/shard_map/ppermute | solution.py:469
  109.4 5.1 %collective-permute-done.21 = bf16[128,1152]{1,0:T(8,128)(2,1)S(1)} collective-permute-done((bf16[128,1152]{1,0:T(8,128)(2,1)S(1)}, bf16[128,1152]{1,0:T(8,128)(2,1)S(1)}, u32[]{:S(2)}, u32[]{:S(2)}) %collective-permute-start.21) | collective-permute-done | bytes 294944 | tf_op jit(solution)/shard_map/ppermute | solution.py:469
  116.5 5.8 %collective-permute-done.22 = bf16[128,1152]{1,0:T(8,128)(2,1)S(1)} collective-permute-done((bf16[128,1152]{1,0:T(8,128)(2,1)S(1)}, bf16[128,1152]{1,0:T(8,128)(2,1)S(1)}, u32[]{:S(2)}, u32[]{:S(2)}) %collective-permute-start.22) | collective-permute-done | bytes 294944 | tf_op jit(solution)/shard_map/ppermute | solution.py:475
  124.7 2.6 %finish.1 = (f32[128,3072]{1,0:T(8,128)}, f32[128,1024]{1,0:T(8,128)}) custom-call(s32[1]{0:T(128)} %bitcast.env_ref, bf16[128,1152]{1,0:T(8,128)(2,1)} %copy-done.1, bf16[128,1152]{1,0:T(8,128)(2,1)} %copy-done.4, f32[1,1024]{1,0:T(1,128)} %get-tuple-element.75.u_ref, f32[1,1024]{1,0:T(1,128)} %bitcast.33), custom_call_target="tpu_custom_call" | custom-call | flops 1048576 | bytes 2621440 | tf_op jit(solution)/shard_map/finish/pallas_call | solution.py:639
  (88 shorter events, 16.3 us)
Async XLA Ops:
  2.7 11.6 %collective-permute-start = (bf16[128,1664]{1,0:T(8,128)(2,1)}, bf16[128,1664]{1,0:T(8,128)(2,1)S(1)}, u32[]{:S(2)}, u32[]{:S(2)}) collective-permute-start(bf16[128,1664]{1,0:T(8,128)(2,1)} %pack_block.1.own_ref), channel_id=1, source_target_pairs={{0,2},{1,0},{2,4},{3,1},{4,6},{5,3},{6,7},{7,5},{8,9},{9,11},{10,8... | collective-permute-start | bytes 1277960 | tf_op jit(solution)/shard_map/ppermute | solution.py:469
  14.3 11.3 %collective-permute-start.2 = (bf16[128,1664]{1,0:T(8,128)(2,1)S(1)}, bf16[128,1664]{1,0:T(8,128)(2,1)S(1)}, u32[]{:S(2)}, u32[]{:S(2)}) collective-permute-start(bf16[128,1664]{1,0:T(8,128)(2,1)S(1)} %collective-permute-done.rest_0_), channel_id=1, source_target_pairs={{0,16},{8,24},{16,0},{24,8},{1,17},{9,25},{17,1},{25,9},{2,18},{10... | collective-permute-start | bytes 1277960 | tf_op jit(solution)/shard_map/ppermute | solution.py:475
  15.8 9.8 %collective-permute-start.1 = (bf16[128,1664]{1,0:T(8,128)(2,1)S(1)}, bf16[128,1664]{1,0:T(8,128)(2,1)S(1)}, u32[]{:S(2)}, u32[]{:S(2)}) collective-permute-start(bf16[128,1664]{1,0:T(8,128)(2,1)S(1)} %collective-permute-done.rest_0_), channel_id=1, source_target_pairs={{0,2},{1,0},{2,4},{3,1},{4,6},{5,3},{6,7},{7,5},{8,9},{9,11},{10,8... | collective-permute-start | bytes 1277960 | tf_op jit(solution)/shard_map/ppermute | solution.py:469
  16.3 25.7 %all-to-all-start = ((bf16[8,32,1024]{2,1,0:T(8,128)(2,1)}), bf16[8,32,1024]{2,1,0:T(8,128)(2,1)S(1)}, u32[]{:S(2)}, u32[]{:S(2)}) async-start(bf16[8,32,1024]{2,1,0:T(8,128)(2,1)} %bitcast.25), calls=%async_computation | async-start | bytes 1048576 | tf_op jit(solution)/shard_map/all_to_all | solution.py:525
  25.6 10.3 %collective-permute-start.4 = (bf16[128,1664]{1,0:T(8,128)(2,1)S(1)}, bf16[128,1664]{1,0:T(8,128)(2,1)S(1)}, u32[]{:S(2)}, u32[]{:S(2)}) collective-permute-start(bf16[128,1664]{1,0:T(8,128)(2,1)S(1)} %collective-permute-done.1.rest_1_), channel_id=1, source_target_pairs={{0,16},{8,24},{16,0},{24,8},{1,17},{9,25},{17,1},{25,9},{2,18},{10... | collective-permute-start | bytes 1277960 | tf_op jit(solution)/shard_map/ppermute | solution.py:475
  27.2 9.5 %collective-permute-start.3 = (bf16[128,1664]{1,0:T(8,128)(2,1)S(1)}, bf16[128,1664]{1,0:T(8,128)(2,1)S(1)}, u32[]{:S(2)}, u32[]{:S(2)}) collective-permute-start(bf16[128,1664]{1,0:T(8,128)(2,1)S(1)} %collective-permute-done.1.rest_1_), channel_id=1, source_target_pairs={{0,2},{1,0},{2,4},{3,1},{4,6},{5,3},{6,7},{7,5},{8,9},{9,11},{10,8... | collective-permute-start | bytes 1277960 | tf_op jit(solution)/shard_map/ppermute | solution.py:469
  28.8 13.2 %collective-permute-start.7 = (bf16[128,1664]{1,0:T(8,128)(2,1)S(1)}, bf16[128,1664]{1,0:T(8,128)(2,1)S(1)}, u32[]{:S(2)}, u32[]{:S(2)}) collective-permute-start(bf16[128,1664]{1,0:T(8,128)(2,1)S(1)} %collective-permute-done.rest_0_), channel_id=1, source_target_pairs={{0,8},{8,0},{16,24},{24,16},{1,9},{9,1},{17,25},{25,17},{2,10},{10... | collective-permute-start | bytes 1277960 | tf_op jit(solution)/shard_map/ppermute | solution.py:472
  28.8 13.8 %collective-permute-start.11 = (bf16[128,1664]{1,0:T(8,128)(2,1)S(1)}, bf16[128,1664]{1,0:T(8,128)(2,1)S(1)}, u32[]{:S(2)}, u32[]{:S(2)}) collective-permute-start(bf16[128,1664]{1,0:T(8,128)(2,1)S(1)} %collective-permute-done.2.rest_4_), channel_id=1, source_target_pairs={{0,8},{8,0},{16,24},{24,16},{1,9},{9,1},{17,25},{25,17},{2,10},{10... | collective-permute-start | bytes 1277960 | tf_op jit(solution)/shard_map/ppermute | solution.py:472
  36.7 12.6 %collective-permute-start.6 = (bf16[128,1664]{1,0:T(8,128)(2,1)S(1)}, bf16[128,1664]{1,0:T(8,128)(2,1)}, u32[]{:S(2)}, u32[]{:S(2)}) collective-permute-start(bf16[128,1664]{1,0:T(8,128)(2,1)S(1)} %collective-permute-done.3.rest_2_), channel_id=1, source_target_pairs={{0,16},{8,24},{16,0},{24,8},{1,17},{9,25},{17,1},{25,9},{2,18},{10... | collective-permute-start | bytes 1277960 | tf_op jit(solution)/shard_map/ppermute | solution.py:475
  38.2 11.2 %collective-permute-start.5 = (bf16[128,1664]{1,0:T(8,128)(2,1)S(1)}, bf16[128,1664]{1,0:T(8,128)(2,1)}, u32[]{:S(2)}, u32[]{:S(2)}) collective-permute-start(bf16[128,1664]{1,0:T(8,128)(2,1)S(1)} %collective-permute-done.3.rest_2_), channel_id=1, source_target_pairs={{0,2},{1,0},{2,4},{3,1},{4,6},{5,3},{6,7},{7,5},{8,9},{9,11},{10,8... | collective-permute-start | bytes 1277960 | tf_op jit(solution)/shard_map/ppermute | solution.py:469
  42.0 9.3 %collective-permute-start.8 = (bf16[128,1664]{1,0:T(8,128)(2,1)S(1)}, bf16[128,1664]{1,0:T(8,128)(2,1)}, u32[]{:S(2)}, u32[]{:S(2)}) collective-permute-start(bf16[128,1664]{1,0:T(8,128)(2,1)S(1)} %collective-permute-done.1.rest_1_), channel_id=1, source_target_pairs={{0,8},{8,0},{16,24},{24,16},{1,9},{9,1},{17,25},{25,17},{2,10},{10... | collective-permute-start | bytes 1277960 | tf_op jit(solution)/shard_map/ppermute | solution.py:472
  42.0 9.3 %collective-permute-start.9 = (bf16[128,1664]{1,0:T(8,128)(2,1)S(1)}, bf16[128,1664]{1,0:T(8,128)(2,1)}, u32[]{:S(2)}, u32[]{:S(2)}) collective-permute-start(bf16[128,1664]{1,0:T(8,128)(2,1)S(1)} %collective-permute-done.3.rest_2_), channel_id=1, source_target_pairs={{0,8},{8,0},{16,24},{24,16},{1,9},{9,1},{17,25},{25,17},{2,10},{10... | collective-permute-start | bytes 1277960 | tf_op jit(solution)/shard_map/ppermute | solution.py:472
  42.6 8.7 %collective-permute-start.12 = (bf16[128,1664]{1,0:T(8,128)(2,1)S(1)}, bf16[128,1664]{1,0:T(8,128)(2,1)}, u32[]{:S(2)}, u32[]{:S(2)}) collective-permute-start(bf16[128,1664]{1,0:T(8,128)(2,1)S(1)} %collective-permute-done.4.rest_5_), channel_id=1, source_target_pairs={{0,8},{8,0},{16,24},{24,16},{1,9},{9,1},{17,25},{25,17},{2,10},{10... | collective-permute-start | bytes 1277960 | tf_op jit(solution)/shard_map/ppermute | solution.py:472
  49.4 2.7 %collective-permute-start.10 = (bf16[128,1664]{1,0:T(8,128)(2,1)}, bf16[128,1664]{1,0:T(8,128)(2,1)}, u32[]{:S(2)}, u32[]{:S(2)}) collective-permute-start(bf16[128,1664]{1,0:T(8,128)(2,1)} %collective-permute-done.5.rest_3_), channel_id=1, source_target_pairs={{0,8},{8,0},{16,24},{24,16},{1,9},{9,1},{17,25},{25,17},{2,10},{10... | collective-permute-start | bytes 1277960 | tf_op jit(solution)/shard_map/ppermute | solution.py:472
  63.1 2.9 %collective-permute-start.14 = (bf16[512,1024]{1,0:T(8,128)(2,1)}, bf16[512,1024]{1,0:T(8,128)(2,1)S(1)}, u32[]{:S(2)}, u32[]{:S(2)}) collective-permute-start(bf16[512,1024]{1,0:T(8,128)(2,1)} %get-tuple-element.50.pack_ref), channel_id=1, source_target_pairs={{0,8},{8,0},{16,24},{24,16},{1,9},{9,1},{17,25},{25,17},{2,10},{10... | collective-permute-start | bytes 3145736 | tf_op jit(solution)/shard_map/ppermute | solution.py:472
  71.5 9.3 %collective-permute-start.16 = (bf16[128,1152]{1,0:T(8,128)(2,1)}, bf16[128,1152]{1,0:T(8,128)(2,1)S(1)}, u32[]{:S(2)}, u32[]{:S(2)}) collective-permute-start(bf16[128,1152]{1,0:T(8,128)(2,1)} %get-tuple-element.56), channel_id=1, source_target_pairs={{0,16},{8,24},{16,0},{24,8},{1,17},{9,25},{17,1},{25,9},{2,18},{10... | collective-permute-start | bytes 884744 | tf_op jit(solution)/shard_map/ppermute | solution.py:475
  71.9 9.3 %collective-permute-start.15 = (bf16[128,1152]{1,0:T(8,128)(2,1)}, bf16[128,1152]{1,0:T(8,128)(2,1)S(1)}, u32[]{:S(2)}, u32[]{:S(2)}) collective-permute-start(bf16[128,1152]{1,0:T(8,128)(2,1)} %get-tuple-element.53), channel_id=1, source_target_pairs={{0,2},{1,0},{2,4},{3,1},{4,6},{5,3},{6,7},{7,5},{8,9},{9,11},{10,8... | collective-permute-start | bytes 884744 | tf_op jit(solution)/shard_map/ppermute | solution.py:469
  75.1 19.1 %all-to-all-start.1 = ((bf16[8,32,1024]{2,1,0:T(8,128)(2,1)}), bf16[8,32,1024]{2,1,0:T(8,128)(2,1)S(1)}, u32[]{:S(2)}, u32[]{:S(2)}) async-start(bf16[8,32,1024]{2,1,0:T(8,128)(2,1)} %bitcast.11), calls=%async_computation.1 | async-start | bytes 1048576 | tf_op jit(solution)/shard_map/all_to_all | solution.py:581
  82.2 12.0 %collective-permute-start.17 = (bf16[128,1152]{1,0:T(8,128)(2,1)S(1)}, bf16[128,1152]{1,0:T(8,128)(2,1)S(1)}, u32[]{:S(2)}, u32[]{:S(2)}) collective-permute-start(bf16[128,1152]{1,0:T(8,128)(2,1)S(1)} %add_convert_fusion.4), channel_id=1, source_target_pairs={{0,2},{1,0},{2,4},{3,1},{4,6},{5,3},{6,7},{7,5},{8,9},{9,11},{10,8... | collective-permute-start | bytes 884744 | tf_op jit(solution)/shard_map/ppermute | solution.py:469
  85.2 9.0 %collective-permute-start.18 = (bf16[128,1152]{1,0:T(8,128)(2,1)S(1)}, bf16[128,1152]{1,0:T(8,128)(2,1)S(1)}, u32[]{:S(2)}, u32[]{:S(2)}) collective-permute-start(bf16[128,1152]{1,0:T(8,128)(2,1)S(1)} %copy-done.18), channel_id=1, source_target_pairs={{0,16},{8,24},{16,0},{24,8},{1,17},{9,25},{17,1},{25,9},{2,18},{10... | collective-permute-start | bytes 884744 | tf_op jit(solution)/shard_map/ppermute | solution.py:475
  94.4 13.2 %collective-permute-start.19 = (bf16[128,1152]{1,0:T(8,128)(2,1)S(1)}, bf16[128,1152]{1,0:T(8,128)(2,1)S(1)}, u32[]{:S(2)}, u32[]{:S(2)}) collective-permute-start(bf16[128,1152]{1,0:T(8,128)(2,1)S(1)} %add_convert_fusion.3), channel_id=1, source_target_pairs={{0,2},{1,0},{2,4},{3,1},{4,6},{5,3},{6,7},{7,5},{8,9},{9,11},{10,8... | collective-permute-start | bytes 884744 | tf_op jit(solution)/shard_map/ppermute | solution.py:469
  95.0 12.6 %collective-permute-start.20 = (bf16[128,1152]{1,0:T(8,128)(2,1)S(1)}, bf16[128,1152]{1,0:T(8,128)(2,1)S(1)}, u32[]{:S(2)}, u32[]{:S(2)}) collective-permute-start(bf16[128,1152]{1,0:T(8,128)(2,1)S(1)} %copy-done.17), channel_id=1, source_target_pairs={{0,16},{8,24},{16,0},{24,8},{1,17},{9,25},{17,1},{25,9},{2,18},{10... | collective-permute-start | bytes 884744 | tf_op jit(solution)/shard_map/ppermute | solution.py:475
  107.7 6.8 %collective-permute-start.21 = (bf16[128,1152]{1,0:T(8,128)(2,1)S(1)}, bf16[128,1152]{1,0:T(8,128)(2,1)S(1)}, u32[]{:S(2)}, u32[]{:S(2)}) collective-permute-start(bf16[128,1152]{1,0:T(8,128)(2,1)S(1)} %add_convert_fusion.2), channel_id=1, source_target_pairs={{0,2},{1,0},{2,4},{3,1},{4,6},{5,3},{6,7},{7,5},{8,9},{9,11},{10,8... | collective-permute-start | bytes 884744 | tf_op jit(solution)/shard_map/ppermute | solution.py:469
  114.5 7.7 %collective-permute-start.22 = (bf16[128,1152]{1,0:T(8,128)(2,1)S(1)}, bf16[128,1152]{1,0:T(8,128)(2,1)S(1)}, u32[]{:S(2)}, u32[]{:S(2)}) collective-permute-start(bf16[128,1152]{1,0:T(8,128)(2,1)S(1)} %add_convert_fusion.1), channel_id=1, source_target_pairs={{0,16},{8,24},{16,0},{24,8},{1,17},{9,25},{17,1},{25,9},{2,18},{10... | collective-permute-start | bytes 884744 | tf_op jit(solution)/shard_map/ppermute | solution.py:475
  (21 other events, 337.5 us)

commit v4 on v3

--- a/solution.py
+++ b/solution.py
@@ -13,7 +13,6 @@
 F32 = jnp.float32
 BF16 = jnp.bfloat16
 TILE = 256
-VMEM_BYTES = 60 * 1024 * 1024
 
 
 def dot_nn(a, b):
@@ -115,67 +114,86 @@
         out.wait()
 
 
-def temporal_backward(
-    gain_ref, grad_ref, rows_hbm, qkv_hbm, probs_hbm, w_qkv_hbm, w_out_hbm, out_ref,
-    rows_ref, qkv_ref, probs_ref, w_qkv, w_out, grad_mixed, grad_qkv, grad_normed, sems,
+def mix_grad_kernel(
+    first_head, grad_ref, w_hbm, qkv_hbm, probs_hbm, out_ref, w_ref, qkv_ref, probs_ref,
+    grad_mixed, sems,
 ):
-    length, width = rows_ref.shape
+    length, width = grad_ref.shape
     size = width // HEADS
+    heads, part = probs_ref.shape[0], out_ref.shape[1] // 3
     scale = 1.0 / math.sqrt(size)
-    tiles = width // TILE
-
-    def rows_of(step):
-        return pl.ds(pl.multiple_of(step * TILE, TILE), TILE)
-
-    def w_out_copy(step):
-        return pltpu.make_async_copy(
-            w_out_hbm.at[rows_of(step), :], w_out.at[rows_of(step), :], sems.at[step]
-        )
-
-    def w_qkv_copy(step):
-        return pltpu.make_async_copy(
-            w_qkv_hbm.at[rows_of(step), :], w_qkv.at[rows_of(step), :], sems.at[tiles + step]
-        )
-
-    qkv_copy = pltpu.make_async_copy(qkv_hbm, qkv_ref, sems.at[2 * tiles])
-    probs_copy = pltpu.make_async_copy(probs_hbm, probs_ref, sems.at[2 * tiles + 1])
-    rows_copy = pltpu.make_async_copy(rows_hbm, rows_ref, sems.at[2 * tiles + 2])
+    tiles, start = part // TILE, first_head * size
+
+    def w_copy(step):
+        source = pl.ds(pl.multiple_of(start + step * TILE, TILE), TILE)
+        target = pl.ds(pl.multiple_of(step * TILE, TILE), TILE)
+        return pltpu.make_async_copy(w_hbm.at[source, :], w_ref.at[target, :], sems.at[step])
+
     for step in range(tiles):
-        w_out_copy(step).start()
-    qkv_copy.start()
-    probs_copy.start()
+        w_copy(step).start()
+    moves = [
+        (qkv_hbm.at[:, pl.ds(at * width + start, part)], qkv_ref.at[:, pl.ds(at * part, part)])
+        for at in range(3)
+    ]
+    moves.append((probs_hbm.at[pl.ds(first_head, heads)], probs_ref))
+    copies = [
+        pltpu.make_async_copy(source, target, sems.at[tiles + at])
+        for at, (source, target) in enumerate(moves)
+    ]
+    for copy in copies:
+        copy.start()
 
     @pl.loop(0, tiles)
     def _(step):
-        w_out_copy(step).wait()
-        grad_mixed[:, rows_of(step)] = dot_nt(grad_ref[...], w_out[rows_of(step), :]).astype(BF16)
-
-    for step in range(tiles):
-        w_qkv_copy(step).start()
-    rows_copy.start()
-    qkv_copy.wait()
-    probs_copy.wait()
-
-    for head in range(HEADS):
+        w_copy(step).wait()
+        span = pl.ds(pl.multiple_of(step * TILE, TILE), TILE)
+        grad_mixed[:, span] = dot_nt(grad_ref[...], w_ref[span, :]).astype(BF16)
+
+    for copy in copies:
+        copy.wait()
+    for head in range(heads):
         query_span = pl.ds(head * size, size)
-        key_span = pl.ds(width + head * size, size)
-        value_span = pl.ds(2 * width + head * size, size)
+        key_span = pl.ds(part + head * size, size)
+        value_span = pl.ds(2 * part + head * size, size)
         probs = probs_ref[head]
         head_grad = grad_mixed[:, query_span]
-        grad_qkv[:, value_span] = dot_tn(probs, head_grad).astype(BF16)
+        out_ref[:, value_span] = dot_tn(probs, head_grad).astype(BF16)
         grad_probs = dot_nt(head_grad, qkv_ref[:, value_span])
         wide = probs.astype(F32)
         inner = jnp.sum(wide * grad_probs, axis=-1, keepdims=True)
         grad_scores = (wide * (grad_probs - inner) * scale).astype(BF16)
-        grad_qkv[:, query_span] = dot_nn(grad_scores, qkv_ref[:, key_span]).astype(BF16)
-        grad_qkv[:, key_span] = dot_tn(grad_scores, qkv_ref[:, query_span]).astype(BF16)
+        out_ref[:, query_span] = dot_nn(grad_scores, qkv_ref[:, key_span]).astype(BF16)
+        out_ref[:, key_span] = dot_tn(grad_scores, qkv_ref[:, query_span]).astype(BF16)
+
+
+def norm_grad_kernel(
+    gain_ref, grad_ref, rows_ref, low_ref, high_ref, w_hbm, out_ref, w_ref, grad_normed, sems
+):
+    width = rows_ref.shape[1]
+    tiles, part = width // TILE, low_ref.shape[1] // 3
+
+    def rows_of(step):
+        return pl.ds(pl.multiple_of(step * TILE, TILE), TILE)
+
+    def w_copy(step):
+        return pltpu.make_async_copy(
+            w_hbm.at[rows_of(step), :], w_ref.at[rows_of(step), :], sems.at[step]
+        )
+
+    for step in range(tiles):
+        w_copy(step).start()
 
     @pl.loop(0, tiles)
     def _(step):
-        w_qkv_copy(step).wait()
-        grad_normed[:, rows_of(step)] = dot_nt(grad_qkv[...], w_qkv[rows_of(step), :])
-
-    rows_copy.wait()
+        w_copy(step).wait()
+        total = None
+        for side, grads_ref in enumerate((low_ref, high_ref)):
+            for at in range(3):
+                columns = pl.ds(at * width + side * part, part)
+                product = dot_nt(grads_ref[:, pl.ds(at * part, part)], w_ref[rows_of(step), columns])
+                total = product if total is None else total + product
+        grad_normed[:, rows_of(step)] = total
+
     rows = rows_ref[...].astype(F32)
     pulled = norm_pull(rows, gain_ref[...], grad_normed[...])
     out_ref[...] = (grad_ref[...].astype(F32) + pulled).astype(BF16)
@@ -434,12 +452,14 @@
     return pl.BlockSpec(memory_space=pltpu.SMEM)
 
 
-def params():
-    return pltpu.CompilerParams(vmem_limit_bytes=VMEM_BYTES)
-
-
-def cost(flops, moved):
-    return pl.CostEstimate(flops=flops, bytes_accessed=moved, transcendentals=0)
+def params(mebibytes=60):
+    return pltpu.CompilerParams(vmem_limit_bytes=mebibytes * 1024 * 1024)
+
+
+def cost(microseconds):
+    return pl.CostEstimate(
+        flops=int(microseconds * 1e9), bytes_accessed=int(microseconds * 2e6), transcendentals=0
+    )
 
 
 def ring_order(count):
@@ -460,9 +480,9 @@
 
     ways = [1 if at in (0, 3) else -1 for at in range(env_count)]
 
-    def ring(block):
+    def ring(block, along=1):
         pairs = [
-            (env * tm_count + at, env * tm_count + order[(spot[at] + ways[env]) % tm_count])
+            (env * tm_count + at, env * tm_count + order[(spot[at] + along * ways[env]) % tm_count])
             for env in range(env_count)
             for at in range(tm_count)
         ]
@@ -494,7 +514,7 @@
             out_specs=pl.BlockSpec((depth, block_width), lambda at, env: (0, 0)),
         ),
         compiler_params=params(),
-        cost_estimate=cost(2 * depth * width, 8 * depth * width),
+        cost_estimate=cost(2),
     )(env_index, w_qkv_a, w_qkv_a, w_out_a, w_value[None])
     first_block = ring(own_block)
 
@@ -519,7 +539,7 @@
             pltpu.SemaphoreType.DMA((HEADS + 1,)),
         ],
         compiler_params=params(),
-        cost_estimate=cost(8 * length * width * width, 8 * width * width),
+        cost_estimate=cost(8),
     )(done_step[0], rows, gain_t[None], w_qkv_t, w_out_t)
     h1, first_block = lax.optimization_barrier((h1, first_block))
     lifted = lax.all_to_all(h1, "tm", split_axis=0, concat_axis=0, tiled=True)
@@ -570,7 +590,7 @@
             pltpu.SemaphoreType.DMA((2 * tm_count + 2,)),
         ],
         compiler_params=params(),
-        cost_estimate=cost(8 * total_rows * width * width, 4 * width * width),
+        cost_estimate=cost(11),
     )(
         env_index, tm_index, lifted, grouped(alive[0].astype(F32)), grouped(targets[0]), gain_a[None],
         w_value[None], w_qkv_a, own_block, *own_blocks, *other_blocks,
@@ -587,54 +607,68 @@
         name="weight_grad",
         out_shape=[jax.ShapeDtypeStruct((depth, width + 128), BF16)] * tm_count,
         in_specs=[smem_spec()] * 2 + [vmem_spec()] * 4,
-        out_specs=[hbm_spec()] * tm_count,
+        out_specs=[any_spec()] * tm_count,
         scratch_shapes=[
             pltpu.VMEM((width, width + 128), BF16),
             pltpu.SemaphoreType.DMA((tm_count,)),
         ],
-        compiler_params=params(),
-        cost_estimate=cost(4 * total_rows * width * width, 4 * width * width),
+        compiler_params=params(20),
+        cost_estimate=cost(4),
     )(env_index, tm_index, pack, keep, moved, extra)
-    def temporal_gradient(returned):
+    def mix_grad(first_head):
+        heads, part = HEADS // 2, width // 2
         return pl.pallas_call(
-            temporal_backward,
-            name="temporal_backward",
-            out_shape=jax.ShapeDtypeStruct((length, width), BF16),
-            in_specs=[vmem_spec()] * 2 + [hbm_spec()] * 5,
+            functools.partial(mix_grad_kernel, first_head),
+            name="temporal_mix_grad",
+            out_shape=jax.ShapeDtypeStruct((length, 3 * part), BF16),
+            in_specs=[vmem_spec()] + [hbm_spec()] * 3,
             out_specs=vmem_spec(),
             scratch_shapes=[
-                pltpu.VMEM((length, width), BF16),
-                pltpu.VMEM((length, 3 * width), BF16),
-                pltpu.VMEM((HEADS, length, length), BF16),
-                pltpu.VMEM((width, 3 * width), BF16),
-                pltpu.VMEM((width, width), BF16),
-                pltpu.VMEM((length, width), BF16),
-                pltpu.VMEM((length, 3 * width), BF16),
-                pltpu.VMEM((length, width), F32),
-                pltpu.SemaphoreType.DMA((3 + 2 * (width // TILE),)),
+                pltpu.VMEM((part, width), BF16),
+                pltpu.VMEM((length, 3 * part), BF16),
+                pltpu.VMEM((heads, length, length), BF16),
+                pltpu.VMEM((length, part), BF16),
+                pltpu.SemaphoreType.DMA((part // TILE + 4,)),
             ],
             compiler_params=params(),
-            cost_estimate=cost(8 * length * width * width, 8 * width * width),
-        )(gain_t[None], returned, rows, qkv, probs, w_qkv_t, w_out_t)
+            cost_estimate=cost(4),
+        )(returned, w_out_t, qkv, probs)
 
     term = dict(zip(hops, terms))
     travelling = ring(term[far])
-    chip_term = swap_chip(term[-near])
+    chip_terms = {hop: swap_chip(term[-hop]) for hop in range(near, 1, -1)}
+    arriving = ring(term[-1], -1)
     for hop in range(far - 1, 0, -1):
-        if hop > 1:
-            following, chip_term = lax.optimization_barrier((term[1 - hop], chip_term))
-            next_chip_term = swap_chip(following)
-        if hop == 2:
+        if hop == far - 1:
             travelling, returned = lax.optimization_barrier((travelling, returned))
-        if hop == 1:
-            input_grad = temporal_gradient(returned)
-            travelling, input_grad = lax.optimization_barrier((travelling, input_grad))
-        total = travelling.astype(F32) + term[hop].astype(F32) + chip_term.astype(F32)
+        if hop == max(far - 2, 1):
+            travelling, low_grads, arriving = lax.optimization_barrier(
+                (travelling, mix_grad(0), arriving)
+            )
+        if hop == max(far - 3, 1):
+            travelling, high_grads = lax.optimization_barrier((travelling, mix_grad(HEADS // 2)))
+        total = travelling.astype(F32) + term[hop].astype(F32)
+        if hop in chip_terms:
+            total = total + chip_terms[hop].astype(F32)
         travelling = ring(total.astype(BF16))
-        chip_term = next_chip_term
-    reduced = (travelling.astype(F32) + term[0].astype(F32)).astype(BF16)
+    input_grad = pl.pallas_call(
+        norm_grad_kernel,
+        name="temporal_norm_grad",
+        out_shape=jax.ShapeDtypeStruct((length, width), BF16),
+        in_specs=[vmem_spec()] * 5 + [hbm_spec()],
+        out_specs=vmem_spec(),
+        scratch_shapes=[
+            pltpu.VMEM((width, 3 * width), BF16),
+            pltpu.VMEM((length, width), F32),
+            pltpu.SemaphoreType.DMA((width // TILE,)),
+        ],
+        compiler_params=params(),
+        cost_estimate=cost(6),
+    )(gain_t[None], returned, rows, low_grads, high_grads, w_qkv_t)
+    reduced = travelling.astype(F32) + arriving.astype(F32) + term[0].astype(F32)
+    reduced = reduced.astype(BF16)
     reduced = (reduced.astype(F32) + swap_chip(reduced).astype(F32)).astype(BF16)
-    reduced, values = lax.optimization_barrier((reduced, values))
+    reduced, values, input_grad = lax.optimization_barrier((reduced, values, input_grad))
     other = swap_core(reduced)
     qkv_grad, out_grad = pl.pallas_call(
         finish_kernel,
@@ -645,8 +679,8 @@
         ),
         in_specs=[smem_spec()] + [vmem_spec()] * 4,
         out_specs=[vmem_spec()] * 2,
-        compiler_params=params(),
-        cost_estimate=cost(8 * depth * width, 20 * depth * width),
+        compiler_params=params(14),
+        cost_estimate=cost(2),
     )(env_index, reduced, other, u, w_value[None])
     return values, input_grad[None, None], qkv_grad, out_grad
 

time: 128 us -> 121 us (0.945)
  waiting for transfers between devices: 44.7 us -> 30.3 us
  Pallas kernels: 38.4 us -> 41.8 us
  starting transfers between devices: 36.6 us -> 39.7 us
  local copies, waits for them, and re-layouts: 4.64 us -> 6.23 us
    pallas_call x1 -> x3, Pallas kernels: 10.4 us -> 17.5 us  [the longest x2 10.7 us: mix_grad(): pl.pallas_call(functools.partial(mix_grad_kernel, first_head), name='temp...]
    ppermute x7 -> x6, waiting for transfers between devices: 24.4 us -> 18 us  [swap_chip(): return lax.ppermute(block, 'env', [(at, at ^ 2) for at in range(env_count)])]
    all_to_all x1, waiting for transfers between devices: 8.99 us -> 5.28 us  [per_device(): lax.all_to_all(grad_lifted, 'tm', split_axis=0, concat_axis=0, tiled=True)]
    ppermute x9, waiting for transfers between devices: 5.07 us -> 2.28 us  [swap_core(): return lax.ppermute(block, 'env', [(at, at ^ 1) for at in range(env_count)])]
    pallas_call x1, Pallas kernels: 4.53 us -> 1.91 us  [per_device(): pl.pallas_call(functools.partial(weight_grad_kernel, hops), name='weight_...]
    all_to_all x1, starting transfers between devices: 3.84 us -> 5.46 us  [per_device(): lax.all_to_all(grad_lifted, 'tm', split_axis=0, concat_axis=0, tiled=True)]
    ppermute x8 -> x9, starting transfers between devices: 17.5 us -> 19.1 us  [ring(): return lax.ppermute(block, ('env', 'tm'), pairs)]
    unnamed x38 -> x30, local copies, waits for them, and re-layouts: 1.73 us -> 3.26 us
  transfers between devices with their start and end apart: 26 -> 26, of which waited for: 13 -> 10; matrix products, arithmetic and copies ran while one was open for 3% -> 3% of each run, Pallas kernels for 14% -> 23%
where the time goes in v4:
time: 121 us; the launch traced here: 120 us
  Pallas kernels  41.8 us (35%)
  starting transfers between devices  39.7 us (33%)
  waiting for transfers between devices  30.3 us (25%)
  local copies, waits for them, and re-layouts  6.23 us (5%)
  between operations  1.57 us (1%)
    ppermute x9, starting transfers between devices, ring(): return lax.ppermute(block, ('env', 'tm'), pairs)  19.1 us
    ppermute x6, waiting for transfers between devices, swap_chip(): return lax.ppermute(block, 'env', [(at, at ^ 2) for at in range(env_count)])  18 us
    pallas_call x1, Pallas kernels, per_device(): pl.pallas_call(functools.partial(agent_kernel, tm_count - 1, group_steps)...  10.9 us
    pallas_call x2, Pallas kernels, mix_grad(): pl.pallas_call(functools.partial(mix_grad_kernel, first_head), name='temp...  10.7 us
    pallas_call x1, Pallas kernels, per_device(): pl.pallas_call(temporal_forward, name='temporal_forward', out_shape=(jax....  7.9 us
    ppermute x6, starting transfers between devices, swap_chip(): return lax.ppermute(block, 'env', [(at, at ^ 2) for at in range(env_count)])  7.34 us
    pallas_call x1, Pallas kernels, per_device(): pl.pallas_call(norm_grad_kernel, name='temporal_norm_grad', out_shape=jax...  6.79 us
    all_to_all x1, starting transfers between devices, per_device(): lifted = lax.all_to_all(h1, 'tm', split_axis=0, concat_axis=0, tiled=True)  5.84 us
  transfers between devices with their start and end apart: 26, of which 10 were waited for; matrix products, arithmetic and copies ran while one was open for 3% of the time, Pallas kernels for 23%

profile of v4, /device:TPU:0, one launch (start us, length us, event | category | flops | bytes accessed | tf_op | source)
XLA Modules:
  0.0 120.0 jit_solution(5600496120858487947)
XLA Ops:
  0.6 2.0 %pack_block.1.own_ref = bf16[128,1664]{1,0:T(8,128)(2,1)} custom-call(s32[1]{0:T(128)} %bitcast.env_ref, bf16[128,3072]{1,0:T(8,128)(2,1)} %shard_ref.1, bf16[128,3072]{1,0:T(8,128)(2,1)} %shard_ref.1, bf16[128,1024]{1,0:T(8,128)(2,1)} %w_out_ref.1, f32[1,1024]{1,0:T(1,128)} %bitcast.20), custom_call_target="tpu_custom_call" | custom-call | flops 2000000000 | bytes 4000000 | tf_op jit(solution)/shard_map/pack_block/pallas_call | solution.py:501
  2.6 3.0 %collective-permute-start = (bf16[128,1664]{1,0:T(8,128)(2,1)}, bf16[128,1664]{1,0:T(8,128)(2,1)S(1)}, u32[]{:S(2)}, u32[]{:S(2)}) collective-permute-start(bf16[128,1664]{1,0:T(8,128)(2,1)} %pack_block.1.own_ref), channel_id=1, source_target_pairs={{0,2},{1,0},{2,4},{3,1},{4,6},{5,3},{6,7},{7,5},{8,9},{9,11},{10,8... | collective-permute-start | bytes 1277960 | tf_op jit(solution)/shard_map/ppermute | solution.py:489
  6.3 7.9 %temporal_forward.1 = (bf16[256,1024]{1,0:T(8,128)(2,1)}, bf16[256,3072]{1,0:T(8,128)(2,1)}, bf16[8,256,256]{2,1,0:T(8,128)(2,1)}) custom-call(s32[1]{0:T(128)} %bitcast.19.done_ref, bf16[256,1024]{1,0:T(8,128)(2,1)} %bitcast.29, f32[1,1024]{1,0:T(1,128)} %bitcast.32, bf16[1024,3072]{1,0:T(8,128)(2,1)} %w_hbm.5, bf16[1024,1024]{1,0:T(8,128)(2,1)} %w_hbm.4), custom_call_target="tpu_custom_call" | custom-call | flops 8000000000 | bytes 16000000 | tf_op jit(solution)/shard_map/temporal_forward/pallas_call | solution.py:522
  16.3 5.8 %all-to-all-start = ((bf16[8,32,1024]{2,1,0:T(8,128)(2,1)}), bf16[8,32,1024]{2,1,0:T(8,128)(2,1)S(1)}, u32[]{:S(2)}, u32[]{:S(2)}) async-start(bf16[8,32,1024]{2,1,0:T(8,128)(2,1)} %bitcast.25), calls=%async_computation | async-start | bytes 1048576 | tf_op jit(solution)/shard_map/all_to_all | solution.py:545
  22.1 3.4 %collective-permute-done.2.rest_4_ = bf16[128,1664]{1,0:T(8,128)(2,1)S(1)} collective-permute-done((bf16[128,1664]{1,0:T(8,128)(2,1)S(1)}, bf16[128,1664]{1,0:T(8,128)(2,1)S(1)}, u32[]{:S(2)}, u32[]{:S(2)}) %collective-permute-start.2) | collective-permute-done | bytes 426016 | tf_op jit(solution)/shard_map/ppermute | solution.py:495
  25.6 1.6 %collective-permute-start.4 = (bf16[128,1664]{1,0:T(8,128)(2,1)S(1)}, bf16[128,1664]{1,0:T(8,128)(2,1)S(1)}, u32[]{:S(2)}, u32[]{:S(2)}) collective-permute-start(bf16[128,1664]{1,0:T(8,128)(2,1)S(1)} %collective-permute-done.1.rest_1_), channel_id=1, source_target_pairs={{0,16},{8,24},{16,0},{24,8},{1,17},{9,25},{17,1},{25,9},{2,18},{10... | collective-permute-start | bytes 1277960 | tf_op jit(solution)/shard_map/ppermute | solution.py:495
  27.2 1.6 %collective-permute-start.3 = (bf16[128,1664]{1,0:T(8,128)(2,1)S(1)}, bf16[128,1664]{1,0:T(8,128)(2,1)S(1)}, u32[]{:S(2)}, u32[]{:S(2)}) collective-permute-start(bf16[128,1664]{1,0:T(8,128)(2,1)S(1)} %collective-permute-done.1.rest_1_), channel_id=1, source_target_pairs={{0,2},{1,0},{2,4},{3,1},{4,6},{5,3},{6,7},{7,5},{8,9},{9,11},{10,8... | collective-permute-start | bytes 1277960 | tf_op jit(solution)/shard_map/ppermute | solution.py:489
  29.3 6.7 %collective-permute-done.4.rest_5_ = bf16[128,1664]{1,0:T(8,128)(2,1)S(1)} collective-permute-done((bf16[128,1664]{1,0:T(8,128)(2,1)S(1)}, bf16[128,1664]{1,0:T(8,128)(2,1)S(1)}, u32[]{:S(2)}, u32[]{:S(2)}) %collective-permute-start.4) | collective-permute-done | bytes 426016 | tf_op jit(solution)/shard_map/ppermute | solution.py:495
  38.2 3.8 %collective-permute-start.5 = (bf16[128,1664]{1,0:T(8,128)(2,1)S(1)}, bf16[128,1664]{1,0:T(8,128)(2,1)}, u32[]{:S(2)}, u32[]{:S(2)}) collective-permute-start(bf16[128,1664]{1,0:T(8,128)(2,1)S(1)} %collective-permute-done.3.rest_2_), channel_id=1, source_target_pairs={{0,2},{1,0},{2,4},{3,1},{4,6},{5,3},{6,7},{7,5},{8,9},{9,11},{10,8... | collective-permute-start | bytes 1277960 | tf_op jit(solution)/shard_map/ppermute | solution.py:489
  42.7 6.7 %collective-permute-done.6.rest_6_ = bf16[128,1664]{1,0:T(8,128)(2,1)} collective-permute-done((bf16[128,1664]{1,0:T(8,128)(2,1)S(1)}, bf16[128,1664]{1,0:T(8,128)(2,1)}, u32[]{:S(2)}, u32[]{:S(2)}) %collective-permute-start.6) | collective-permute-done | bytes 426016 | tf_op jit(solution)/shard_map/ppermute | solution.py:495
  52.1 10.9 %agent_block.1 = (bf16[256,1024]{1,0:T(8,128)(2,1)}, bf16[512,1024]{1,0:T(8,128)(2,1)}, bf16[256,1024]{1,0:T(8,128)(2,1)}, bf16[1024,128]{1,0:T(8,128)(2,1)}, f32[1,1024]{1,0:T(1,128)}, /*index=5*/f32[2,8,128]{2,1,0:T(8,128)}) custom-call(s32[1]{0:T(128)} %bitcast.env_ref, s32[1]{0:T(128)} %bitcast.1.tm_ref, bf16[256,1024]{1,0:T(8,128)(2,1)} %bitcast.23, ...), custom_call_target="tpu_custom_call" | custom-call | flops 11000000512 | bytes 22000000 | tf_op jit(solution)/shard_map/agent_block/pallas_call | solution.py:569
  63.2 5.5 %all-to-all-start.1 = ((bf16[8,32,1024]{2,1,0:T(8,128)(2,1)}), bf16[8,32,1024]{2,1,0:T(8,128)(2,1)}, u32[]{:S(2)}, u32[]{:S(2)}) async-start(bf16[8,32,1024]{2,1,0:T(8,128)(2,1)} %bitcast.24), calls=%async_computation.1 | async-start | bytes 1048576 | tf_op jit(solution)/shard_map/all_to_all | solution.py:601
  71.9 1.9 %weight_grad.1 = (bf16[128,1152]{1,0:T(8,128)(2,1)S(1)}, bf16[128,1152]{1,0:T(8,128)(2,1)S(1)}, bf16[128,1152]{1,0:T(8,128)(2,1)S(1)}, bf16[128,1152]{1,0:T(8,12...) custom-call(s32[1]{0:T(128)} %bitcast.env_ref, ...), custom_call_target="tpu_custom_call" | custom-call | flops 4000000000 | bytes 8000000 | tf_op jit(solution)/shard_map/weight_grad/pallas_call | solution.py:605
  73.8 2.2 %collective-permute-start.15 = (bf16[128,1152]{1,0:T(8,128)(2,1)S(1)}, bf16[128,1152]{1,0:T(8,128)(2,1)S(1)}, u32[]{:S(2)}, u32[]{:S(2)}) collective-permute-start(bf16[128,1152]{1,0:T(8,128)(2,1)S(1)} %get-tuple-element.53), channel_id=1, source_target_pairs={{0,2},{1,0},{2,4},{3,1},{4,6},{5,3},{6,7},{7,5},{8,9},{9,11},{10,8... | collective-permute-start | bytes 884744 | tf_op jit(solution)/shard_map/ppermute | solution.py:489
  76.4 1.6 %collective-permute-start.18 = (bf16[128,1152]{1,0:T(8,128)(2,1)S(1)}, bf16[128,1152]{1,0:T(8,128)(2,1)S(1)}, u32[]{:S(2)}, u32[]{:S(2)}) collective-permute-start(bf16[128,1152]{1,0:T(8,128)(2,1)S(1)} %get-tuple-element.61), channel_id=1, source_target_pairs={{0,1},{1,3},{2,0},{3,5},{4,2},{5,7},{6,4},{7,6},{8,10},{9,8},{10,1... | collective-permute-start | bytes 884744 | tf_op jit(solution)/shard_map/ppermute | solution.py:489
  79.4 5.3 %all-to-all-done.1 = bf16[8,32,1024]{2,1,0:T(8,128)(2,1)} async-done(((bf16[8,32,1024]{2,1,0:T(8,128)(2,1)}), bf16[8,32,1024]{2,1,0:T(8,128)(2,1)}, u32[]{:S(2)}, u32[]{:S(2)}) %all-to-all-start.1) | async-done | bytes 524320 | tf_op jit(solution)/shard_map/all_to_all | solution.py:601
  86.0 2.6 %collective-permute-start.17 = (bf16[128,1152]{1,0:T(8,128)(2,1)S(1)}, bf16[128,1152]{1,0:T(8,128)(2,1)S(1)}, u32[]{:S(2)}, u32[]{:S(2)}) collective-permute-start(bf16[128,1152]{1,0:T(8,128)(2,1)S(1)} %add_convert_fusion.4), channel_id=1, source_target_pairs={{0,2},{1,0},{2,4},{3,1},{4,6},{5,3},{6,7},{7,5},{8,9},{9,11},{10,8... | collective-permute-start | bytes 884744 | tf_op jit(solution)/shard_map/ppermute | solution.py:489
  88.6 5.3 %temporal_mix_grad.2.low_ref = bf16[256,1536]{1,0:T(8,128)(2,1)} custom-call(bf16[256,1024]{1,0:T(8,128)(2,1)} %bitcast.12.grad_ref, bf16[1024,1024]{1,0:T(8,128)(2,1)} %w_hbm.4, bf16[256,3072]{1,0:T(8,128)(2,1)} %get-tuple-element.59.qkv_hbm, bf16[8,256,256]{2,1,0:T(8,128)(2,1)} %get-tuple-element.60.probs_hbm), custom_call_target="tpu_custom_call" | custom-call | flops 4000000000 | bytes 8000000 | tf_op jit(solution)/shard_map/temporal_mix_grad/pallas_call | solution.py:620
  94.1 2.5 %collective-permute-start.20 = (bf16[128,1152]{1,0:T(8,128)(2,1)S(1)}, bf16[128,1152]{1,0:T(8,128)(2,1)S(1)}, u32[]{:S(2)}, u32[]{:S(2)}) collective-permute-start(bf16[128,1152]{1,0:T(8,128)(2,1)S(1)} %add_convert_fusion.3), channel_id=1, source_target_pairs={{0,2},{1,0},{2,4},{3,1},{4,6},{5,3},{6,7},{7,5},{8,9},{9,11},{10,8... | collective-permute-start | bytes 884744 | tf_op jit(solution)/shard_map/ppermute | solution.py:489
  96.6 5.3 %temporal_mix_grad.3.high_ref = bf16[256,1536]{1,0:T(8,128)(2,1)} custom-call(bf16[256,1024]{1,0:T(8,128)(2,1)} %bitcast.12.grad_ref, bf16[1024,1024]{1,0:T(8,128)(2,1)} %w_hbm.4, bf16[256,3072]{1,0:T(8,128)(2,1)} %get-tuple-element.59.qkv_hbm, bf16[8,256,256]{2,1,0:T(8,128)(2,1)} %get-tuple-element.60.probs_hbm), custom_call_target="tpu_custom_call" | custom-call | flops 4000000000 | bytes 8000000 | tf_op jit(solution)/shard_map/temporal_mix_grad/pallas_call | solution.py:620
  105.0 3.9 %collective-permute-done.21 = bf16[128,1152]{1,0:T(8,128)(2,1)S(1)} collective-permute-done((bf16[128,1152]{1,0:T(8,128)(2,1)S(1)}, bf16[128,1152]{1,0:T(8,128)(2,1)S(1)}, u32[]{:S(2)}, u32[]{:S(2)}) %collective-permute-start.21) | collective-permute-done | bytes 294944 | tf_op jit(solution)/shard_map/ppermute | solution.py:489
  109.9 6.8 %temporal_norm_grad.1 = bf16[256,1024]{1,0:T(8,128)(2,1)} custom-call(f32[1,1024]{1,0:T(1,128)} %bitcast.33, bf16[256,1024]{1,0:T(8,128)(2,1)} %bitcast.12.grad_ref, bf16[256,1024]{1,0:T(8,128)(2,1)} %bitcast.30, bf16[256,1536]{1,0:T(8,128)(2,1)} %temporal_mix_grad.2.low_ref, bf16[256,1536]{1,0:T(8,128)(2,1)} %temporal_mix_grad.3.high_ref, ...), custom_call_target="tpu_custom_call" | custom-call | flops 6000000000 | bytes 12000000 | tf_op jit(solution)/shard_map/temporal_norm_grad/pallas_call | solution.py:654
  116.9 1.6 %collective-permute-done.23.other_ref = bf16[128,1152]{1,0:T(8,128)(2,1)S(1)} collective-permute-done((bf16[128,1152]{1,0:T(8,128)(2,1)S(1)}, bf16[128,1152]{1,0:T(8,128)(2,1)S(1)}, u32[]{:S(2)}, u32[]{:S(2)}) %collective-permute-start.23) | collective-permute-done | bytes 294944 | tf_op jit(solution)/shard_map/ppermute | solution.py:492
  118.4 1.6 %finish.1 = (f32[128,3072]{1,0:T(8,128)}, f32[128,1024]{1,0:T(8,128)}) custom-call(s32[1]{0:T(128)} %bitcast.env_ref, bf16[128,1152]{1,0:T(8,128)(2,1)S(1)} %add_convert_fusion.own_ref, bf16[128,1152]{1,0:T(8,128)(2,1)S(1)} %collective-permute-done.23.other_ref, f32[1,1024]{1,0:T(1,128)S(1)} %copy-done.4, f32[1,1024]{1,0:T(1,128)S(1)} %bitcast.22), custom_call_target="tpu_custom_call" | custom-call | flops 2000000000 | bytes 4000000 | tf_op jit(solution)/shard_map/finish/pallas_call | solution.py:673
  (82 shorter events, 19.1 us)
Async XLA Ops:
  2.6 11.6 %collective-permute-start = (bf16[128,1664]{1,0:T(8,128)(2,1)}, bf16[128,1664]{1,0:T(8,128)(2,1)S(1)}, u32[]{:S(2)}, u32[]{:S(2)}) collective-permute-start(bf16[128,1664]{1,0:T(8,128)(2,1)} %pack_block.1.own_ref), channel_id=1, source_target_pairs={{0,2},{1,0},{2,4},{3,1},{4,6},{5,3},{6,7},{7,5},{8,9},{9,11},{10,8... | collective-permute-start | bytes 1277960 | tf_op jit(solution)/shard_map/ppermute | solution.py:489
  14.3 11.3 %collective-permute-start.2 = (bf16[128,1664]{1,0:T(8,128)(2,1)S(1)}, bf16[128,1664]{1,0:T(8,128)(2,1)S(1)}, u32[]{:S(2)}, u32[]{:S(2)}) collective-permute-start(bf16[128,1664]{1,0:T(8,128)(2,1)S(1)} %collective-permute-done.rest_0_), channel_id=1, source_target_pairs={{0,16},{8,24},{16,0},{24,8},{1,17},{9,25},{17,1},{25,9},{2,18},{10... | collective-permute-start | bytes 1277960 | tf_op jit(solution)/shard_map/ppermute | solution.py:495
  15.8 9.8 %collective-permute-start.1 = (bf16[128,1664]{1,0:T(8,128)(2,1)S(1)}, bf16[128,1664]{1,0:T(8,128)(2,1)S(1)}, u32[]{:S(2)}, u32[]{:S(2)}) collective-permute-start(bf16[128,1664]{1,0:T(8,128)(2,1)S(1)} %collective-permute-done.rest_0_), channel_id=1, source_target_pairs={{0,2},{1,0},{2,4},{3,1},{4,6},{5,3},{6,7},{7,5},{8,9},{9,11},{10,8... | collective-permute-start | bytes 1277960 | tf_op jit(solution)/shard_map/ppermute | solution.py:489
  16.3 25.7 %all-to-all-start = ((bf16[8,32,1024]{2,1,0:T(8,128)(2,1)}), bf16[8,32,1024]{2,1,0:T(8,128)(2,1)S(1)}, u32[]{:S(2)}, u32[]{:S(2)}) async-start(bf16[8,32,1024]{2,1,0:T(8,128)(2,1)} %bitcast.25), calls=%async_computation | async-start | bytes 1048576 | tf_op jit(solution)/shard_map/all_to_all | solution.py:545
  25.6 10.4 %collective-permute-start.4 = (bf16[128,1664]{1,0:T(8,128)(2,1)S(1)}, bf16[128,1664]{1,0:T(8,128)(2,1)S(1)}, u32[]{:S(2)}, u32[]{:S(2)}) collective-permute-start(bf16[128,1664]{1,0:T(8,128)(2,1)S(1)} %collective-permute-done.1.rest_1_), channel_id=1, source_target_pairs={{0,16},{8,24},{16,0},{24,8},{1,17},{9,25},{17,1},{25,9},{2,18},{10... | collective-permute-start | bytes 1277960 | tf_op jit(solution)/shard_map/ppermute | solution.py:495
  27.2 9.5 %collective-permute-start.3 = (bf16[128,1664]{1,0:T(8,128)(2,1)S(1)}, bf16[128,1664]{1,0:T(8,128)(2,1)S(1)}, u32[]{:S(2)}, u32[]{:S(2)}) collective-permute-start(bf16[128,1664]{1,0:T(8,128)(2,1)S(1)} %collective-permute-done.1.rest_1_), channel_id=1, source_target_pairs={{0,2},{1,0},{2,4},{3,1},{4,6},{5,3},{6,7},{7,5},{8,9},{9,11},{10,8... | collective-permute-start | bytes 1277960 | tf_op jit(solution)/shard_map/ppermute | solution.py:489
  28.8 13.2 %collective-permute-start.7 = (bf16[128,1664]{1,0:T(8,128)(2,1)S(1)}, bf16[128,1664]{1,0:T(8,128)(2,1)S(1)}, u32[]{:S(2)}, u32[]{:S(2)}) collective-permute-start(bf16[128,1664]{1,0:T(8,128)(2,1)S(1)} %collective-permute-done.rest_0_), channel_id=1, source_target_pairs={{0,8},{8,0},{16,24},{24,16},{1,9},{9,1},{17,25},{25,17},{2,10},{10... | collective-permute-start | bytes 1277960 | tf_op jit(solution)/shard_map/ppermute | solution.py:492
  28.8 13.8 %collective-permute-start.11 = (bf16[128,1664]{1,0:T(8,128)(2,1)S(1)}, bf16[128,1664]{1,0:T(8,128)(2,1)S(1)}, u32[]{:S(2)}, u32[]{:S(2)}) collective-permute-start(bf16[128,1664]{1,0:T(8,128)(2,1)S(1)} %collective-permute-done.2.rest_4_), channel_id=1, source_target_pairs={{0,8},{8,0},{16,24},{24,16},{1,9},{9,1},{17,25},{25,17},{2,10},{10... | collective-permute-start | bytes 1277960 | tf_op jit(solution)/shard_map/ppermute | solution.py:492
  36.7 12.6 %collective-permute-start.6 = (bf16[128,1664]{1,0:T(8,128)(2,1)S(1)}, bf16[128,1664]{1,0:T(8,128)(2,1)}, u32[]{:S(2)}, u32[]{:S(2)}) collective-permute-start(bf16[128,1664]{1,0:T(8,128)(2,1)S(1)} %collective-permute-done.3.rest_2_), channel_id=1, source_target_pairs={{0,16},{8,24},{16,0},{24,8},{1,17},{9,25},{17,1},{25,9},{2,18},{10... | collective-permute-start | bytes 1277960 | tf_op jit(solution)/shard_map/ppermute | solution.py:495
  38.2 11.2 %collective-permute-start.5 = (bf16[128,1664]{1,0:T(8,128)(2,1)S(1)}, bf16[128,1664]{1,0:T(8,128)(2,1)}, u32[]{:S(2)}, u32[]{:S(2)}) collective-permute-start(bf16[128,1664]{1,0:T(8,128)(2,1)S(1)} %collective-permute-done.3.rest_2_), channel_id=1, source_target_pairs={{0,2},{1,0},{2,4},{3,1},{4,6},{5,3},{6,7},{7,5},{8,9},{9,11},{10,8... | collective-permute-start | bytes 1277960 | tf_op jit(solution)/shard_map/ppermute | solution.py:489
  42.0 9.4 %collective-permute-start.8 = (bf16[128,1664]{1,0:T(8,128)(2,1)S(1)}, bf16[128,1664]{1,0:T(8,128)(2,1)}, u32[]{:S(2)}, u32[]{:S(2)}) collective-permute-start(bf16[128,1664]{1,0:T(8,128)(2,1)S(1)} %collective-permute-done.1.rest_1_), channel_id=1, source_target_pairs={{0,8},{8,0},{16,24},{24,16},{1,9},{9,1},{17,25},{25,17},{2,10},{10... | collective-permute-start | bytes 1277960 | tf_op jit(solution)/shard_map/ppermute | solution.py:492
  42.0 9.4 %collective-permute-start.9 = (bf16[128,1664]{1,0:T(8,128)(2,1)S(1)}, bf16[128,1664]{1,0:T(8,128)(2,1)}, u32[]{:S(2)}, u32[]{:S(2)}) collective-permute-start(bf16[128,1664]{1,0:T(8,128)(2,1)S(1)} %collective-permute-done.3.rest_2_), channel_id=1, source_target_pairs={{0,8},{8,0},{16,24},{24,16},{1,9},{9,1},{17,25},{25,17},{2,10},{10... | collective-permute-start | bytes 1277960 | tf_op jit(solution)/shard_map/ppermute | solution.py:492
  42.6 8.8 %collective-permute-start.12 = (bf16[128,1664]{1,0:T(8,128)(2,1)S(1)}, bf16[128,1664]{1,0:T(8,128)(2,1)}, u32[]{:S(2)}, u32[]{:S(2)}) collective-permute-start(bf16[128,1664]{1,0:T(8,128)(2,1)S(1)} %collective-permute-done.4.rest_5_), channel_id=1, source_target_pairs={{0,8},{8,0},{16,24},{24,16},{1,9},{9,1},{17,25},{25,17},{2,10},{10... | collective-permute-start | bytes 1277960 | tf_op jit(solution)/shard_map/ppermute | solution.py:492
  49.3 2.7 %collective-permute-start.10 = (bf16[128,1664]{1,0:T(8,128)(2,1)}, bf16[128,1664]{1,0:T(8,128)(2,1)}, u32[]{:S(2)}, u32[]{:S(2)}) collective-permute-start(bf16[128,1664]{1,0:T(8,128)(2,1)} %collective-permute-done.5.rest_3_), channel_id=1, source_target_pairs={{0,8},{8,0},{16,24},{24,16},{1,9},{9,1},{17,25},{25,17},{2,10},{10... | collective-permute-start | bytes 1277960 | tf_op jit(solution)/shard_map/ppermute | solution.py:492
  63.0 5.7 %collective-permute-start.14 = (bf16[512,1024]{1,0:T(8,128)(2,1)}, bf16[512,1024]{1,0:T(8,128)(2,1)S(1)}, u32[]{:S(2)}, u32[]{:S(2)}) collective-permute-start(bf16[512,1024]{1,0:T(8,128)(2,1)} %get-tuple-element.50.pack_ref), channel_id=1, source_target_pairs={{0,8},{8,0},{16,24},{24,16},{1,9},{9,1},{17,25},{25,17},{2,10},{10... | collective-permute-start | bytes 3145736 | tf_op jit(solution)/shard_map/ppermute | solution.py:492
  63.2 21.4 %all-to-all-start.1 = ((bf16[8,32,1024]{2,1,0:T(8,128)(2,1)}), bf16[8,32,1024]{2,1,0:T(8,128)(2,1)}, u32[]{:S(2)}, u32[]{:S(2)}) async-start(bf16[8,32,1024]{2,1,0:T(8,128)(2,1)} %bitcast.24), calls=%async_computation.1 | async-start | bytes 1048576 | tf_op jit(solution)/shard_map/all_to_all | solution.py:601
  73.8 10.8 %collective-permute-start.15 = (bf16[128,1152]{1,0:T(8,128)(2,1)S(1)}, bf16[128,1152]{1,0:T(8,128)(2,1)S(1)}, u32[]{:S(2)}, u32[]{:S(2)}) collective-permute-start(bf16[128,1152]{1,0:T(8,128)(2,1)S(1)} %get-tuple-element.53), channel_id=1, source_target_pairs={{0,2},{1,0},{2,4},{3,1},{4,6},{5,3},{6,7},{7,5},{8,9},{9,11},{10,8... | collective-permute-start | bytes 884744 | tf_op jit(solution)/shard_map/ppermute | solution.py:489
  76.0 9.9 %collective-permute-start.16 = (bf16[128,1152]{1,0:T(8,128)(2,1)S(1)}, bf16[128,1152]{1,0:T(8,128)(2,1)S(1)}, u32[]{:S(2)}, u32[]{:S(2)}) collective-permute-start(bf16[128,1152]{1,0:T(8,128)(2,1)S(1)} %get-tuple-element.57), channel_id=1, source_target_pairs={{0,16},{8,24},{16,0},{24,8},{1,17},{9,25},{17,1},{25,9},{2,18},{10... | collective-permute-start | bytes 884744 | tf_op jit(solution)/shard_map/ppermute | solution.py:495
  76.4 17.6 %collective-permute-start.18 = (bf16[128,1152]{1,0:T(8,128)(2,1)S(1)}, bf16[128,1152]{1,0:T(8,128)(2,1)S(1)}, u32[]{:S(2)}, u32[]{:S(2)}) collective-permute-start(bf16[128,1152]{1,0:T(8,128)(2,1)S(1)} %get-tuple-element.61), channel_id=1, source_target_pairs={{0,1},{1,3},{2,0},{3,5},{4,2},{5,7},{6,4},{7,6},{8,10},{9,8},{10,1... | collective-permute-start | bytes 884744 | tf_op jit(solution)/shard_map/ppermute | solution.py:489
  78.0 16.0 %collective-permute-start.19 = (bf16[128,1152]{1,0:T(8,128)(2,1)S(1)}, bf16[128,1152]{1,0:T(8,128)(2,1)S(1)}, u32[]{:S(2)}, u32[]{:S(2)}) collective-permute-start(bf16[128,1152]{1,0:T(8,128)(2,1)S(1)} %get-tuple-element.64), channel_id=1, source_target_pairs={{0,16},{8,24},{16,0},{24,8},{1,17},{9,25},{17,1},{25,9},{2,18},{10... | collective-permute-start | bytes 884744 | tf_op jit(solution)/shard_map/ppermute | solution.py:495
  86.0 7.9 %collective-permute-start.17 = (bf16[128,1152]{1,0:T(8,128)(2,1)S(1)}, bf16[128,1152]{1,0:T(8,128)(2,1)S(1)}, u32[]{:S(2)}, u32[]{:S(2)}) collective-permute-start(bf16[128,1152]{1,0:T(8,128)(2,1)S(1)} %add_convert_fusion.4), channel_id=1, source_target_pairs={{0,2},{1,0},{2,4},{3,1},{4,6},{5,3},{6,7},{7,5},{8,9},{9,11},{10,8... | collective-permute-start | bytes 884744 | tf_op jit(solution)/shard_map/ppermute | solution.py:489
  94.1 7.9 %collective-permute-start.20 = (bf16[128,1152]{1,0:T(8,128)(2,1)S(1)}, bf16[128,1152]{1,0:T(8,128)(2,1)S(1)}, u32[]{:S(2)}, u32[]{:S(2)}) collective-permute-start(bf16[128,1152]{1,0:T(8,128)(2,1)S(1)} %add_convert_fusion.3), channel_id=1, source_target_pairs={{0,2},{1,0},{2,4},{3,1},{4,6},{5,3},{6,7},{7,5},{8,9},{9,11},{10,8... | collective-permute-start | bytes 884744 | tf_op jit(solution)/shard_map/ppermute | solution.py:489
  102.1 6.8 %collective-permute-start.21 = (bf16[128,1152]{1,0:T(8,128)(2,1)S(1)}, bf16[128,1152]{1,0:T(8,128)(2,1)S(1)}, u32[]{:S(2)}, u32[]{:S(2)}) collective-permute-start(bf16[128,1152]{1,0:T(8,128)(2,1)S(1)} %add_convert_fusion.2), channel_id=1, source_target_pairs={{0,2},{1,0},{2,4},{3,1},{4,6},{5,3},{6,7},{7,5},{8,9},{9,11},{10,8... | collective-permute-start | bytes 884744 | tf_op jit(solution)/shard_map/ppermute | solution.py:489
  109.0 7.7 %collective-permute-start.22 = (bf16[128,1152]{1,0:T(8,128)(2,1)S(1)}, bf16[128,1152]{1,0:T(8,128)(2,1)S(1)}, u32[]{:S(2)}, u32[]{:S(2)}) collective-permute-start(bf16[128,1152]{1,0:T(8,128)(2,1)S(1)} %add_convert_fusion.1), channel_id=1, source_target_pairs={{0,16},{8,24},{16,0},{24,8},{1,17},{9,25},{17,1},{25,9},{2,18},{10... | collective-permute-start | bytes 884744 | tf_op jit(solution)/shard_map/ppermute | solution.py:495
  (17 other events, 265.7 us)

commit v5 on v4

--- a/solution.py
+++ b/solution.py
@@ -115,7 +115,7 @@
 
 
 def mix_grad_kernel(
-    first_head, grad_ref, w_hbm, qkv_hbm, probs_hbm, out_ref, w_ref, qkv_ref, probs_ref,
+    first_head, grad_hbm, w_hbm, qkv_hbm, probs_hbm, out_ref, grad_ref, w_ref, qkv_ref, probs_ref,
     grad_mixed, sems,
 ):
     length, width = grad_ref.shape
@@ -129,6 +129,8 @@
         target = pl.ds(pl.multiple_of(step * TILE, TILE), TILE)
         return pltpu.make_async_copy(w_hbm.at[source, :], w_ref.at[target, :], sems.at[step])
 
+    grad_copy = pltpu.make_async_copy(grad_hbm, grad_ref, sems.at[tiles + 4])
+    grad_copy.start()
     for step in range(tiles):
         w_copy(step).start()
     moves = [
@@ -142,6 +144,7 @@
     ]
     for copy in copies:
         copy.start()
+    grad_copy.wait()
 
     @pl.loop(0, tiles)
     def _(step):
@@ -167,7 +170,8 @@
 
 
 def norm_grad_kernel(
-    gain_ref, grad_ref, rows_ref, low_ref, high_ref, w_hbm, out_ref, w_ref, grad_normed, sems
+    gain_ref, grad_hbm, rows_hbm, low_hbm, high_hbm, w_hbm, out_ref,
+    grad_ref, rows_ref, low_ref, high_ref, w_ref, grad_normed, sems,
 ):
     width = rows_ref.shape[1]
     tiles, part = width // TILE, low_ref.shape[1] // 3
@@ -180,8 +184,19 @@
             w_hbm.at[rows_of(step), :], w_ref.at[rows_of(step), :], sems.at[step]
         )
 
+    moves = [(low_hbm, low_ref), (high_hbm, high_ref), (grad_hbm, grad_ref), (rows_hbm, rows_ref)]
+    copies = [
+        pltpu.make_async_copy(source, target, sems.at[tiles + at])
+        for at, (source, target) in enumerate(moves)
+    ]
+    for copy in copies[:2]:
+        copy.start()
     for step in range(tiles):
         w_copy(step).start()
+    for copy in copies[2:]:
+        copy.start()
+    for copy in copies[:2]:
+        copy.wait()
 
     @pl.loop(0, tiles)
     def _(step):
@@ -194,6 +209,8 @@
                 total = product if total is None else total + product
         grad_normed[:, rows_of(step)] = total
 
+    for copy in copies[2:]:
+        copy.wait()
     rows = rows_ref[...].astype(F32)
     pulled = norm_pull(rows, gain_ref[...], grad_normed[...])
     out_ref[...] = (grad_ref[...].astype(F32) + pulled).astype(BF16)
@@ -488,6 +505,14 @@
         ]
         return lax.ppermute(block, ("env", "tm"), pairs)
 
+    def ring_other_chip(block):
+        pairs = [
+            (env * tm_count + at, (env ^ 2) * tm_count + order[(spot[at] + ways[env]) % tm_count])
+            for env in range(env_count)
+            for at in range(tm_count)
+        ]
+        return lax.ppermute(block, ("env", "tm"), pairs)
+
     def swap_core(block):
         return lax.ppermute(block, "env", [(at, at ^ 1) for at in range(env_count)])
 
@@ -621,14 +646,15 @@
             functools.partial(mix_grad_kernel, first_head),
             name="temporal_mix_grad",
             out_shape=jax.ShapeDtypeStruct((length, 3 * part), BF16),
-            in_specs=[vmem_spec()] + [hbm_spec()] * 3,
+            in_specs=[hbm_spec()] * 4,
             out_specs=vmem_spec(),
             scratch_shapes=[
+                pltpu.VMEM((length, width), BF16),
                 pltpu.VMEM((part, width), BF16),
                 pltpu.VMEM((length, 3 * part), BF16),
                 pltpu.VMEM((heads, length, length), BF16),
                 pltpu.VMEM((length, part), BF16),
-                pltpu.SemaphoreType.DMA((part // TILE + 4,)),
+                pltpu.SemaphoreType.DMA((part // TILE + 5,)),
             ],
             compiler_params=params(),
             cost_estimate=cost(4),
@@ -640,34 +666,44 @@
     arriving = ring(term[-1], -1)
     for hop in range(far - 1, 0, -1):
         if hop == far - 1:
-            travelling, returned = lax.optimization_barrier((travelling, returned))
+            travelling, returned, arriving = lax.optimization_barrier(
+                (travelling, returned, arriving)
+            )
+            near_sum = (arriving.astype(F32) + term[0].astype(F32)).astype(BF16)
+            far_sum = swap_chip(near_sum)
         if hop == max(far - 2, 1):
-            travelling, low_grads, arriving = lax.optimization_barrier(
-                (travelling, mix_grad(0), arriving)
+            travelling, low_grads = lax.optimization_barrier((travelling, mix_grad(0)))
+        if hop == max(far - 3, 1):
+            travelling, high_grads, far_sum = lax.optimization_barrier(
+                (travelling, mix_grad(HEADS // 2), far_sum)
             )
-        if hop == max(far - 3, 1):
-            travelling, high_grads = lax.optimization_barrier((travelling, mix_grad(HEADS // 2)))
         total = travelling.astype(F32) + term[hop].astype(F32)
         if hop in chip_terms:
             total = total + chip_terms[hop].astype(F32)
-        travelling = ring(total.astype(BF16))
+        total = total.astype(BF16)
+        if hop == 1:
+            crossing = ring_other_chip(total)
+        travelling = ring(total)
     input_grad = pl.pallas_call(
         norm_grad_kernel,
         name="temporal_norm_grad",
         out_shape=jax.ShapeDtypeStruct((length, width), BF16),
-        in_specs=[vmem_spec()] * 5 + [hbm_spec()],
+        in_specs=[vmem_spec()] + [hbm_spec()] * 5,
         out_specs=vmem_spec(),
         scratch_shapes=[
+            pltpu.VMEM((length, width), BF16),
+            pltpu.VMEM((length, width), BF16),
+            pltpu.VMEM((length, 3 * width // 2), BF16),
+            pltpu.VMEM((length, 3 * width // 2), BF16),
             pltpu.VMEM((width, 3 * width), BF16),
             pltpu.VMEM((length, width), F32),
-            pltpu.SemaphoreType.DMA((width // TILE,)),
+            pltpu.SemaphoreType.DMA((width // TILE + 4,)),
         ],
         compiler_params=params(),
         cost_estimate=cost(6),
     )(gain_t[None], returned, rows, low_grads, high_grads, w_qkv_t)
-    reduced = travelling.astype(F32) + arriving.astype(F32) + term[0].astype(F32)
-    reduced = reduced.astype(BF16)
-    reduced = (reduced.astype(F32) + swap_chip(reduced).astype(F32)).astype(BF16)
+    reduced = travelling.astype(F32) + crossing.astype(F32)
+    reduced = (reduced + near_sum.astype(F32) + far_sum.astype(F32)).astype(BF16)
     reduced, values, input_grad = lax.optimization_barrier((reduced, values, input_grad))
     other = swap_core(reduced)
     qkv_grad, out_grad = pl.pallas_call(

time: 121 us -> 118 us (0.975)
  Pallas kernels: 41.8 us -> 39.6 us
  waiting for transfers between devices: 30.3 us -> 28.3 us
    ppermute x0 -> x1, starting transfers between devices: none -> 3.26 us  [ring_other_chip(): return lax.ppermute(block, ('env', 'tm'), pairs)]
    pallas_call x2, Pallas kernels: 10.7 us -> 8.94 us  [mix_grad(): pl.pallas_call(functools.partial(mix_grad_kernel, first_head), name='temp...]
    ppermute x9, starting transfers between devices: 19.1 us -> 17.6 us  [ring(): return lax.ppermute(block, ('env', 'tm'), pairs)]
  transfers between devices with their start and end apart: 26 -> 27, of which waited for: 10 -> 12; matrix products, arithmetic and copies ran while one was open for 3% -> 3% of each run, Pallas kernels for 23% -> 21%
where the time goes in v5:
time: 118 us; the launch traced here: 117 us
  starting transfers between devices  40.9 us (35%)
  Pallas kernels  39.6 us (34%)
  waiting for transfers between devices  28.3 us (24%)
  local copies, waits for them, and re-layouts  6.17 us (5%)
  between operations  1.56 us (1%)
    ppermute x9, starting transfers between devices, ring(): return lax.ppermute(block, ('env', 'tm'), pairs)  17.6 us
    ppermute x6, waiting for transfers between devices, swap_chip(): return lax.ppermute(block, 'env', [(at, at ^ 2) for at in range(env_count)])  16.9 us
    pallas_call x1, Pallas kernels, per_device(): pl.pallas_call(functools.partial(agent_kernel, tm_count - 1, group_steps)...  10.9 us
    pallas_call x2, Pallas kernels, mix_grad(): pl.pallas_call(functools.partial(mix_grad_kernel, first_head), name='temp...  8.94 us
    pallas_call x1, Pallas kernels, per_device(): pl.pallas_call(temporal_forward, name='temporal_forward', out_shape=(jax....  7.9 us
    ppermute x6, starting transfers between devices, swap_chip(): return lax.ppermute(block, 'env', [(at, at ^ 2) for at in range(env_count)])  6.8 us
    pallas_call x1, Pallas kernels, per_device(): pl.pallas_call(norm_grad_kernel, name='temporal_norm_grad', out_shape=jax...  6.29 us
    all_to_all x1, starting transfers between devices, per_device(): lifted = lax.all_to_all(h1, 'tm', split_axis=0, concat_axis=0, tiled=True)  5.84 us
  transfers between devices with their start and end apart: 27, of which 12 were waited for; matrix products, arithmetic and copies ran while one was open for 3% of the time, Pallas kernels for 21%

profile of v5, /device:TPU:0, one launch (start us, length us, event | category | flops | bytes accessed | tf_op | source)
XLA Modules:
  0.0 117.0 jit_solution(12662863172866590070)
XLA Ops:
  0.6 2.0 %pack_block.1.own_ref = bf16[128,1664]{1,0:T(8,128)(2,1)} custom-call(s32[1]{0:T(128)} %bitcast.env_ref, bf16[128,3072]{1,0:T(8,128)(2,1)} %shard_ref.1, bf16[128,3072]{1,0:T(8,128)(2,1)} %shard_ref.1, bf16[128,1024]{1,0:T(8,128)(2,1)} %w_out_ref.1, f32[1,1024]{1,0:T(1,128)} %bitcast.20), custom_call_target="tpu_custom_call" | custom-call | flops 2000000000 | bytes 4000000 | tf_op jit(solution)/shard_map/pack_block/pallas_call | solution.py:526
  2.6 3.0 %collective-permute-start = (bf16[128,1664]{1,0:T(8,128)(2,1)}, bf16[128,1664]{1,0:T(8,128)(2,1)S(1)}, u32[]{:S(2)}, u32[]{:S(2)}) collective-permute-start(bf16[128,1664]{1,0:T(8,128)(2,1)} %pack_block.1.own_ref), channel_id=1, source_target_pairs={{0,2},{1,0},{2,4},{3,1},{4,6},{5,3},{6,7},{7,5},{8,9},{9,11},{10,8... | collective-permute-start | bytes 1277960 | tf_op jit(solution)/shard_map/ppermute | solution.py:506
  6.3 7.9 %temporal_forward.1 = (bf16[256,1024]{1,0:T(8,128)(2,1)}, bf16[256,3072]{1,0:T(8,128)(2,1)}, bf16[8,256,256]{2,1,0:T(8,128)(2,1)}) custom-call(s32[1]{0:T(128)} %bitcast.19.done_ref, bf16[256,1024]{1,0:T(8,128)(2,1)} %bitcast.29, f32[1,1024]{1,0:T(1,128)} %bitcast.32, bf16[1024,3072]{1,0:T(8,128)(2,1)} %w_hbm.5, bf16[1024,1024]{1,0:T(8,128)(2,1)} %w_hbm.4), custom_call_target="tpu_custom_call" | custom-call | flops 8000000000 | bytes 16000000 | tf_op jit(solution)/shard_map/temporal_forward/pallas_call | solution.py:547
  16.3 5.8 %all-to-all-start = ((bf16[8,32,1024]{2,1,0:T(8,128)(2,1)}), bf16[8,32,1024]{2,1,0:T(8,128)(2,1)S(1)}, u32[]{:S(2)}, u32[]{:S(2)}) async-start(bf16[8,32,1024]{2,1,0:T(8,128)(2,1)} %bitcast.25), calls=%async_computation | async-start | bytes 1048576 | tf_op jit(solution)/shard_map/all_to_all | solution.py:570
  22.1 3.4 %collective-permute-done.2.rest_4_ = bf16[128,1664]{1,0:T(8,128)(2,1)S(1)} collective-permute-done((bf16[128,1664]{1,0:T(8,128)(2,1)S(1)}, bf16[128,1664]{1,0:T(8,128)(2,1)S(1)}, u32[]{:S(2)}, u32[]{:S(2)}) %collective-permute-start.2) | collective-permute-done | bytes 426016 | tf_op jit(solution)/shard_map/ppermute | solution.py:520
  25.6 1.6 %collective-permute-start.4 = (bf16[128,1664]{1,0:T(8,128)(2,1)S(1)}, bf16[128,1664]{1,0:T(8,128)(2,1)S(1)}, u32[]{:S(2)}, u32[]{:S(2)}) collective-permute-start(bf16[128,1664]{1,0:T(8,128)(2,1)S(1)} %collective-permute-done.1.rest_1_), channel_id=1, source_target_pairs={{0,16},{8,24},{16,0},{24,8},{1,17},{9,25},{17,1},{25,9},{2,18},{10... | collective-permute-start | bytes 1277960 | tf_op jit(solution)/shard_map/ppermute | solution.py:520
  27.2 1.6 %collective-permute-start.3 = (bf16[128,1664]{1,0:T(8,128)(2,1)S(1)}, bf16[128,1664]{1,0:T(8,128)(2,1)S(1)}, u32[]{:S(2)}, u32[]{:S(2)}) collective-permute-start(bf16[128,1664]{1,0:T(8,128)(2,1)S(1)} %collective-permute-done.1.rest_1_), channel_id=1, source_target_pairs={{0,2},{1,0},{2,4},{3,1},{4,6},{5,3},{6,7},{7,5},{8,9},{9,11},{10,8... | collective-permute-start | bytes 1277960 | tf_op jit(solution)/shard_map/ppermute | solution.py:506
  29.3 6.7 %collective-permute-done.4.rest_5_ = bf16[128,1664]{1,0:T(8,128)(2,1)S(1)} collective-permute-done((bf16[128,1664]{1,0:T(8,128)(2,1)S(1)}, bf16[128,1664]{1,0:T(8,128)(2,1)S(1)}, u32[]{:S(2)}, u32[]{:S(2)}) %collective-permute-start.4) | collective-permute-done | bytes 426016 | tf_op jit(solution)/shard_map/ppermute | solution.py:520
  38.2 3.8 %collective-permute-start.5 = (bf16[128,1664]{1,0:T(8,128)(2,1)S(1)}, bf16[128,1664]{1,0:T(8,128)(2,1)}, u32[]{:S(2)}, u32[]{:S(2)}) collective-permute-start(bf16[128,1664]{1,0:T(8,128)(2,1)S(1)} %collective-permute-done.3.rest_2_), channel_id=1, source_target_pairs={{0,2},{1,0},{2,4},{3,1},{4,6},{5,3},{6,7},{7,5},{8,9},{9,11},{10,8... | collective-permute-start | bytes 1277960 | tf_op jit(solution)/shard_map/ppermute | solution.py:506
  42.7 6.6 %collective-permute-done.6.rest_6_ = bf16[128,1664]{1,0:T(8,128)(2,1)} collective-permute-done((bf16[128,1664]{1,0:T(8,128)(2,1)S(1)}, bf16[128,1664]{1,0:T(8,128)(2,1)}, u32[]{:S(2)}, u32[]{:S(2)}) %collective-permute-start.6) | collective-permute-done | bytes 426016 | tf_op jit(solution)/shard_map/ppermute | solution.py:520
  52.1 10.9 %agent_block.1 = (bf16[256,1024]{1,0:T(8,128)(2,1)}, bf16[512,1024]{1,0:T(8,128)(2,1)}, bf16[256,1024]{1,0:T(8,128)(2,1)}, bf16[1024,128]{1,0:T(8,128)(2,1)}, f32[1,1024]{1,0:T(1,128)}, /*index=5*/f32[2,8,128]{2,1,0:T(8,128)}) custom-call(s32[1]{0:T(128)} %bitcast.env_ref, s32[1]{0:T(128)} %bitcast.1.tm_ref, bf16[256,1024]{1,0:T(8,128)(2,1)} %bitcast.23, ...), custom_call_target="tpu_custom_call" | custom-call | flops 11000000512 | bytes 22000000 | tf_op jit(solution)/shard_map/agent_block/pallas_call | solution.py:594
  63.2 5.5 %all-to-all-start.1 = ((bf16[8,32,1024]{2,1,0:T(8,128)(2,1)}), bf16[8,32,1024]{2,1,0:T(8,128)(2,1)}, u32[]{:S(2)}, u32[]{:S(2)}) async-start(bf16[8,32,1024]{2,1,0:T(8,128)(2,1)} %bitcast.24), calls=%async_computation.1 | async-start | bytes 1048576 | tf_op jit(solution)/shard_map/all_to_all | solution.py:626
  71.9 1.9 %weight_grad.1 = (bf16[128,1152]{1,0:T(8,128)(2,1)S(1)}, bf16[128,1152]{1,0:T(8,128)(2,1)S(1)}, bf16[128,1152]{1,0:T(8,128)(2,1)S(1)}, bf16[128,1152]{1,0:T(8,12...) custom-call(s32[1]{0:T(128)} %bitcast.env_ref, ...), custom_call_target="tpu_custom_call" | custom-call | flops 4000000000 | bytes 8000000 | tf_op jit(solution)/shard_map/weight_grad/pallas_call | solution.py:630
  73.8 2.1 %collective-permute-start.15 = (bf16[128,1152]{1,0:T(8,128)(2,1)S(1)}, bf16[128,1152]{1,0:T(8,128)(2,1)S(1)}, u32[]{:S(2)}, u32[]{:S(2)}) collective-permute-start(bf16[128,1152]{1,0:T(8,128)(2,1)S(1)} %get-tuple-element.54), channel_id=1, source_target_pairs={{0,2},{1,0},{2,4},{3,1},{4,6},{5,3},{6,7},{7,5},{8,9},{9,11},{10,8... | collective-permute-start | bytes 884744 | tf_op jit(solution)/shard_map/ppermute | solution.py:506
  79.5 5.2 %all-to-all-done.1 = bf16[8,32,1024]{2,1,0:T(8,128)(2,1)} async-done(((bf16[8,32,1024]{2,1,0:T(8,128)(2,1)}), bf16[8,32,1024]{2,1,0:T(8,128)(2,1)}, u32[]{:S(2)}, u32[]{:S(2)}) %all-to-all-start.1) | async-done | bytes 524320 | tf_op jit(solution)/shard_map/all_to_all | solution.py:626
  84.9 2.0 %collective-permute-done.16 = bf16[128,1152]{1,0:T(8,128)(2,1)S(1)} collective-permute-done((bf16[128,1152]{1,0:T(8,128)(2,1)S(1)}, bf16[128,1152]{1,0:T(8,128)(2,1)S(1)}, u32[]{:S(2)}, u32[]{:S(2)}) %collective-permute-start.16) | collective-permute-done | bytes 294944 | tf_op jit(solution)/shard_map/ppermute | solution.py:506
  87.4 3.9 %collective-permute-start.18 = (bf16[128,1152]{1,0:T(8,128)(2,1)S(1)}, bf16[128,1152]{1,0:T(8,128)(2,1)S(1)}, u32[]{:S(2)}, u32[]{:S(2)}) collective-permute-start(bf16[128,1152]{1,0:T(8,128)(2,1)S(1)} %add_convert_fusion.4), channel_id=1, source_target_pairs={{0,2},{1,0},{2,4},{3,1},{4,6},{5,3},{6,7},{7,5},{8,9},{9,11},{10,8... | collective-permute-start | bytes 884744 | tf_op jit(solution)/shard_map/ppermute | solution.py:506
  91.4 4.5 %temporal_mix_grad.2.low_hbm = bf16[256,1536]{1,0:T(8,128)(2,1)} custom-call(bf16[256,1024]{1,0:T(8,128)(2,1)} %bitcast.12.grad_hbm, bf16[1024,1024]{1,0:T(8,128)(2,1)} %w_hbm.4, bf16[256,3072]{1,0:T(8,128)(2,1)} %get-tuple-element.61.qkv_hbm, bf16[8,256,256]{2,1,0:T(8,128)(2,1)} %get-tuple-element.62.probs_hbm), custom_call_target="tpu_custom_call" | custom-call | flops 4000000000 | bytes 8000000 | tf_op jit(solution)/shard_map/temporal_mix_grad/pallas_call | solution.py:645
  96.0 2.3 %collective-permute-start.20 = (bf16[128,1152]{1,0:T(8,128)(2,1)S(1)}, bf16[128,1152]{1,0:T(8,128)(2,1)S(1)}, u32[]{:S(2)}, u32[]{:S(2)}) collective-permute-start(bf16[128,1152]{1,0:T(8,128)(2,1)S(1)} %add_convert_fusion.3), channel_id=1, source_target_pairs={{0,2},{1,0},{2,4},{3,1},{4,6},{5,3},{6,7},{7,5},{8,9},{9,11},{10,8... | collective-permute-start | bytes 884744 | tf_op jit(solution)/shard_map/ppermute | solution.py:506
  98.3 4.5 %temporal_mix_grad.3.high_hbm = bf16[256,1536]{1,0:T(8,128)(2,1)} custom-call(bf16[256,1024]{1,0:T(8,128)(2,1)} %bitcast.12.grad_hbm, bf16[1024,1024]{1,0:T(8,128)(2,1)} %w_hbm.4, bf16[256,3072]{1,0:T(8,128)(2,1)} %get-tuple-element.61.qkv_hbm, bf16[8,256,256]{2,1,0:T(8,128)(2,1)} %get-tuple-element.62.probs_hbm), custom_call_target="tpu_custom_call" | custom-call | flops 4000000000 | bytes 8000000 | tf_op jit(solution)/shard_map/temporal_mix_grad/pallas_call | solution.py:645
  102.9 3.3 %collective-permute-start.23 = (bf16[128,1152]{1,0:T(8,128)(2,1)S(1)}, bf16[128,1152]{1,0:T(8,128)(2,1)S(1)}, u32[]{:S(2)}, u32[]{:S(2)}) collective-permute-start(bf16[128,1152]{1,0:T(8,128)(2,1)S(1)} %add_convert_fusion.1), channel_id=1, source_target_pairs={{0,18},{1,16},{2,20},{3,17},{4,22},{5,19},{6,23},{7,21},{8,25},{9,... | collective-permute-start | bytes 884744 | tf_op jit(solution)/shard_map/ppermute | solution.py:514
  106.5 6.3 %temporal_norm_grad.1 = bf16[256,1024]{1,0:T(8,128)(2,1)} custom-call(f32[1,1024]{1,0:T(1,128)} %bitcast.33, bf16[256,1024]{1,0:T(8,128)(2,1)} %bitcast.12.grad_hbm, bf16[256,1024]{1,0:T(8,128)(2,1)} %bitcast.30, bf16[256,1536]{1,0:T(8,128)(2,1)} %temporal_mix_grad.2.low_hbm, bf16[256,1536]{1,0:T(8,128)(2,1)} %temporal_mix_grad.3.high_hbm, ...), custom_call_target="tpu_custom_call" | custom-call | flops 6000000000 | bytes 12000000 | tf_op jit(solution)/shard_map/temporal_norm_grad/pallas_call | solution.py:687
  113.9 1.6 %collective-permute-done.24.other_ref = bf16[128,1152]{1,0:T(8,128)(2,1)S(1)} collective-permute-done((bf16[128,1152]{1,0:T(8,128)(2,1)S(1)}, bf16[128,1152]{1,0:T(8,128)(2,1)S(1)}, u32[]{:S(2)}, u32[]{:S(2)}) %collective-permute-start.24) | collective-permute-done | bytes 294944 | tf_op jit(solution)/shard_map/ppermute | solution.py:517
  115.4 1.6 %finish.1 = (f32[128,3072]{1,0:T(8,128)}, f32[128,1024]{1,0:T(8,128)}) custom-call(s32[1]{0:T(128)} %bitcast.env_ref, bf16[128,1152]{1,0:T(8,128)(2,1)S(1)} %add_convert_fusion.own_ref, bf16[128,1152]{1,0:T(8,128)(2,1)S(1)} %collective-permute-done.24.other_ref, f32[1,1024]{1,0:T(1,128)S(1)} %copy-done.4, f32[1,1024]{1,0:T(1,128)S(1)} %bitcast.22), custom_call_target="tpu_custom_call" | custom-call | flops 2000000000 | bytes 4000000 | tf_op jit(solution)/shard_map/finish/pallas_call | solution.py:709
  (84 shorter events, 17.4 us)
Async XLA Ops:
  2.6 11.6 %collective-permute-start = (bf16[128,1664]{1,0:T(8,128)(2,1)}, bf16[128,1664]{1,0:T(8,128)(2,1)S(1)}, u32[]{:S(2)}, u32[]{:S(2)}) collective-permute-start(bf16[128,1664]{1,0:T(8,128)(2,1)} %pack_block.1.own_ref), channel_id=1, source_target_pairs={{0,2},{1,0},{2,4},{3,1},{4,6},{5,3},{6,7},{7,5},{8,9},{9,11},{10,8... | collective-permute-start | bytes 1277960 | tf_op jit(solution)/shard_map/ppermute | solution.py:506
  14.3 11.3 %collective-permute-start.2 = (bf16[128,1664]{1,0:T(8,128)(2,1)S(1)}, bf16[128,1664]{1,0:T(8,128)(2,1)S(1)}, u32[]{:S(2)}, u32[]{:S(2)}) collective-permute-start(bf16[128,1664]{1,0:T(8,128)(2,1)S(1)} %collective-permute-done.rest_0_), channel_id=1, source_target_pairs={{0,16},{8,24},{16,0},{24,8},{1,17},{9,25},{17,1},{25,9},{2,18},{10... | collective-permute-start | bytes 1277960 | tf_op jit(solution)/shard_map/ppermute | solution.py:520
  15.8 9.8 %collective-permute-start.1 = (bf16[128,1664]{1,0:T(8,128)(2,1)S(1)}, bf16[128,1664]{1,0:T(8,128)(2,1)S(1)}, u32[]{:S(2)}, u32[]{:S(2)}) collective-permute-start(bf16[128,1664]{1,0:T(8,128)(2,1)S(1)} %collective-permute-done.rest_0_), channel_id=1, source_target_pairs={{0,2},{1,0},{2,4},{3,1},{4,6},{5,3},{6,7},{7,5},{8,9},{9,11},{10,8... | collective-permute-start | bytes 1277960 | tf_op jit(solution)/shard_map/ppermute | solution.py:506
  16.3 25.7 %all-to-all-start = ((bf16[8,32,1024]{2,1,0:T(8,128)(2,1)}), bf16[8,32,1024]{2,1,0:T(8,128)(2,1)S(1)}, u32[]{:S(2)}, u32[]{:S(2)}) async-start(bf16[8,32,1024]{2,1,0:T(8,128)(2,1)} %bitcast.25), calls=%async_computation | async-start | bytes 1048576 | tf_op jit(solution)/shard_map/all_to_all | solution.py:570
  25.6 10.4 %collective-permute-start.4 = (bf16[128,1664]{1,0:T(8,128)(2,1)S(1)}, bf16[128,1664]{1,0:T(8,128)(2,1)S(1)}, u32[]{:S(2)}, u32[]{:S(2)}) collective-permute-start(bf16[128,1664]{1,0:T(8,128)(2,1)S(1)} %collective-permute-done.1.rest_1_), channel_id=1, source_target_pairs={{0,16},{8,24},{16,0},{24,8},{1,17},{9,25},{17,1},{25,9},{2,18},{10... | collective-permute-start | bytes 1277960 | tf_op jit(solution)/shard_map/ppermute | solution.py:520
  27.2 9.5 %collective-permute-start.3 = (bf16[128,1664]{1,0:T(8,128)(2,1)S(1)}, bf16[128,1664]{1,0:T(8,128)(2,1)S(1)}, u32[]{:S(2)}, u32[]{:S(2)}) collective-permute-start(bf16[128,1664]{1,0:T(8,128)(2,1)S(1)} %collective-permute-done.1.rest_1_), channel_id=1, source_target_pairs={{0,2},{1,0},{2,4},{3,1},{4,6},{5,3},{6,7},{7,5},{8,9},{9,11},{10,8... | collective-permute-start | bytes 1277960 | tf_op jit(solution)/shard_map/ppermute | solution.py:506
  28.8 13.2 %collective-permute-start.7 = (bf16[128,1664]{1,0:T(8,128)(2,1)S(1)}, bf16[128,1664]{1,0:T(8,128)(2,1)S(1)}, u32[]{:S(2)}, u32[]{:S(2)}) collective-permute-start(bf16[128,1664]{1,0:T(8,128)(2,1)S(1)} %collective-permute-done.rest_0_), channel_id=1, source_target_pairs={{0,8},{8,0},{16,24},{24,16},{1,9},{9,1},{17,25},{25,17},{2,10},{10... | collective-permute-start | bytes 1277960 | tf_op jit(solution)/shard_map/ppermute | solution.py:517
  28.8 13.8 %collective-permute-start.11 = (bf16[128,1664]{1,0:T(8,128)(2,1)S(1)}, bf16[128,1664]{1,0:T(8,128)(2,1)S(1)}, u32[]{:S(2)}, u32[]{:S(2)}) collective-permute-start(bf16[128,1664]{1,0:T(8,128)(2,1)S(1)} %collective-permute-done.2.rest_4_), channel_id=1, source_target_pairs={{0,8},{8,0},{16,24},{24,16},{1,9},{9,1},{17,25},{25,17},{2,10},{10... | collective-permute-start | bytes 1277960 | tf_op jit(solution)/shard_map/ppermute | solution.py:517
  36.7 12.6 %collective-permute-start.6 = (bf16[128,1664]{1,0:T(8,128)(2,1)S(1)}, bf16[128,1664]{1,0:T(8,128)(2,1)}, u32[]{:S(2)}, u32[]{:S(2)}) collective-permute-start(bf16[128,1664]{1,0:T(8,128)(2,1)S(1)} %collective-permute-done.3.rest_2_), channel_id=1, source_target_pairs={{0,16},{8,24},{16,0},{24,8},{1,17},{9,25},{17,1},{25,9},{2,18},{10... | collective-permute-start | bytes 1277960 | tf_op jit(solution)/shard_map/ppermute | solution.py:520
  38.2 11.1 %collective-permute-start.5 = (bf16[128,1664]{1,0:T(8,128)(2,1)S(1)}, bf16[128,1664]{1,0:T(8,128)(2,1)}, u32[]{:S(2)}, u32[]{:S(2)}) collective-permute-start(bf16[128,1664]{1,0:T(8,128)(2,1)S(1)} %collective-permute-done.3.rest_2_), channel_id=1, source_target_pairs={{0,2},{1,0},{2,4},{3,1},{4,6},{5,3},{6,7},{7,5},{8,9},{9,11},{10,8... | collective-permute-start | bytes 1277960 | tf_op jit(solution)/shard_map/ppermute | solution.py:506
  42.0 9.3 %collective-permute-start.8 = (bf16[128,1664]{1,0:T(8,128)(2,1)S(1)}, bf16[128,1664]{1,0:T(8,128)(2,1)}, u32[]{:S(2)}, u32[]{:S(2)}) collective-permute-start(bf16[128,1664]{1,0:T(8,128)(2,1)S(1)} %collective-permute-done.1.rest_1_), channel_id=1, source_target_pairs={{0,8},{8,0},{16,24},{24,16},{1,9},{9,1},{17,25},{25,17},{2,10},{10... | collective-permute-start | bytes 1277960 | tf_op jit(solution)/shard_map/ppermute | solution.py:517
  42.0 9.2 %collective-permute-start.9 = (bf16[128,1664]{1,0:T(8,128)(2,1)S(1)}, bf16[128,1664]{1,0:T(8,128)(2,1)}, u32[]{:S(2)}, u32[]{:S(2)}) collective-permute-start(bf16[128,1664]{1,0:T(8,128)(2,1)S(1)} %collective-permute-done.3.rest_2_), channel_id=1, source_target_pairs={{0,8},{8,0},{16,24},{24,16},{1,9},{9,1},{17,25},{25,17},{2,10},{10... | collective-permute-start | bytes 1277960 | tf_op jit(solution)/shard_map/ppermute | solution.py:517
  42.6 8.7 %collective-permute-start.12 = (bf16[128,1664]{1,0:T(8,128)(2,1)S(1)}, bf16[128,1664]{1,0:T(8,128)(2,1)}, u32[]{:S(2)}, u32[]{:S(2)}) collective-permute-start(bf16[128,1664]{1,0:T(8,128)(2,1)S(1)} %collective-permute-done.4.rest_5_), channel_id=1, source_target_pairs={{0,8},{8,0},{16,24},{24,16},{1,9},{9,1},{17,25},{25,17},{2,10},{10... | collective-permute-start | bytes 1277960 | tf_op jit(solution)/shard_map/ppermute | solution.py:517
  63.0 5.7 %collective-permute-start.14 = (bf16[512,1024]{1,0:T(8,128)(2,1)}, bf16[512,1024]{1,0:T(8,128)(2,1)S(1)}, u32[]{:S(2)}, u32[]{:S(2)}) collective-permute-start(bf16[512,1024]{1,0:T(8,128)(2,1)} %get-tuple-element.51.pack_ref), channel_id=1, source_target_pairs={{0,8},{8,0},{16,24},{24,16},{1,9},{9,1},{17,25},{25,17},{2,10},{10... | collective-permute-start | bytes 3145736 | tf_op jit(solution)/shard_map/ppermute | solution.py:517
  63.2 21.5 %all-to-all-start.1 = ((bf16[8,32,1024]{2,1,0:T(8,128)(2,1)}), bf16[8,32,1024]{2,1,0:T(8,128)(2,1)}, u32[]{:S(2)}, u32[]{:S(2)}) async-start(bf16[8,32,1024]{2,1,0:T(8,128)(2,1)} %bitcast.24), calls=%async_computation.1 | async-start | bytes 1048576 | tf_op jit(solution)/shard_map/all_to_all | solution.py:626
  73.8 11.1 %collective-permute-start.15 = (bf16[128,1152]{1,0:T(8,128)(2,1)S(1)}, bf16[128,1152]{1,0:T(8,128)(2,1)S(1)}, u32[]{:S(2)}, u32[]{:S(2)}) collective-permute-start(bf16[128,1152]{1,0:T(8,128)(2,1)S(1)} %get-tuple-element.54), channel_id=1, source_target_pairs={{0,2},{1,0},{2,4},{3,1},{4,6},{5,3},{6,7},{7,5},{8,9},{9,11},{10,8... | collective-permute-start | bytes 884744 | tf_op jit(solution)/shard_map/ppermute | solution.py:506
  76.0 10.9 %collective-permute-start.16 = (bf16[128,1152]{1,0:T(8,128)(2,1)S(1)}, bf16[128,1152]{1,0:T(8,128)(2,1)S(1)}, u32[]{:S(2)}, u32[]{:S(2)}) collective-permute-start(bf16[128,1152]{1,0:T(8,128)(2,1)S(1)} %get-tuple-element.56), channel_id=1, source_target_pairs={{0,1},{1,3},{2,0},{3,5},{4,2},{5,7},{6,4},{7,6},{8,10},{9,8},{10,1... | collective-permute-start | bytes 884744 | tf_op jit(solution)/shard_map/ppermute | solution.py:506
  77.5 9.9 %collective-permute-start.17 = (bf16[128,1152]{1,0:T(8,128)(2,1)S(1)}, bf16[128,1152]{1,0:T(8,128)(2,1)S(1)}, u32[]{:S(2)}, u32[]{:S(2)}) collective-permute-start(bf16[128,1152]{1,0:T(8,128)(2,1)S(1)} %get-tuple-element.59), channel_id=1, source_target_pairs={{0,16},{8,24},{16,0},{24,8},{1,17},{9,25},{17,1},{25,9},{2,18},{10... | collective-permute-start | bytes 884744 | tf_op jit(solution)/shard_map/ppermute | solution.py:520
  77.9 17.9 %collective-permute-start.19 = (bf16[128,1152]{1,0:T(8,128)(2,1)S(1)}, bf16[128,1152]{1,0:T(8,128)(2,1)S(1)}, u32[]{:S(2)}, u32[]{:S(2)}) collective-permute-start(bf16[128,1152]{1,0:T(8,128)(2,1)S(1)} %get-tuple-element.65), channel_id=1, source_target_pairs={{0,16},{8,24},{16,0},{24,8},{1,17},{9,25},{17,1},{25,9},{2,18},{10... | collective-permute-start | bytes 884744 | tf_op jit(solution)/shard_map/ppermute | solution.py:520
  87.0 15.8 %collective-permute-start.21 = (bf16[128,1152]{1,0:T(8,128)(2,1)S(1)}, bf16[128,1152]{1,0:T(8,128)(2,1)S(1)}, u32[]{:S(2)}, u32[]{:S(2)}) collective-permute-start(bf16[128,1152]{1,0:T(8,128)(2,1)S(1)} %add_convert_fusion.2), channel_id=1, source_target_pairs={{0,16},{8,24},{16,0},{24,8},{1,17},{9,25},{17,1},{25,9},{2,18},{10... | collective-permute-start | bytes 884744 | tf_op jit(solution)/shard_map/ppermute | solution.py:520
  87.4 8.4 %collective-permute-start.18 = (bf16[128,1152]{1,0:T(8,128)(2,1)S(1)}, bf16[128,1152]{1,0:T(8,128)(2,1)S(1)}, u32[]{:S(2)}, u32[]{:S(2)}) collective-permute-start(bf16[128,1152]{1,0:T(8,128)(2,1)S(1)} %add_convert_fusion.4), channel_id=1, source_target_pairs={{0,2},{1,0},{2,4},{3,1},{4,6},{5,3},{6,7},{7,5},{8,9},{9,11},{10,8... | collective-permute-start | bytes 884744 | tf_op jit(solution)/shard_map/ppermute | solution.py:506
  96.0 6.8 %collective-permute-start.20 = (bf16[128,1152]{1,0:T(8,128)(2,1)S(1)}, bf16[128,1152]{1,0:T(8,128)(2,1)S(1)}, u32[]{:S(2)}, u32[]{:S(2)}) collective-permute-start(bf16[128,1152]{1,0:T(8,128)(2,1)S(1)} %add_convert_fusion.3), channel_id=1, source_target_pairs={{0,2},{1,0},{2,4},{3,1},{4,6},{5,3},{6,7},{7,5},{8,9},{9,11},{10,8... | collective-permute-start | bytes 884744 | tf_op jit(solution)/shard_map/ppermute | solution.py:506
  102.9 9.9 %collective-permute-start.23 = (bf16[128,1152]{1,0:T(8,128)(2,1)S(1)}, bf16[128,1152]{1,0:T(8,128)(2,1)S(1)}, u32[]{:S(2)}, u32[]{:S(2)}) collective-permute-start(bf16[128,1152]{1,0:T(8,128)(2,1)S(1)} %add_convert_fusion.1), channel_id=1, source_target_pairs={{0,18},{1,16},{2,20},{3,17},{4,22},{5,19},{6,23},{7,21},{8,25},{9,... | collective-permute-start | bytes 884744 | tf_op jit(solution)/shard_map/ppermute | solution.py:514
  106.1 7.5 %collective-permute-start.22 = (bf16[128,1152]{1,0:T(8,128)(2,1)S(1)}, bf16[128,1152]{1,0:T(8,128)(2,1)S(1)}, u32[]{:S(2)}, u32[]{:S(2)}) collective-permute-start(bf16[128,1152]{1,0:T(8,128)(2,1)S(1)} %add_convert_fusion.1), channel_id=1, source_target_pairs={{0,2},{1,0},{2,4},{3,1},{4,6},{5,3},{6,7},{7,5},{8,9},{9,11},{10,8... | collective-permute-start | bytes 884744 | tf_op jit(solution)/shard_map/ppermute | solution.py:506
  (18 other events, 274.3 us)

commit v6 on v5

--- a/solution.py
+++ b/solution.py
@@ -222,11 +222,10 @@
 ):
     moved = rest[: 2 * blocks]
     grad_ref, pack_ref, keep_ref, extra_ref, u_ref, predicted_ref = rest[2 * blocks : 2 * blocks + 6]
-    w_all, qk, grad_qk, probs_all, slopes, column, grad_normed, sems = rest[2 * blocks + 6 :]
+    w_all, qk, grad_qk, probs_all, slopes, column, grad_normed, normed_ref, sems, out_sems = rest[2 * blocks + 6 :]
     total_rows, width = rows_ref.shape
     size = width // HEADS
     scale = 1.0 / math.sqrt(size)
-    normed_ref = pack_ref.at[pl.ds(0, total_rows), :]
     groups, group_rows = alive_ref.shape[0], alive_ref.shape[2]
     agents = group_rows // group_steps
     local_steps = total_rows // agents
@@ -296,6 +295,10 @@
             column[target, :] = jnp.broadcast_to(
                 jnp.sum(rows * value_ref[...], axis=-1, keepdims=True), (rows.shape[0], 128)
             )
+    normed_out = pltpu.make_async_copy(
+        normed_ref, pack_ref.at[pl.ds(0, total_rows), :], out_sems.at[0]
+    )
+    normed_out.start()
     for copy in copies:
         copy.wait()
 
@@ -363,6 +366,18 @@
                 jnp.sum(probs_all[group * HEADS + head] * error, axis=0, keepdims=True)
             )
         pulls.append(jnp.concatenate(pull_rows, axis=0))
+    grad_outs = [
+        pltpu.make_async_copy(
+            grad_qk.at[:, column_span(core * width, width)], keep_ref, out_sems.at[1]
+        ),
+        pltpu.make_async_copy(
+            grad_qk.at[:, column_span(other * width, width)],
+            pack_ref.at[pl.ds(total_rows, total_rows), :],
+            out_sems.at[2],
+        ),
+    ]
+    for out in grad_outs:
+        out.start()
     pull = jnp.concatenate(pulls, axis=1) if groups > 1 else pulls[0]
     pull = pull.astype(BF16)
     twice = jnp.concatenate([pull, pull], axis=0)
@@ -379,8 +394,6 @@
             pulled = norm_pull(rows, gain_ref[...], grad_normed[target, :])
             top = column[target, :1] * value_ref[...]
             grad_ref[source, :] = (top + pulled).astype(BF16)
-    keep_ref[...] = grad_qk[:, column_span(core * width, width)]
-    pack_ref[pl.ds(total_rows, total_rows), :] = grad_qk[:, column_span(other * width, width)]
 
     folded_grad = dot_nn(pull, normed_ref[...])
     folded_grad_low = folded_grad.astype(BF16)
@@ -394,6 +407,8 @@
         [folded_grad, pooled, jnp.zeros((127 - HEADS, width), F32)], axis=0
     )
     extra_ref[...] = jnp.transpose(extra).astype(BF16)
+    for out in [normed_out] + grad_outs:
+        out.wait()
 
 
 def weight_grad_kernel(hops, env_ref, tm_ref, pack_ref, keep_ref, moved_ref, extra_ref, *rest):
@@ -603,7 +618,7 @@
             jax.ShapeDtypeStruct((groups, 8, group_rows), F32),
         ),
         in_specs=[smem_spec()] * 2 + [vmem_spec()] * 5 + [hbm_spec()] * (2 * tm_count),
-        out_specs=[vmem_spec()] * 6,
+        out_specs=[vmem_spec()] + [hbm_spec()] * 2 + [vmem_spec()] * 3,
         scratch_shapes=[
             pltpu.VMEM((width, 2 * block_width), BF16),
             pltpu.VMEM((total_rows, 2 * width), BF16),
@@ -612,7 +627,9 @@
             pltpu.VMEM((groups * HEADS, group_rows, group_rows), F32),
             pltpu.VMEM((total_rows, 128), F32),
             pltpu.VMEM((total_rows, width), F32),
+            pltpu.VMEM((total_rows, width), BF16),
             pltpu.SemaphoreType.DMA((2 * tm_count + 2,)),
+            pltpu.SemaphoreType.DMA((3,)),
         ],
         compiler_params=params(),
         cost_estimate=cost(11),

time: 118 us -> 118 us (level)
  no operation moved by 1% of the time
where the time goes in v6:
time: 118 us; the launch traced here: 117 us
  starting transfers between devices  41 us (35%)
  Pallas kernels  39.7 us (34%)
  waiting for transfers between devices  28.3 us (24%)
  local copies, waits for them, and re-layouts  6.17 us (5%)
  between operations  1.56 us (1%)
    ppermute x9, starting transfers between devices, ring(): return lax.ppermute(block, ('env', 'tm'), pairs)  17.6 us
    ppermute x6, waiting for transfers between devices, swap_chip(): return lax.ppermute(block, 'env', [(at, at ^ 2) for at in range(env_count)])  16.9 us
    pallas_call x1, Pallas kernels, per_device(): pl.pallas_call(functools.partial(agent_kernel, tm_count - 1, group_steps)...  11.1 us
    pallas_call x2, Pallas kernels, mix_grad(): pl.pallas_call(functools.partial(mix_grad_kernel, first_head), name='temp...  8.92 us
    pallas_call x1, Pallas kernels, per_device(): pl.pallas_call(temporal_forward, name='temporal_forward', out_shape=(jax....  7.9 us
    ppermute x6, starting transfers between devices, swap_chip(): return lax.ppermute(block, 'env', [(at, at ^ 2) for at in range(env_count)])  6.8 us
    pallas_call x1, Pallas kernels, per_device(): pl.pallas_call(norm_grad_kernel, name='temporal_norm_grad', out_shape=jax...  6.29 us
    all_to_all x1, starting transfers between devices, per_device(): lifted = lax.all_to_all(h1, 'tm', split_axis=0, concat_axis=0, tiled=True)  5.84 us
  transfers between devices with their start and end apart: 27, of which 12 were waited for; matrix products, arithmetic and copies ran while one was open for 3% of the time, Pallas kernels for 21%

profile of v6, /device:TPU:0, one launch (start us, length us, event | category | flops | bytes accessed | tf_op | source)
XLA Modules:
  0.0 117.2 jit_solution(9957627412292928489)
XLA Ops:
  0.6 2.0 %pack_block.1.own_ref = bf16[128,1664]{1,0:T(8,128)(2,1)} custom-call(s32[1]{0:T(128)} %bitcast.env_ref, bf16[128,3072]{1,0:T(8,128)(2,1)} %shard_ref.1, bf16[128,3072]{1,0:T(8,128)(2,1)} %shard_ref.1, bf16[128,1024]{1,0:T(8,128)(2,1)} %w_out_ref.1, f32[1,1024]{1,0:T(1,128)} %bitcast.20), custom_call_target="tpu_custom_call" | custom-call | flops 2000000000 | bytes 4000000 | tf_op jit(solution)/shard_map/pack_block/pallas_call | solution.py:541
  2.6 3.0 %collective-permute-start = (bf16[128,1664]{1,0:T(8,128)(2,1)}, bf16[128,1664]{1,0:T(8,128)(2,1)S(1)}, u32[]{:S(2)}, u32[]{:S(2)}) collective-permute-start(bf16[128,1664]{1,0:T(8,128)(2,1)} %pack_block.1.own_ref), channel_id=1, source_target_pairs={{0,2},{1,0},{2,4},{3,1},{4,6},{5,3},{6,7},{7,5},{8,9},{9,11},{10,8... | collective-permute-start | bytes 1277960 | tf_op jit(solution)/shard_map/ppermute | solution.py:521
  6.3 7.9 %temporal_forward.1 = (bf16[256,1024]{1,0:T(8,128)(2,1)}, bf16[256,3072]{1,0:T(8,128)(2,1)}, bf16[8,256,256]{2,1,0:T(8,128)(2,1)}) custom-call(s32[1]{0:T(128)} %bitcast.19.done_ref, bf16[256,1024]{1,0:T(8,128)(2,1)} %bitcast.29, f32[1,1024]{1,0:T(1,128)} %bitcast.32, bf16[1024,3072]{1,0:T(8,128)(2,1)} %w_hbm.5, bf16[1024,1024]{1,0:T(8,128)(2,1)} %w_hbm.4), custom_call_target="tpu_custom_call" | custom-call | flops 8000000000 | bytes 16000000 | tf_op jit(solution)/shard_map/temporal_forward/pallas_call | solution.py:562
  16.3 5.8 %all-to-all-start = ((bf16[8,32,1024]{2,1,0:T(8,128)(2,1)}), bf16[8,32,1024]{2,1,0:T(8,128)(2,1)S(1)}, u32[]{:S(2)}, u32[]{:S(2)}) async-start(bf16[8,32,1024]{2,1,0:T(8,128)(2,1)} %bitcast.25), calls=%async_computation | async-start | bytes 1048576 | tf_op jit(solution)/shard_map/all_to_all | solution.py:585
  22.1 3.4 %collective-permute-done.2.rest_4_ = bf16[128,1664]{1,0:T(8,128)(2,1)S(1)} collective-permute-done((bf16[128,1664]{1,0:T(8,128)(2,1)S(1)}, bf16[128,1664]{1,0:T(8,128)(2,1)S(1)}, u32[]{:S(2)}, u32[]{:S(2)}) %collective-permute-start.2) | collective-permute-done | bytes 426016 | tf_op jit(solution)/shard_map/ppermute | solution.py:535
  25.6 1.6 %collective-permute-start.4 = (bf16[128,1664]{1,0:T(8,128)(2,1)S(1)}, bf16[128,1664]{1,0:T(8,128)(2,1)S(1)}, u32[]{:S(2)}, u32[]{:S(2)}) collective-permute-start(bf16[128,1664]{1,0:T(8,128)(2,1)S(1)} %collective-permute-done.1.rest_1_), channel_id=1, source_target_pairs={{0,16},{8,24},{16,0},{24,8},{1,17},{9,25},{17,1},{25,9},{2,18},{10... | collective-permute-start | bytes 1277960 | tf_op jit(solution)/shard_map/ppermute | solution.py:535
  27.2 1.6 %collective-permute-start.3 = (bf16[128,1664]{1,0:T(8,128)(2,1)S(1)}, bf16[128,1664]{1,0:T(8,128)(2,1)S(1)}, u32[]{:S(2)}, u32[]{:S(2)}) collective-permute-start(bf16[128,1664]{1,0:T(8,128)(2,1)S(1)} %collective-permute-done.1.rest_1_), channel_id=1, source_target_pairs={{0,2},{1,0},{2,4},{3,1},{4,6},{5,3},{6,7},{7,5},{8,9},{9,11},{10,8... | collective-permute-start | bytes 1277960 | tf_op jit(solution)/shard_map/ppermute | solution.py:521
  29.3 6.7 %collective-permute-done.4.rest_5_ = bf16[128,1664]{1,0:T(8,128)(2,1)S(1)} collective-permute-done((bf16[128,1664]{1,0:T(8,128)(2,1)S(1)}, bf16[128,1664]{1,0:T(8,128)(2,1)S(1)}, u32[]{:S(2)}, u32[]{:S(2)}) %collective-permute-start.4) | collective-permute-done | bytes 426016 | tf_op jit(solution)/shard_map/ppermute | solution.py:535
  38.2 3.8 %collective-permute-start.5 = (bf16[128,1664]{1,0:T(8,128)(2,1)S(1)}, bf16[128,1664]{1,0:T(8,128)(2,1)}, u32[]{:S(2)}, u32[]{:S(2)}) collective-permute-start(bf16[128,1664]{1,0:T(8,128)(2,1)S(1)} %collective-permute-done.3.rest_2_), channel_id=1, source_target_pairs={{0,2},{1,0},{2,4},{3,1},{4,6},{5,3},{6,7},{7,5},{8,9},{9,11},{10,8... | collective-permute-start | bytes 1277960 | tf_op jit(solution)/shard_map/ppermute | solution.py:521
  42.7 6.6 %collective-permute-done.6.rest_6_ = bf16[128,1664]{1,0:T(8,128)(2,1)} collective-permute-done((bf16[128,1664]{1,0:T(8,128)(2,1)S(1)}, bf16[128,1664]{1,0:T(8,128)(2,1)}, u32[]{:S(2)}, u32[]{:S(2)}) %collective-permute-start.6) | collective-permute-done | bytes 426016 | tf_op jit(solution)/shard_map/ppermute | solution.py:535
  52.1 11.1 %agent_block.1 = (bf16[256,1024]{1,0:T(8,128)(2,1)}, bf16[512,1024]{1,0:T(8,128)(2,1)}, bf16[256,1024]{1,0:T(8,128)(2,1)}, bf16[1024,128]{1,0:T(8,128)(2,1)}, f32[1,1024]{1,0:T(1,128)}, /*index=5*/f32[2,8,128]{2,1,0:T(8,128)}) custom-call(s32[1]{0:T(128)} %bitcast.env_ref, s32[1]{0:T(128)} %bitcast.1.tm_ref, bf16[256,1024]{1,0:T(8,128)(2,1)} %bitcast.23, ...), custom_call_target="tpu_custom_call" | custom-call | flops 11000000512 | bytes 22000000 | tf_op jit(solution)/shard_map/agent_block/pallas_call | solution.py:609
  63.4 5.5 %all-to-all-start.1 = ((bf16[8,32,1024]{2,1,0:T(8,128)(2,1)}), bf16[8,32,1024]{2,1,0:T(8,128)(2,1)}, u32[]{:S(2)}, u32[]{:S(2)}) async-start(bf16[8,32,1024]{2,1,0:T(8,128)(2,1)} %bitcast.24), calls=%async_computation.1 | async-start | bytes 1048576 | tf_op jit(solution)/shard_map/all_to_all | solution.py:643
  72.1 1.9 %weight_grad.1 = (bf16[128,1152]{1,0:T(8,128)(2,1)S(1)}, bf16[128,1152]{1,0:T(8,128)(2,1)S(1)}, bf16[128,1152]{1,0:T(8,128)(2,1)S(1)}, bf16[128,1152]{1,0:T(8,12...) custom-call(s32[1]{0:T(128)} %bitcast.env_ref, ...), custom_call_target="tpu_custom_call" | custom-call | flops 4000000000 | bytes 8000000 | tf_op jit(solution)/shard_map/weight_grad/pallas_call | solution.py:647
  74.0 2.1 %collective-permute-start.15 = (bf16[128,1152]{1,0:T(8,128)(2,1)S(1)}, bf16[128,1152]{1,0:T(8,128)(2,1)S(1)}, u32[]{:S(2)}, u32[]{:S(2)}) collective-permute-start(bf16[128,1152]{1,0:T(8,128)(2,1)S(1)} %get-tuple-element.54), channel_id=1, source_target_pairs={{0,2},{1,0},{2,4},{3,1},{4,6},{5,3},{6,7},{7,5},{8,9},{9,11},{10,8... | collective-permute-start | bytes 884744 | tf_op jit(solution)/shard_map/ppermute | solution.py:521
  79.7 5.2 %all-to-all-done.1 = bf16[8,32,1024]{2,1,0:T(8,128)(2,1)} async-done(((bf16[8,32,1024]{2,1,0:T(8,128)(2,1)}), bf16[8,32,1024]{2,1,0:T(8,128)(2,1)}, u32[]{:S(2)}, u32[]{:S(2)}) %all-to-all-start.1) | async-done | bytes 524320 | tf_op jit(solution)/shard_map/all_to_all | solution.py:643
  85.1 2.0 %collective-permute-done.16 = bf16[128,1152]{1,0:T(8,128)(2,1)S(1)} collective-permute-done((bf16[128,1152]{1,0:T(8,128)(2,1)S(1)}, bf16[128,1152]{1,0:T(8,128)(2,1)S(1)}, u32[]{:S(2)}, u32[]{:S(2)}) %collective-permute-start.16) | collective-permute-done | bytes 294944 | tf_op jit(solution)/shard_map/ppermute | solution.py:521
  87.6 4.0 %collective-permute-start.18 = (bf16[128,1152]{1,0:T(8,128)(2,1)S(1)}, bf16[128,1152]{1,0:T(8,128)(2,1)S(1)}, u32[]{:S(2)}, u32[]{:S(2)}) collective-permute-start(bf16[128,1152]{1,0:T(8,128)(2,1)S(1)} %add_convert_fusion.4), channel_id=1, source_target_pairs={{0,2},{1,0},{2,4},{3,1},{4,6},{5,3},{6,7},{7,5},{8,9},{9,11},{10,8... | collective-permute-start | bytes 884744 | tf_op jit(solution)/shard_map/ppermute | solution.py:521
  91.6 4.5 %temporal_mix_grad.2.low_hbm = bf16[256,1536]{1,0:T(8,128)(2,1)} custom-call(bf16[256,1024]{1,0:T(8,128)(2,1)} %bitcast.12.grad_hbm, bf16[1024,1024]{1,0:T(8,128)(2,1)} %w_hbm.4, bf16[256,3072]{1,0:T(8,128)(2,1)} %get-tuple-element.61.qkv_hbm, bf16[8,256,256]{2,1,0:T(8,128)(2,1)} %get-tuple-element.62.probs_hbm), custom_call_target="tpu_custom_call" | custom-call | flops 4000000000 | bytes 8000000 | tf_op jit(solution)/shard_map/temporal_mix_grad/pallas_call | solution.py:662
  96.2 2.3 %collective-permute-start.20 = (bf16[128,1152]{1,0:T(8,128)(2,1)S(1)}, bf16[128,1152]{1,0:T(8,128)(2,1)S(1)}, u32[]{:S(2)}, u32[]{:S(2)}) collective-permute-start(bf16[128,1152]{1,0:T(8,128)(2,1)S(1)} %add_convert_fusion.3), channel_id=1, source_target_pairs={{0,2},{1,0},{2,4},{3,1},{4,6},{5,3},{6,7},{7,5},{8,9},{9,11},{10,8... | collective-permute-start | bytes 884744 | tf_op jit(solution)/shard_map/ppermute | solution.py:521
  98.5 4.5 %temporal_mix_grad.3.high_hbm = bf16[256,1536]{1,0:T(8,128)(2,1)} custom-call(bf16[256,1024]{1,0:T(8,128)(2,1)} %bitcast.12.grad_hbm, bf16[1024,1024]{1,0:T(8,128)(2,1)} %w_hbm.4, bf16[256,3072]{1,0:T(8,128)(2,1)} %get-tuple-element.61.qkv_hbm, bf16[8,256,256]{2,1,0:T(8,128)(2,1)} %get-tuple-element.62.probs_hbm), custom_call_target="tpu_custom_call" | custom-call | flops 4000000000 | bytes 8000000 | tf_op jit(solution)/shard_map/temporal_mix_grad/pallas_call | solution.py:662
  103.1 3.3 %collective-permute-start.23 = (bf16[128,1152]{1,0:T(8,128)(2,1)S(1)}, bf16[128,1152]{1,0:T(8,128)(2,1)S(1)}, u32[]{:S(2)}, u32[]{:S(2)}) collective-permute-start(bf16[128,1152]{1,0:T(8,128)(2,1)S(1)} %add_convert_fusion.1), channel_id=1, source_target_pairs={{0,18},{1,16},{2,20},{3,17},{4,22},{5,19},{6,23},{7,21},{8,25},{9,... | collective-permute-start | bytes 884744 | tf_op jit(solution)/shard_map/ppermute | solution.py:529
  106.7 6.3 %temporal_norm_grad.1 = bf16[256,1024]{1,0:T(8,128)(2,1)} custom-call(f32[1,1024]{1,0:T(1,128)} %bitcast.33, bf16[256,1024]{1,0:T(8,128)(2,1)} %bitcast.12.grad_hbm, bf16[256,1024]{1,0:T(8,128)(2,1)} %bitcast.30, bf16[256,1536]{1,0:T(8,128)(2,1)} %temporal_mix_grad.2.low_hbm, bf16[256,1536]{1,0:T(8,128)(2,1)} %temporal_mix_grad.3.high_hbm, ...), custom_call_target="tpu_custom_call" | custom-call | flops 6000000000 | bytes 12000000 | tf_op jit(solution)/shard_map/temporal_norm_grad/pallas_call | solution.py:704
  114.1 1.6 %collective-permute-done.24.other_ref = bf16[128,1152]{1,0:T(8,128)(2,1)S(1)} collective-permute-done((bf16[128,1152]{1,0:T(8,128)(2,1)S(1)}, bf16[128,1152]{1,0:T(8,128)(2,1)S(1)}, u32[]{:S(2)}, u32[]{:S(2)}) %collective-permute-start.24) | collective-permute-done | bytes 294944 | tf_op jit(solution)/shard_map/ppermute | solution.py:532
  115.6 1.6 %finish.1 = (f32[128,3072]{1,0:T(8,128)}, f32[128,1024]{1,0:T(8,128)}) custom-call(s32[1]{0:T(128)} %bitcast.env_ref, bf16[128,1152]{1,0:T(8,128)(2,1)S(1)} %add_convert_fusion.own_ref, bf16[128,1152]{1,0:T(8,128)(2,1)S(1)} %collective-permute-done.24.other_ref, f32[1,1024]{1,0:T(1,128)S(1)} %copy-done.4, f32[1,1024]{1,0:T(1,128)S(1)} %bitcast.22), custom_call_target="tpu_custom_call" | custom-call | flops 2000000000 | bytes 4000000 | tf_op jit(solution)/shard_map/finish/pallas_call | solution.py:726
  (84 shorter events, 17.4 us)
Async XLA Ops:
  2.6 11.6 %collective-permute-start = (bf16[128,1664]{1,0:T(8,128)(2,1)}, bf16[128,1664]{1,0:T(8,128)(2,1)S(1)}, u32[]{:S(2)}, u32[]{:S(2)}) collective-permute-start(bf16[128,1664]{1,0:T(8,128)(2,1)} %pack_block.1.own_ref), channel_id=1, source_target_pairs={{0,2},{1,0},{2,4},{3,1},{4,6},{5,3},{6,7},{7,5},{8,9},{9,11},{10,8... | collective-permute-start | bytes 1277960 | tf_op jit(solution)/shard_map/ppermute | solution.py:521
  14.3 11.3 %collective-permute-start.2 = (bf16[128,1664]{1,0:T(8,128)(2,1)S(1)}, bf16[128,1664]{1,0:T(8,128)(2,1)S(1)}, u32[]{:S(2)}, u32[]{:S(2)}) collective-permute-start(bf16[128,1664]{1,0:T(8,128)(2,1)S(1)} %collective-permute-done.rest_0_), channel_id=1, source_target_pairs={{0,16},{8,24},{16,0},{24,8},{1,17},{9,25},{17,1},{25,9},{2,18},{10... | collective-permute-start | bytes 1277960 | tf_op jit(solution)/shard_map/ppermute | solution.py:535
  15.8 9.8 %collective-permute-start.1 = (bf16[128,1664]{1,0:T(8,128)(2,1)S(1)}, bf16[128,1664]{1,0:T(8,128)(2,1)S(1)}, u32[]{:S(2)}, u32[]{:S(2)}) collective-permute-start(bf16[128,1664]{1,0:T(8,128)(2,1)S(1)} %collective-permute-done.rest_0_), channel_id=1, source_target_pairs={{0,2},{1,0},{2,4},{3,1},{4,6},{5,3},{6,7},{7,5},{8,9},{9,11},{10,8... | collective-permute-start | bytes 1277960 | tf_op jit(solution)/shard_map/ppermute | solution.py:521
  16.3 25.7 %all-to-all-start = ((bf16[8,32,1024]{2,1,0:T(8,128)(2,1)}), bf16[8,32,1024]{2,1,0:T(8,128)(2,1)S(1)}, u32[]{:S(2)}, u32[]{:S(2)}) async-start(bf16[8,32,1024]{2,1,0:T(8,128)(2,1)} %bitcast.25), calls=%async_computation | async-start | bytes 1048576 | tf_op jit(solution)/shard_map/all_to_all | solution.py:585
  25.6 10.4 %collective-permute-start.4 = (bf16[128,1664]{1,0:T(8,128)(2,1)S(1)}, bf16[128,1664]{1,0:T(8,128)(2,1)S(1)}, u32[]{:S(2)}, u32[]{:S(2)}) collective-permute-start(bf16[128,1664]{1,0:T(8,128)(2,1)S(1)} %collective-permute-done.1.rest_1_), channel_id=1, source_target_pairs={{0,16},{8,24},{16,0},{24,8},{1,17},{9,25},{17,1},{25,9},{2,18},{10... | collective-permute-start | bytes 1277960 | tf_op jit(solution)/shard_map/ppermute | solution.py:535
  27.2 9.5 %collective-permute-start.3 = (bf16[128,1664]{1,0:T(8,128)(2,1)S(1)}, bf16[128,1664]{1,0:T(8,128)(2,1)S(1)}, u32[]{:S(2)}, u32[]{:S(2)}) collective-permute-start(bf16[128,1664]{1,0:T(8,128)(2,1)S(1)} %collective-permute-done.1.rest_1_), channel_id=1, source_target_pairs={{0,2},{1,0},{2,4},{3,1},{4,6},{5,3},{6,7},{7,5},{8,9},{9,11},{10,8... | collective-permute-start | bytes 1277960 | tf_op jit(solution)/shard_map/ppermute | solution.py:521
  28.8 13.2 %collective-permute-start.7 = (bf16[128,1664]{1,0:T(8,128)(2,1)S(1)}, bf16[128,1664]{1,0:T(8,128)(2,1)S(1)}, u32[]{:S(2)}, u32[]{:S(2)}) collective-permute-start(bf16[128,1664]{1,0:T(8,128)(2,1)S(1)} %collective-permute-done.rest_0_), channel_id=1, source_target_pairs={{0,8},{8,0},{16,24},{24,16},{1,9},{9,1},{17,25},{25,17},{2,10},{10... | collective-permute-start | bytes 1277960 | tf_op jit(solution)/shard_map/ppermute | solution.py:532
  28.8 13.8 %collective-permute-start.11 = (bf16[128,1664]{1,0:T(8,128)(2,1)S(1)}, bf16[128,1664]{1,0:T(8,128)(2,1)S(1)}, u32[]{:S(2)}, u32[]{:S(2)}) collective-permute-start(bf16[128,1664]{1,0:T(8,128)(2,1)S(1)} %collective-permute-done.2.rest_4_), channel_id=1, source_target_pairs={{0,8},{8,0},{16,24},{24,16},{1,9},{9,1},{17,25},{25,17},{2,10},{10... | collective-permute-start | bytes 1277960 | tf_op jit(solution)/shard_map/ppermute | solution.py:532
  36.7 12.6 %collective-permute-start.6 = (bf16[128,1664]{1,0:T(8,128)(2,1)S(1)}, bf16[128,1664]{1,0:T(8,128)(2,1)}, u32[]{:S(2)}, u32[]{:S(2)}) collective-permute-start(bf16[128,1664]{1,0:T(8,128)(2,1)S(1)} %collective-permute-done.3.rest_2_), channel_id=1, source_target_pairs={{0,16},{8,24},{16,0},{24,8},{1,17},{9,25},{17,1},{25,9},{2,18},{10... | collective-permute-start | bytes 1277960 | tf_op jit(solution)/shard_map/ppermute | solution.py:535
  38.2 11.1 %collective-permute-start.5 = (bf16[128,1664]{1,0:T(8,128)(2,1)S(1)}, bf16[128,1664]{1,0:T(8,128)(2,1)}, u32[]{:S(2)}, u32[]{:S(2)}) collective-permute-start(bf16[128,1664]{1,0:T(8,128)(2,1)S(1)} %collective-permute-done.3.rest_2_), channel_id=1, source_target_pairs={{0,2},{1,0},{2,4},{3,1},{4,6},{5,3},{6,7},{7,5},{8,9},{9,11},{10,8... | collective-permute-start | bytes 1277960 | tf_op jit(solution)/shard_map/ppermute | solution.py:521
  42.0 9.3 %collective-permute-start.8 = (bf16[128,1664]{1,0:T(8,128)(2,1)S(1)}, bf16[128,1664]{1,0:T(8,128)(2,1)}, u32[]{:S(2)}, u32[]{:S(2)}) collective-permute-start(bf16[128,1664]{1,0:T(8,128)(2,1)S(1)} %collective-permute-done.1.rest_1_), channel_id=1, source_target_pairs={{0,8},{8,0},{16,24},{24,16},{1,9},{9,1},{17,25},{25,17},{2,10},{10... | collective-permute-start | bytes 1277960 | tf_op jit(solution)/shard_map/ppermute | solution.py:532
  42.0 9.2 %collective-permute-start.9 = (bf16[128,1664]{1,0:T(8,128)(2,1)S(1)}, bf16[128,1664]{1,0:T(8,128)(2,1)}, u32[]{:S(2)}, u32[]{:S(2)}) collective-permute-start(bf16[128,1664]{1,0:T(8,128)(2,1)S(1)} %collective-permute-done.3.rest_2_), channel_id=1, source_target_pairs={{0,8},{8,0},{16,24},{24,16},{1,9},{9,1},{17,25},{25,17},{2,10},{10... | collective-permute-start | bytes 1277960 | tf_op jit(solution)/shard_map/ppermute | solution.py:532
  42.6 8.7 %collective-permute-start.12 = (bf16[128,1664]{1,0:T(8,128)(2,1)S(1)}, bf16[128,1664]{1,0:T(8,128)(2,1)}, u32[]{:S(2)}, u32[]{:S(2)}) collective-permute-start(bf16[128,1664]{1,0:T(8,128)(2,1)S(1)} %collective-permute-done.4.rest_5_), channel_id=1, source_target_pairs={{0,8},{8,0},{16,24},{24,16},{1,9},{9,1},{17,25},{25,17},{2,10},{10... | collective-permute-start | bytes 1277960 | tf_op jit(solution)/shard_map/ppermute | solution.py:532
  63.2 5.7 %collective-permute-start.14 = (bf16[512,1024]{1,0:T(8,128)(2,1)}, bf16[512,1024]{1,0:T(8,128)(2,1)S(1)}, u32[]{:S(2)}, u32[]{:S(2)}) collective-permute-start(bf16[512,1024]{1,0:T(8,128)(2,1)} %get-tuple-element.51.pack_ref), channel_id=1, source_target_pairs={{0,8},{8,0},{16,24},{24,16},{1,9},{9,1},{17,25},{25,17},{2,10},{10... | collective-permute-start | bytes 3145736 | tf_op jit(solution)/shard_map/ppermute | solution.py:532
  63.4 21.5 %all-to-all-start.1 = ((bf16[8,32,1024]{2,1,0:T(8,128)(2,1)}), bf16[8,32,1024]{2,1,0:T(8,128)(2,1)}, u32[]{:S(2)}, u32[]{:S(2)}) async-start(bf16[8,32,1024]{2,1,0:T(8,128)(2,1)} %bitcast.24), calls=%async_computation.1 | async-start | bytes 1048576 | tf_op jit(solution)/shard_map/all_to_all | solution.py:643
  74.0 11.0 %collective-permute-start.15 = (bf16[128,1152]{1,0:T(8,128)(2,1)S(1)}, bf16[128,1152]{1,0:T(8,128)(2,1)S(1)}, u32[]{:S(2)}, u32[]{:S(2)}) collective-permute-start(bf16[128,1152]{1,0:T(8,128)(2,1)S(1)} %get-tuple-element.54), channel_id=1, source_target_pairs={{0,2},{1,0},{2,4},{3,1},{4,6},{5,3},{6,7},{7,5},{8,9},{9,11},{10,8... | collective-permute-start | bytes 884744 | tf_op jit(solution)/shard_map/ppermute | solution.py:521
  76.2 10.9 %collective-permute-start.16 = (bf16[128,1152]{1,0:T(8,128)(2,1)S(1)}, bf16[128,1152]{1,0:T(8,128)(2,1)S(1)}, u32[]{:S(2)}, u32[]{:S(2)}) collective-permute-start(bf16[128,1152]{1,0:T(8,128)(2,1)S(1)} %get-tuple-element.56), channel_id=1, source_target_pairs={{0,1},{1,3},{2,0},{3,5},{4,2},{5,7},{6,4},{7,6},{8,10},{9,8},{10,1... | collective-permute-start | bytes 884744 | tf_op jit(solution)/shard_map/ppermute | solution.py:521
  77.7 9.9 %collective-permute-start.17 = (bf16[128,1152]{1,0:T(8,128)(2,1)S(1)}, bf16[128,1152]{1,0:T(8,128)(2,1)S(1)}, u32[]{:S(2)}, u32[]{:S(2)}) collective-permute-start(bf16[128,1152]{1,0:T(8,128)(2,1)S(1)} %get-tuple-element.59), channel_id=1, source_target_pairs={{0,16},{8,24},{16,0},{24,8},{1,17},{9,25},{17,1},{25,9},{2,18},{10... | collective-permute-start | bytes 884744 | tf_op jit(solution)/shard_map/ppermute | solution.py:535
  78.1 17.9 %collective-permute-start.19 = (bf16[128,1152]{1,0:T(8,128)(2,1)S(1)}, bf16[128,1152]{1,0:T(8,128)(2,1)S(1)}, u32[]{:S(2)}, u32[]{:S(2)}) collective-permute-start(bf16[128,1152]{1,0:T(8,128)(2,1)S(1)} %get-tuple-element.65), channel_id=1, source_target_pairs={{0,16},{8,24},{16,0},{24,8},{1,17},{9,25},{17,1},{25,9},{2,18},{10... | collective-permute-start | bytes 884744 | tf_op jit(solution)/shard_map/ppermute | solution.py:535
  87.2 15.7 %collective-permute-start.21 = (bf16[128,1152]{1,0:T(8,128)(2,1)S(1)}, bf16[128,1152]{1,0:T(8,128)(2,1)S(1)}, u32[]{:S(2)}, u32[]{:S(2)}) collective-permute-start(bf16[128,1152]{1,0:T(8,128)(2,1)S(1)} %add_convert_fusion.2), channel_id=1, source_target_pairs={{0,16},{8,24},{16,0},{24,8},{1,17},{9,25},{17,1},{25,9},{2,18},{10... | collective-permute-start | bytes 884744 | tf_op jit(solution)/shard_map/ppermute | solution.py:535
  87.6 8.4 %collective-permute-start.18 = (bf16[128,1152]{1,0:T(8,128)(2,1)S(1)}, bf16[128,1152]{1,0:T(8,128)(2,1)S(1)}, u32[]{:S(2)}, u32[]{:S(2)}) collective-permute-start(bf16[128,1152]{1,0:T(8,128)(2,1)S(1)} %add_convert_fusion.4), channel_id=1, source_target_pairs={{0,2},{1,0},{2,4},{3,1},{4,6},{5,3},{6,7},{7,5},{8,9},{9,11},{10,8... | collective-permute-start | bytes 884744 | tf_op jit(solution)/shard_map/ppermute | solution.py:521
  96.2 6.8 %collective-permute-start.20 = (bf16[128,1152]{1,0:T(8,128)(2,1)S(1)}, bf16[128,1152]{1,0:T(8,128)(2,1)S(1)}, u32[]{:S(2)}, u32[]{:S(2)}) collective-permute-start(bf16[128,1152]{1,0:T(8,128)(2,1)S(1)} %add_convert_fusion.3), channel_id=1, source_target_pairs={{0,2},{1,0},{2,4},{3,1},{4,6},{5,3},{6,7},{7,5},{8,9},{9,11},{10,8... | collective-permute-start | bytes 884744 | tf_op jit(solution)/shard_map/ppermute | solution.py:521
  103.1 9.9 %collective-permute-start.23 = (bf16[128,1152]{1,0:T(8,128)(2,1)S(1)}, bf16[128,1152]{1,0:T(8,128)(2,1)S(1)}, u32[]{:S(2)}, u32[]{:S(2)}) collective-permute-start(bf16[128,1152]{1,0:T(8,128)(2,1)S(1)} %add_convert_fusion.1), channel_id=1, source_target_pairs={{0,18},{1,16},{2,20},{3,17},{4,22},{5,19},{6,23},{7,21},{8,25},{9,... | collective-permute-start | bytes 884744 | tf_op jit(solution)/shard_map/ppermute | solution.py:529
  106.3 7.5 %collective-permute-start.22 = (bf16[128,1152]{1,0:T(8,128)(2,1)S(1)}, bf16[128,1152]{1,0:T(8,128)(2,1)S(1)}, u32[]{:S(2)}, u32[]{:S(2)}) collective-permute-start(bf16[128,1152]{1,0:T(8,128)(2,1)S(1)} %add_convert_fusion.1), channel_id=1, source_target_pairs={{0,2},{1,0},{2,4},{3,1},{4,6},{5,3},{6,7},{7,5},{8,9},{9,11},{10,8... | collective-permute-start | bytes 884744 | tf_op jit(solution)/shard_map/ppermute | solution.py:521
  (18 other events, 274.3 us)
